TPU v7x, 768 devices: a whole 4x8x12 slice. The times are simulated.
768 devices in a mesh: rows: 192 (over y, z, core), cols: 4 (over x).
Axes of the slice: x: 4, y: 8, z: 12, core: 2. Of those that a mesh axis runs over, the one named last changes fastest.
Arguments:
- features: bfloat16 [294912, 256], P(('rows', 'cols')), may hold values from -6 to 6
- pre_act: bfloat16 [294912, 256], P(('rows', 'cols')), may hold values from -6 to 6
- upstream: float32 [294912, 256], P(('rows', 'cols')), may hold values from -6 to 6
- weight: bfloat16 [256, 256], replicated, may hold values from -0.375 to 0.375
- tile_values: bfloat16 [55296, 128, 128], P(('rows', 'cols')), may hold values from -0.1875 to 0.1875
- tile_list: int32 [55296, 3], P(('rows', 'cols')), may hold values from 0 to 2303, as said below
- tile_counts: int32 [768], P(('rows', 'cols')), may hold values from 9 to 72, as said below
Outputs:
- grad_features: float32 [294912, 256], P(('rows', 'cols'))
- grad_weight: float32 [256, 256], replicated
Inputs may be any that keep to these rules, and one draw needn't show every extreme that they name: `tile_list`: for slot d * 72 + k: column 0 is one of device d's own blocks; column 1 is a block owned by a device whose rows index differs from device d's rows index by at most one; column 2, over device d's 72 slots, takes every value 0 to 71 once. Slots that are not live hold valid entries too. `tile_counts`: some device has all 72 slots live.
All inputs are finite; a program needn't handle non-finite values.
Results may differ from a plain program's by a relative error of at most 0.0041.
Values may be sent and summed in bfloat16 or wider, within the bound.
No kernel may reach another device: no remote copies, remote signals or barrier semaphores. Data moves between devices by JAX's collectives and lax.ppermute only.
A program may use at most 128 MiB of HBM per device.

v0:
```python
import math

import jax
import jax.numpy as jnp
from jax import lax
from jax.sharding import PartitionSpec as P


def extended(array, sides, width):
    for axis, dim in sides:
        peers, length = (lax.axis_size(axis), array.shape[dim])
        up = [(i, (i + 1) % peers) for i in range(peers - 1)]
        down = [(j, i) for i, j in up]
        last = lax.slice_in_dim(array, length - width, length, axis=dim)
        first = lax.slice_in_dim(array, 0, width, axis=dim)
        before = lax.ppermute(last, axis, up)
        after = lax.ppermute(first, axis, down)
        array = jnp.concatenate([before, array, after], axis=dim)
    return array


def from_behind(block, axis, distance):
    devices = range(lax.axis_size(axis))
    route = [(i - distance, i) for i in devices if i - distance in devices]
    return lax.ppermute(block, axis, route)


def local(features, pre_act, upstream, weight, tile_values, tile_list, tile_counts):
    row_count = lax.axis_size("rows")
    col_count = lax.axis_size("cols")
    own_row = lax.axis_index("rows")
    own_col = lax.axis_index("cols")
    rows_dev, channels = features.shape
    slot_count = tile_values.shape[0]
    tile_edge = tile_values.shape[1]
    own_blocks = rows_dev // tile_edge
    row_blocks = col_count * own_blocks
    band_blocks = 3 * row_blocks
    node_count = rows_dev * row_count * col_count
    masked = jnp.where(pre_act > 0, upstream, 0.0).astype(jnp.bfloat16)
    back_grad = lax.dot_general(
        masked, weight, (((1,), (1,)), ((), ())), preferred_element_type=jnp.float32
    ).astype(jnp.bfloat16)
    first_block = (own_row * col_count + own_col) * own_blocks
    dst_index = tile_list[:, 0] - first_block
    src_index = tile_list[:, 1] - (own_row - 1) * row_blocks
    active = (jnp.arange(slot_count, dtype=jnp.int32) < tile_counts[0]).astype(jnp.float32)
    tile_mats = jnp.take(tile_values, tile_list[:, 2], axis=0)
    group_rows = lax.all_gather(features, "cols", axis=0, tiled=True)
    band_rows = extended(group_rows, (("rows", 0),), group_rows.shape[0])
    band_rows = band_rows.reshape(band_blocks, tile_edge, channels)
    dest_data = back_grad.reshape(own_blocks, 1, tile_edge, channels)
    kind_count = dest_data.shape[1]
    group_size = math.gcd(slot_count, 24)
    turn_count = slot_count // group_size

    def tile_step(state_pair, turn_index):
        first_slot = turn_index * group_size
        tile_group = lax.dynamic_slice_in_dim(tile_mats, first_slot, group_size, 0)
        dst_group = lax.dynamic_slice_in_dim(dst_index, first_slot, group_size, 0)
        src_group = lax.dynamic_slice_in_dim(src_index, first_slot, group_size, 0)
        live_group = lax.dynamic_slice_in_dim(active, first_slot, group_size, 0)
        dst_rows = jnp.take(dest_data, dst_group, axis=0)
        contrib = jnp.einsum(
            "tij,tkif->ktjf", tile_group, dst_rows, preferred_element_type=jnp.float32
        )
        contrib = contrib * live_group[None, :, None, None]
        contrib_slab = state_pair[0].at[:, src_group].add(contrib)
        sources = jnp.take(band_rows, src_group, axis=0)
        products = jnp.einsum(
            "tij,tjf->tif", tile_group, sources, preferred_element_type=jnp.float32
        )
        aggregate = state_pair[1].at[dst_group].add(products * live_group[:, None, None])
        return ((contrib_slab, aggregate), None)

    empty_slab = jnp.zeros((kind_count, band_blocks, tile_edge, channels), jnp.float32)
    start_state = (empty_slab, jnp.zeros((own_blocks, tile_edge, channels), jnp.float32))
    final_state, unused = lax.scan(tile_step, start_state, jnp.arange(turn_count, dtype=jnp.int32))
    stacked = final_state[0].reshape(kind_count, 3, col_count * rows_dev, channels)
    summed = stacked[:, 1]
    for shift_by, side_index in ((1, 2), (-1, 0)):
        summed = summed + from_behind(stacked[:, side_index], "rows", shift_by)
    own_grad = lax.psum_scatter(summed, "cols", scatter_dimension=1, tiled=True)
    grad_features = own_grad[0]
    weight_part = lax.dot_general(
        final_state[1].reshape(rows_dev, channels),
        masked,
        (((0,), (0,)), ((), ())),
        precision=lax.Precision.HIGHEST,
        preferred_element_type=jnp.float32,
    )
    weight_total = lax.psum(weight_part, ("rows", "cols"))
    grad_weight = weight_total / math.sqrt(node_count)
    return (grad_features, grad_weight)


def solution(mesh):
    return jax.shard_map(
        local,
        mesh=mesh,
        in_specs=(
            P(("rows", "cols"), None),
            P(("rows", "cols"), None),
            P(("rows", "cols"), None),
            P(),
            P(("rows", "cols"), None, None),
            P(("rows", "cols"), None),
            P(("rows", "cols")),
        ),
        out_specs=(P(("rows", "cols"), None), P()),
        check_vma=False,
    )
```

profile of v0, /device:TPU:1, one launch (start us, length us, event | category | flops | bytes accessed | tf_op | source)
XLA Modules:
  0.0 646.6 jit_solution(1915964693513942801)
XLA Ops:
  8.1 13.7 %all_gather.3 = bf16[1536,256]{1,0:T(8,128)(2,1)} all-gather(bf16[384,256]{1,0:T(8,128)(2,1)} %param.9), channel_id=1, replica_groups=mesh['rows'=192,'cols'=4] {'cols'}, dimensions={0}, use_global_device_ids=true | all-gather | bytes 983040 | tf_op jit(solution)/shard_map/all_gather | solution.py:49
  21.8 13.1 %collective-permute-start.1 = (bf16[1536,256]{1,0:T(8,128)(2,1)}, bf16[1536,256]{1,0:T(8,128)(2,1)}, u32[]{:S(2)}, u32[]{:S(2)}) collective-permute-start(bf16[1536,256]{1,0:T(8,128)(2,1)} %all_gather.3), channel_id=1, source_target_pairs={{4,0},{8,4},{12,8},{16,12},{20,16},{24,20},{28,24},{32,28},{36,32}... | collective-permute-start | bytes 2359304 | tf_op jit(solution)/shard_map/ppermute | solution.py:17
  34.9 1.9 collective-permute-start
  38.9 2.5 gather_fusion.2
  42.3 3.4 broadcast_select_fusion
  46.0 3.2 pad_maximum_fusion
  49.8 2.7 broadcast_in_dim.46
  52.5 108.7 %while.12 = (s32[]{:T(128)}, f32[1,36,128,256]{3,2,1,0:T(8,128)}, f32[3,128,256]{2,1,0:T(8,128)S(1)}, s32[3]{0:T(128)}, s32[72]{0:T(128)S(1)}, /*index=5*/s32[72...) while((s32[]{:T(128)}, f32[1,36,128,256]{3,2,1,0:T(8,128)}, ...), condition=%wide.region_3.4_spmd, body=%wide.region_0.0_spmd.sunk | while | flops 407374112 | bytes 42482920 | solution.py:78
  58.3 3.5 gather_fusion.1
  61.9 3.9 convolution_multiply_fusion.2
  65.8 6.0 scatter_fusion.1
  71.8 4.1 fusion.28
  75.9 3.5 copy.14
  79.4 9.3 %scatter_fusion = f32[36,128,256]{2,1,0:T(8,128)} fusion(f32[36,128,256]{2,1,0:T(8,128)} %bitcast.56, s32[24]{0:T(128)S(1)} %get-tuple-element.163, f32[24,128,256]{2,1,0:T(8,128)} %copy.14), kind=kCustom, calls=%fused_computation.3.clone.1 | custom fusion | flops 786432 | bytes 9437280 | tf_op jit(solution)/shard_map/while/body/eval_jaxpr/scatter-add | solution.py:68
  94.6 3.5 gather_fusion.1
  98.1 3.9 convolution_multiply_fusion.2
  102.0 6.0 scatter_fusion.1
  108.1 4.1 fusion.28
  112.1 3.5 copy.14
  115.7 9.3 %scatter_fusion = f32[36,128,256]{2,1,0:T(8,128)} fusion(f32[36,128,256]{2,1,0:T(8,128)} %bitcast.56, s32[24]{0:T(128)S(1)} %get-tuple-element.163, f32[24,128,256]{2,1,0:T(8,128)} %copy.14), kind=kCustom, calls=%fused_computation.3.clone.1 | custom fusion | flops 786432 | bytes 9437280 | tf_op jit(solution)/shard_map/while/body/eval_jaxpr/scatter-add | solution.py:68
  130.8 3.5 gather_fusion.1
  134.4 3.9 convolution_multiply_fusion.2
  138.3 6.0 scatter_fusion.1
  144.3 4.1 fusion.28
  148.4 3.5 copy.14
  151.9 9.3 %scatter_fusion = f32[36,128,256]{2,1,0:T(8,128)} fusion(f32[36,128,256]{2,1,0:T(8,128)} %bitcast.56, s32[24]{0:T(128)S(1)} %get-tuple-element.163, f32[24,128,256]{2,1,0:T(8,128)} %copy.14), kind=kCustom, calls=%fused_computation.3.clone.1 | custom fusion | flops 786432 | bytes 9437280 | tf_op jit(solution)/shard_map/while/body/eval_jaxpr/scatter-add | solution.py:68
  161.2 3.8 slice_bitcast_fusion.1
  165.0 4.7 collective-permute-start.2
  173.0 14.4 %collective-permute-done.2 = f32[1,1536,256]{2,1,0:T(8,128)} collective-permute-done((f32[1,1536,256]{2,1,0:T(8,128)}, f32[1,1536,256]{2,1,0:T(8,128)}, u32[]{:S(2)}, u32[]{:S(2)}) %collective-permute-start.2) | collective-permute-done | bytes 1572896 | tf_op jit(solution)/shard_map/ppermute | solution.py:25
  187.4 4.4 collective-permute-done.3
  191.8 3.9 fusion.14
  195.7 441.7 %all-reduce.2.cloned.1.call-done = f32[256,256]{1,0:T(8,128)} async-done(((f32[256,256]{1,0:T(8,128)}), f32[256,256]{1,0:T(8,128)}) %all-reduce.2.cloned.1.call-update) | async-done | bytes 262160 | tf_op jit(solution)/shard_map/psum | solution.py:92
  (79 shorter events, 23.5 us)
Async XLA Ops:
  8.0 30.9 %copy-start = (bf16[72,128,128]{2,1,0:T(8,128)(2,1)S(1)}, bf16[72,128,128]{2,1,0:T(8,128)(2,1)}, u32[]{:S(2)}) copy-start(bf16[72,128,128]{2,1,0:T(8,128)(2,1)} %param.13) | copy-start | bytes 7077892
  8.0 629.4 %all-reduce.2.cloned.1.call-start = ((), (), s32[]{:S(2)}) async-start(), calls=%async_computation.2 | async-start | bytes 524288 | tf_op jit(solution)/shard_map/psum | solution.py:92
  21.8 23.9 %collective-permute-start.1 = (bf16[1536,256]{1,0:T(8,128)(2,1)}, bf16[1536,256]{1,0:T(8,128)(2,1)}, u32[]{:S(2)}, u32[]{:S(2)}) collective-permute-start(bf16[1536,256]{1,0:T(8,128)(2,1)} %all_gather.3), channel_id=1, source_target_pairs={{4,0},{8,4},{12,8},{16,12},{20,16},{24,20},{28,24},{32,28},{36,32}... | collective-permute-start | bytes 2359304 | tf_op jit(solution)/shard_map/ppermute | solution.py:17
  34.9 11.2 %collective-permute-start = (bf16[1536,256]{1,0:T(8,128)(2,1)}, bf16[1536,256]{1,0:T(8,128)(2,1)}, u32[]{:S(2)}, u32[]{:S(2)}) collective-permute-start(bf16[1536,256]{1,0:T(8,128)(2,1)} %all_gather.3), channel_id=1, source_target_pairs={{0,4},{4,8},{8,12},{12,16},{16,20},{20,24},{24,28},{28,32},{32,36}... | collective-permute-start | bytes 2359304 | tf_op jit(solution)/shard_map/ppermute | solution.py:16
  38.9 3.2 copy-start.1
  38.9 3.2 copy-start.2
  38.9 3.2 copy-start.3
  52.5 4.0 copy-start.6
  52.5 4.0 copy-start.8
  58.3 3.5 copy-start.4
  65.8 6.1 copy-start.5
  79.4 9.3 %copy-start.7 = (s32[72]{0:T(128)S(1)}, s32[72]{0:T(128)}, u32[]{:S(2)}) copy-start(s32[72]{0:T(128)} %copy-done.6) | copy-start | bytes 868 | tf_op jit(solution)/shard_map/while
  79.4 9.3 %copy-start.9 = (s32[72]{0:T(128)S(1)}, s32[72]{0:T(128)}, u32[]{:S(2)}) copy-start(s32[72]{0:T(128)} %copy-done.8) | copy-start | bytes 868 | tf_op jit(solution)/shard_map/while
  88.7 4.0 copy-start.6
  88.7 4.0 copy-start.8
  94.6 3.5 copy-start.4
  102.0 6.1 copy-start.5
  115.7 9.4 %copy-start.7 = (s32[72]{0:T(128)S(1)}, s32[72]{0:T(128)}, u32[]{:S(2)}) copy-start(s32[72]{0:T(128)} %copy-done.6) | copy-start | bytes 868 | tf_op jit(solution)/shard_map/while
  115.7 9.4 %copy-start.9 = (s32[72]{0:T(128)S(1)}, s32[72]{0:T(128)}, u32[]{:S(2)}) copy-start(s32[72]{0:T(128)} %copy-done.8) | copy-start | bytes 868 | tf_op jit(solution)/shard_map/while
  125.0 4.0 copy-start.6
  125.0 4.0 copy-start.8
  130.8 3.5 copy-start.4
  138.3 6.1 copy-start.5
  151.9 9.3 %copy-start.7 = (s32[72]{0:T(128)S(1)}, s32[72]{0:T(128)}, u32[]{:S(2)}) copy-start(s32[72]{0:T(128)} %copy-done.6) | copy-start | bytes 868 | tf_op jit(solution)/shard_map/while
  151.9 9.3 %copy-start.9 = (s32[72]{0:T(128)S(1)}, s32[72]{0:T(128)}, u32[]{:S(2)}) copy-start(s32[72]{0:T(128)} %copy-done.8) | copy-start | bytes 868 | tf_op jit(solution)/shard_map/while
  165.0 22.4 %collective-permute-start.2 = (f32[1,1536,256]{2,1,0:T(8,128)}, f32[1,1536,256]{2,1,0:T(8,128)}, u32[]{:S(2)}, u32[]{:S(2)}) collective-permute-start(f32[1,1536,256]{2,1,0:T(8,128)} %get-tuple-element.93), channel_id=1, source_target_pairs={{0,4},{4,8},{8,12},{12,16},{16,20},{20,24},{24,28},{28,32},{32,36}... | collective-permute-start | bytes 4718600 | tf_op jit(solution)/shard_map/ppermute | solution.py:25
  169.7 22.1 %collective-permute-start.3 = (f32[1,1536,256]{2,1,0:T(8,128)}, f32[1,1536,256]{2,1,0:T(8,128)}, u32[]{:S(2)}, u32[]{:S(2)}) collective-permute-start(f32[1,1536,256]{2,1,0:T(8,128)} %get-tuple-element.94), channel_id=1, source_target_pairs={{4,0},{8,4},{12,8},{16,12},{20,16},{24,20},{28,24},{32,28},{36,32}... | collective-permute-start | bytes 4718600 | tf_op jit(solution)/shard_map/ppermute | solution.py:25
  172.9 466.2 %reduce-scatter.2.cloned.1.call-start = ((), (), s32[]{:S(2)}) async-start(), calls=%async_computation.1 | async-start | bytes 1966080 | tf_op jit(solution)/shard_map/reduce_scatter | solution.py:83
Sparse Core Ops, SparseCore 0:
  173.0 464.3 all-reduce.1
Sparse Core Ops, SparseCore 1:
  195.8 35.0 reduce-scatter.1
where the time goes:
time: 648 us; the launch traced here: 647 us
  waiting for transfers between devices  461 us (71%)
  other arithmetic  62.3 us (10%)
  local copies, waits for them, and re-layouts  44.1 us (7%)
  matrix products  25.3 us (4%)
  starting transfers between devices  21.7 us (3%)
  between operations  16.2 us (2%)
  blocking collectives  13.7 us (2%)
    psum x1, waiting for transfers between devices, local(): weight_total = lax.psum(weight_part, ('rows', 'cols'))  442 us
    scatter-add x3, other arithmetic, tile_step(): contrib_slab = state_pair[0].at[:, src_group].add(contrib)  27.9 us
    ppermute x2, waiting for transfers between devices, from_behind(): return lax.ppermute(block, axis, route)  18.8 us
    scatter-add x3, other arithmetic, tile_step(): state_pair[1].at[dst_group].add(products * live_group[:, None, None])  18.1 us
    all_gather x1, blocking collectives, local(): group_rows = lax.all_gather(features, 'cols', axis=0, tiled=True)  13.7 us
    ppermute x1, starting transfers between devices, extended(): after = lax.ppermute(first, axis, down)  13.1 us
  transfers between devices with their start and end apart: 6, of which 4 were waited for; matrix products, arithmetic and copies ran while one was open for 2% of the time, Pallas kernels for 0%

commit v1 on v0

v1 whole, which is shorter than its diff:
```python
import functools
import math

import jax
import jax.numpy as jnp
from jax import lax
from jax.experimental import pallas as pl
from jax.experimental.pallas import tpu as pltpu
from jax.sharding import Mesh, PartitionSpec as P

GROUP = 8
VMEM = pl.BlockSpec(memory_space=pltpu.VMEM)
SMEM = pl.BlockSpec(memory_space=pltpu.SMEM)


def tile_kernel(base, count, slots, pre, up, tiles, beside, own, masked_t, total):
    blocks, _, edge = masked_t.shape
    for d in range(blocks):
        rows = pl.ds(d * edge, edge)
        kept = jnp.where(pre[rows, :].astype(jnp.float32) > 0, up[rows, :], 0.0)
        masked_t[d] = kept.T.astype(jnp.bfloat16)
    total[...] = jnp.zeros_like(total)
    live = count[0]

    def body(group, carry):
        for u in range(GROUP):
            slot = group * GROUP + u
            dst = slots[slot, 0] - base[0]
            src = slots[slot, 1] - base[1]
            tile = tiles[slots[slot, 2]]
            tile = jnp.where(slot < live, tile, jnp.zeros_like(tile))
            total[src] += jnp.dot(masked_t[dst], tile, preferred_element_type=jnp.float32)
        return carry

    lax.fori_loop(0, (live + GROUP - 1) // GROUP, body, 0)
    width = own.shape[0]
    beside[0] = total[pl.ds(0, width)].astype(jnp.bfloat16)
    own[...] = total[pl.ds(width, width)]
    beside[1] = total[pl.ds(2 * width, width)].astype(jnp.bfloat16)


def split(value):
    high = value.astype(jnp.bfloat16)
    return high, (value - high.astype(jnp.float32)).astype(jnp.bfloat16)


def weight_kernel(parts, features, summed, term):
    peers, blocks, _, edge = parts.shape
    acc = None
    for b in range(blocks):
        g = parts[0, b].astype(jnp.float32)
        for p in range(1, peers):
            g = g + parts[p, b].astype(jnp.float32)
        summed[b] = g
        feat = features[pl.ds(b * edge, edge), :]
        for piece in split(g):
            prod = jnp.dot(piece, feat, preferred_element_type=jnp.float32)
            acc = prod if acc is None else acc + prod
    term[...] = acc.T


def feature_kernel(summed, weight, grad):
    blocks, _, edge = summed.shape
    for b in range(blocks):
        acc = None
        for piece in split(summed[b].T):
            prod = lax.dot_general(
                piece, weight[...], (((1,), (1,)), ((), ())), preferred_element_type=jnp.float32
            )
            acc = prod if acc is None else acc + prod
        grad[pl.ds(b * edge, edge), :] = acc


def local(features, pre_act, upstream, weight, tile_values, tile_list, tile_counts, *, sizes):
    y, zc, x = sizes
    rows = y * zc
    own_row = lax.axis_index(("y", "zc"))
    own_col = lax.axis_index("x")
    rows_dev, channels = features.shape
    edge = tile_values.shape[1]
    blocks = rows_dev // edge
    width = x * blocks
    base = jnp.stack([(own_row * x + own_col) * blocks, (own_row - 1) * width]).astype(jnp.int32)
    params = pltpu.CompilerParams(vmem_limit_bytes=40 << 20)
    beside, own = pl.pallas_call(
        tile_kernel,
        out_shape=(
            jax.ShapeDtypeStruct((2, width, channels, edge), jnp.bfloat16),
            jax.ShapeDtypeStruct((width, channels, edge), jnp.float32),
        ),
        in_specs=[SMEM] * 3 + [VMEM] * 3,
        out_specs=(VMEM, VMEM),
        scratch_shapes=[
            pltpu.VMEM((blocks, channels, edge), jnp.bfloat16),
            pltpu.VMEM((3 * width, channels, edge), jnp.float32),
        ],
        compiler_params=params,
        name="tile_sums",
    )(base, tile_counts, tile_list, pre_act, upstream, tile_values)
    ring = ("y", "zc")
    from_next = lax.ppermute(beside[0], ring, [(i + 1, i) for i in range(rows - 1)])
    from_last = lax.ppermute(beside[1], ring, [(i, i + 1) for i in range(rows - 1)])
    summed = own + from_next.astype(jnp.float32) + from_last.astype(jnp.float32)
    summed = summed.astype(jnp.bfloat16).reshape(x, blocks, channels, edge)
    parts = lax.all_to_all(summed, "x", 0, 0)
    grad_t, term = pl.pallas_call(
        weight_kernel,
        out_shape=(
            jax.ShapeDtypeStruct((blocks, channels, edge), jnp.float32),
            jax.ShapeDtypeStruct((channels, channels), jnp.float32),
        ),
        in_specs=[VMEM] * 2,
        out_specs=(VMEM, VMEM),
        compiler_params=params,
        name="weight_term",
    )(parts, features)
    grad_features = pl.pallas_call(
        feature_kernel,
        out_shape=jax.ShapeDtypeStruct((rows_dev, channels), jnp.float32),
        in_specs=[VMEM] * 2,
        out_specs=VMEM,
        compiler_params=params,
        name="feature_grad",
    )(grad_t, weight)
    peers = y * x
    pieces = lax.all_to_all(term.reshape(peers, channels // peers, channels), ("y", "x"), 0, 0)
    piece = jnp.sum(pieces, axis=0)
    copies = jnp.broadcast_to(piece[None], (zc,) + piece.shape)
    piece = jnp.sum(lax.all_to_all(copies, "zc", 0, 0), axis=0)
    piece = piece / math.sqrt(rows * x * rows_dev)
    copies = jnp.broadcast_to(piece[None], (peers,) + piece.shape)
    grad_weight = lax.all_to_all(copies, ("y", "x"), 0, 0).reshape(channels, channels)
    return (grad_features, grad_weight)


def solution(mesh):
    rows, x = mesh.devices.shape
    y = math.gcd(rows, 8)
    zc = rows // y
    fine = Mesh(mesh.devices.reshape(y, zc, x), ("y", "zc", "x"))
    every = ("y", "zc", "x")
    return jax.shard_map(
        functools.partial(local, sizes=(y, zc, x)),
        mesh=fine,
        in_specs=(
            P(every, None),
            P(every, None),
            P(every, None),
            P(),
            P(every, None, None),
            P(every, None),
            P(every),
        ),
        out_specs=(P(every, None), P()),
        check_vma=False,
    )
```

time: 648 us -> 110 us (0.17)
  waiting for transfers between devices: 461 us -> 18.7 us
  other arithmetic: 62.3 us -> 0.45 us
  blocking collectives: 13.7 us -> 60 us
  local copies, waits for them, and re-layouts: 44.1 us -> 5.91 us
  matrix products: 25.3 us -> 0 us
  between operations: 16.2 us -> 1.39 us
    psum x1 -> x0, waiting for transfers between devices: 442 us -> none  [local(): weight_total = lax.psum(weight_part, ('rows', 'cols'))]
    all_to_all x0 -> x3, blocking collectives: none -> 60 us  [the longest x1 33.1 us: local(): piece = jnp.sum(lax.all_to_all(copies, 'zc', 0, 0), axis=0)]
    scatter-add x6 -> x0, other arithmetic: 46 us -> none  [the longest x3 27.9 us: tile_step(): contrib_slab = state_pair[0].at[:, src_group].add(contrib)]
    dot_general x8 -> x0, matrix products: 25.3 us -> none  [the longest x3 12.2 us: tile_step(): jnp.einsum('tij,tkif->ktjf', tile_group, dst_rows, preferred_element_type...]
    gather x7 -> x0, local copies, waits for them, and re-layouts: 18.6 us -> none  [the longest x3 10.6 us: tile_step(): sources = jnp.take(band_rows, src_group, axis=0)]
    all_gather x1 -> x0, blocking collectives: 13.7 us -> none  [local(): group_rows = lax.all_gather(features, 'cols', axis=0, tiled=True)]
    mul x3 -> x0, local copies, waits for them, and re-layouts: 10.6 us -> none  [tile_step(): contrib = contrib * live_group[None, :, None, None]]
    ppermute x4 -> x2, waiting for transfers between devices: 19.2 us -> 8.91 us  [the longest x1 8.22 us: local(): lax.ppermute(beside[1], ring, [(i, i + 1) for i in range(rows - 1)])]
  transfers between devices with their start and end apart: 6 -> 3, of which waited for: 4 -> 3; matrix products, arithmetic and copies ran while one was open for 2% -> 0% of each run, Pallas kernels for 0% -> 1%
where the time goes in v1:
time: 110 us; the launch traced here: 109 us
  blocking collectives  60 us (55%)
  waiting for transfers between devices  18.7 us (17%)
  starting transfers between devices  18.2 us (17%)
  local copies, waits for them, and re-layouts  5.91 us (5%)
  Pallas kernels  4.26 us (4%)
  between operations  1.39 us (1%)
    all_to_all x1, blocking collectives, local(): piece = jnp.sum(lax.all_to_all(copies, 'zc', 0, 0), axis=0)  33.1 us
    all_to_all x1, blocking collectives, local(): lax.all_to_all(term.reshape(peers, channels // peers, channels), ('y', 'x...  16 us
    ppermute x1, starting transfers between devices, local(): lax.ppermute(beside[0], ring, [(i + 1, i) for i in range(rows - 1)])  12.4 us
    all_to_all x1, blocking collectives, local(): parts = lax.all_to_all(summed, 'x', 0, 0)  10.9 us
    all_to_all x1, waiting for transfers between devices, local(): lax.all_to_all(copies, ('y', 'x'), 0, 0).reshape(channels, channels)  9.78 us
    ppermute x1, waiting for transfers between devices, local(): lax.ppermute(beside[1], ring, [(i, i + 1) for i in range(rows - 1)])  8.22 us
    unnamed x12, local copies, waits for them, and re-layouts  5.07 us
    all_to_all x1, starting transfers between devices, local(): lax.all_to_all(copies, ('y', 'x'), 0, 0).reshape(channels, channels)  3.87 us
  transfers between devices with their start and end apart: 3, of which 3 were waited for; matrix products, arithmetic and copies ran while one was open for 0% of the time, Pallas kernels for 1%

profile of v1, /device:TPU:1, one launch (start us, length us, event | category | flops | bytes accessed | tf_op | source)
XLA Modules:
  0.0 108.9 jit_solution(6152107949017452635)
XLA Ops:
  1.3 0.8 copy.10.slots
  2.1 0.1 pad_add_fusion.base
  2.1 0.0 copy-start
  2.1 1.7 %copy-done = bf16[72,128,128]{2,1,0:T(8,128)(2,1)S(1)} copy-done((bf16[72,128,128]{2,1,0:T(8,128)(2,1)S(1)}, bf16[72,128,128]{2,1,0:T(8,128)(2,1)}, u32[]{:S(2)}) %copy-start) | copy-done | bytes 2359320
  3.8 0.0 copy-start.1
  3.8 1.0 copy-done.1
  4.8 0.0 copy-start.3
  4.8 0.9 copy-done.3
  5.7 2.7 %tile_sums.1 = (bf16[2,12,256,128]{3,2,1,0:T(8,128)(2,1)S(1)}, f32[12,256,128]{2,1,0:T(8,128)S(1)}) custom-call(s32[2]{0:T(128)S(1)} %pad_add_fusion.base, s32[1]{0:T(128)S(6)} %copy.12.count, s32[72,3]{1,0:T(8,128)S(1)} %copy.10.slots, bf16[384,256]{1,0:T(8,128)(2,1)S(1)} %copy-done.3, f32[384,256]{1,0:T(8,128)S(1)} %copy-done.1, ...), custom_call_target="tpu_custom_call" | custom-call | tf_op jit(solution)/shard_map/tile_sums/pallas_call | solution.py:85
  8.4 0.1 slice_bitcast_fusion.1
  8.5 12.4 %collective-permute-start = (bf16[12,256,128]{2,1,0:T(8,128)(2,1)S(1)}, bf16[12,256,128]{2,1,0:T(8,128)(2,1)S(1)}, u32[]{:S(2)}, u32[]{:S(2)}) collective-permute-start(bf16[12,256,128]{2,1,0:T(8,128)(2,1)S(1)} %get-tuple-element.10), channel_id=1, source_target_pairs={{4,0},{8,4},{12,8},{16,12},{20,16},{24,20},{28,24},{32,28},{36,32}... | collective-permute-start | bytes 2359304 | tf_op jit(solution)/shard_map/ppermute | solution.py:101
  21.0 1.9 %collective-permute-start.1 = (bf16[12,256,128]{2,1,0:T(8,128)(2,1)S(1)}, bf16[12,256,128]{2,1,0:T(8,128)(2,1)S(1)}, u32[]{:S(2)}, u32[]{:S(2)}) collective-permute-start(bf16[12,256,128]{2,1,0:T(8,128)(2,1)S(1)} %get-tuple-element.11), channel_id=1, source_target_pairs={{0,4},{4,8},{8,12},{12,16},{16,20},{20,24},{24,28},{28,32},{32,36}... | collective-permute-start | bytes 2359304 | tf_op jit(solution)/shard_map/ppermute | solution.py:102
  22.9 0.7 collective-permute-done
  23.6 8.2 %collective-permute-done.1 = bf16[12,256,128]{2,1,0:T(8,128)(2,1)S(1)} collective-permute-done((bf16[12,256,128]{2,1,0:T(8,128)(2,1)S(1)}, bf16[12,256,128]{2,1,0:T(8,128)(2,1)S(1)}, u32[]{:S(2)}, u32[]{:S(2)}) %collective-permute-start.1) | collective-permute-done | bytes 786464 | tf_op jit(solution)/shard_map/ppermute | solution.py:102
  31.8 0.3 add_convert_fusion
  32.1 0.0 copy-start.2
  32.1 10.9 %all_to_all.20.parts = bf16[4,3,256,128]{3,2,1,0:T(8,128)(2,1)S(1)} all-to-all(bf16[4,3,256,128]{3,2,1,0:T(8,128)(2,1)S(1)} %bitcast.10), channel_id=1, replica_groups=mesh['y'=8,'zc'=24,'x'=4] {'x'}, dimensions={0} | all-to-all | bytes 1572864 | tf_op jit(solution)/shard_map/all_to_all | solution.py:105
  43.0 0.0 copy-done.2
  43.0 0.0 copy-start.4
  43.0 0.4 weight_term.1
  43.5 16.0 %all_to_all.21 = f32[32,8,256]{2,1,0:T(8,128)S(1)} all-to-all(f32[32,8,256]{2,1,0:T(8,128)S(1)} %bitcast.9), channel_id=1, replica_groups=mesh['y'=8,'zc'=24,'x'=4] {'y','x'}, dimensions={0} | all-to-all | bytes 524288 | tf_op jit(solution)/shard_map/all_to_all | solution.py:126
  59.5 33.1 %all_to_all.22 = f32[24,8,256]{2,1,0:T(8,128)S(1)} all-to-all(f32[24,8,256]{2,1,0:T(8,128)S(1)} %broadcast_in_dim.4), channel_id=1, replica_groups=mesh['y'=8,'zc'=24,'x'=4] {'zc'}, dimensions={0} | all-to-all | bytes 393216 | tf_op jit(solution)/shard_map/all_to_all | solution.py:129
  92.7 0.7 broadcast_in_dim.5
  93.4 3.9 %all-to-all-start.3 = ((f32[32,8,256]{2,1,0:T(8,128)}), f32[32,8,256]{2,1,0:T(8,128)S(1)}, u32[]{:S(2)}, u32[]{:S(2)}) async-start(f32[32,8,256]{2,1,0:T(8,128)} %broadcast_in_dim.5), calls=%async_computation.3 | async-start | bytes 524288 | tf_op jit(solution)/shard_map/all_to_all | solution.py:132
  97.3 0.0 copy-done.4
  97.3 1.1 %feature_grad.1 = f32[384,256]{1,0:T(8,128)} custom-call(f32[3,256,128]{2,1,0:T(8,128)S(1)} %get-tuple-element.8.summed, bf16[256,256]{1,0:T(8,128)(2,1)S(1)} %copy-done.4), custom_call_target="tpu_custom_call" | custom-call | tf_op jit(solution)/shard_map/feature_grad/pallas_call | solution.py:117
  98.4 9.8 %all-to-all-done.3 = f32[32,8,256]{2,1,0:T(8,128)S(1)} async-done(((f32[32,8,256]{2,1,0:T(8,128)}), f32[32,8,256]{2,1,0:T(8,128)S(1)}, u32[]{:S(2)}, u32[]{:S(2)}) %all-to-all-start.3) | async-done | bytes 262176 | tf_op jit(solution)/shard_map/all_to_all | solution.py:132
  108.2 0.7 copy.13
  (4 shorter events, 0.1 us)
Async XLA Ops:
  2.1 1.7 %copy-start = (bf16[72,128,128]{2,1,0:T(8,128)(2,1)S(1)}, bf16[72,128,128]{2,1,0:T(8,128)(2,1)}, u32[]{:S(2)}) copy-start(bf16[72,128,128]{2,1,0:T(8,128)(2,1)} %tiles.1) | copy-start | bytes 7077892
  3.8 1.0 copy-start.1
  4.8 0.9 copy-start.3
  8.5 15.1 %collective-permute-start = (bf16[12,256,128]{2,1,0:T(8,128)(2,1)S(1)}, bf16[12,256,128]{2,1,0:T(8,128)(2,1)S(1)}, u32[]{:S(2)}, u32[]{:S(2)}) collective-permute-start(bf16[12,256,128]{2,1,0:T(8,128)(2,1)S(1)} %get-tuple-element.10), channel_id=1, source_target_pairs={{4,0},{8,4},{12,8},{16,12},{20,16},{24,20},{28,24},{32,28},{36,32}... | collective-permute-start | bytes 2359304 | tf_op jit(solution)/shard_map/ppermute | solution.py:101
  21.0 10.8 %collective-permute-start.1 = (bf16[12,256,128]{2,1,0:T(8,128)(2,1)S(1)}, bf16[12,256,128]{2,1,0:T(8,128)(2,1)S(1)}, u32[]{:S(2)}, u32[]{:S(2)}) collective-permute-start(bf16[12,256,128]{2,1,0:T(8,128)(2,1)S(1)} %get-tuple-element.11), channel_id=1, source_target_pairs={{0,4},{4,8},{8,12},{12,16},{16,20},{20,24},{24,28},{28,32},{32,36}... | collective-permute-start | bytes 2359304 | tf_op jit(solution)/shard_map/ppermute | solution.py:102
  32.1 10.9 %copy-start.2 = (bf16[384,256]{1,0:T(8,128)(2,1)S(1)}, bf16[384,256]{1,0:T(8,128)(2,1)}, u32[]{:S(2)}) copy-start(bf16[384,256]{1,0:T(8,128)(2,1)} %features.1) | copy-start | bytes 589828
  43.0 54.2 %copy-start.4 = (bf16[256,256]{1,0:T(8,128)(2,1)S(1)}, bf16[256,256]{1,0:T(8,128)(2,1)}, u32[]{:S(2)}) copy-start(bf16[256,256]{1,0:T(8,128)(2,1)} %weight.1) | copy-start | bytes 393220
  93.4 14.8 %all-to-all-start.3 = ((f32[32,8,256]{2,1,0:T(8,128)}), f32[32,8,256]{2,1,0:T(8,128)S(1)}, u32[]{:S(2)}, u32[]{:S(2)}) async-start(f32[32,8,256]{2,1,0:T(8,128)} %broadcast_in_dim.5), calls=%async_computation.3 | async-start | bytes 524288 | tf_op jit(solution)/shard_map/all_to_all | solution.py:132

commit v2 on v1

v2 whole, which is shorter than its diff:
```python
import functools
import math

import jax
import jax.numpy as jnp
from jax import lax
from jax.experimental import pallas as pl
from jax.experimental.pallas import tpu as pltpu
from jax.sharding import Mesh, PartitionSpec as P

GROUP = 24
VMEM = pl.BlockSpec(memory_space=pltpu.VMEM)
SMEM = pl.BlockSpec(memory_space=pltpu.SMEM)
HBM = pl.BlockSpec(memory_space=pltpu.HBM)


def tile_kernel(
    count, slots_hbm, pre_hbm, up_hbm, tiles_hbm,
    cross, chip, own,
    slots, pre, up, tiles, masked_t, total, arrived,
):
    pairs = ((slots_hbm, slots), (up_hbm, up), (pre_hbm, pre), (tiles_hbm, tiles))
    copies = [pltpu.make_async_copy(a, b, arrived.at[i]) for i, (a, b) in enumerate(pairs)]
    for copy in copies:
        copy.start()
    total[...] = jnp.zeros_like(total)
    blocks, _, edge = masked_t.shape
    width = own.shape[0]
    copies[1].wait()
    copies[2].wait()
    for d in range(blocks):
        rows = pl.ds(d * edge, edge)
        kept = jnp.where(pre[rows, :].astype(jnp.float32) > 0, up[rows, :], 0.0)
        masked_t[d] = kept.T.astype(jnp.bfloat16)
    copies[0].wait()
    copies[3].wait()
    live = count[0]
    row = slots[0, 0] // width
    first = (row - 1) * width

    def body(group, carry):
        for u in range(GROUP):
            slot = group * GROUP + u
            dst = slots[0, slot] % blocks
            src = slots[1, slot] - first
            tile = tiles[slots[2, slot]]
            tile = jnp.where(slot < live, tile, jnp.zeros_like(tile))
            total[src] += jnp.dot(masked_t[dst], tile, preferred_element_type=jnp.float32)
        return carry

    lax.fori_loop(0, (live + GROUP - 1) // GROUP, body, 0)
    core = row % 2
    cross[...] = total[pl.ds(2 * core * width, width)].astype(jnp.bfloat16)
    chip[...] = total[pl.ds(2 * (1 - core) * width, width)].astype(jnp.bfloat16)
    own[...] = total[pl.ds(width, width)]


def split(value):
    high = value.astype(jnp.bfloat16)
    return high, (value - high.astype(jnp.float32)).astype(jnp.bfloat16)


def weight_kernel(parts, features, summed, term):
    peers, blocks, _, edge = parts.shape
    acc = None
    for b in range(blocks):
        g = parts[0, b].astype(jnp.float32)
        for p in range(1, peers):
            g = g + parts[p, b].astype(jnp.float32)
        summed[b] = g
        feat = features[pl.ds(b * edge, edge), :]
        for piece in split(g):
            prod = jnp.dot(piece, feat, preferred_element_type=jnp.float32)
            acc = prod if acc is None else acc + prod
    acc = acc.T
    _, height, breadth = term.shape
    across = acc.shape[1] // breadth
    for i in range(acc.shape[0] // height):
        for j in range(across):
            term[i * across + j] = acc[
                i * height : (i + 1) * height, j * breadth : (j + 1) * breadth
            ]


def feature_kernel(summed, weight, grad):
    blocks, _, edge = summed.shape
    for b in range(blocks):
        acc = None
        for piece in split(summed[b].T):
            prod = lax.dot_general(
                piece, weight[...], (((1,), (1,)), ((), ())), preferred_element_type=jnp.float32
            )
            acc = prod if acc is None else acc + prod
        grad[pl.ds(b * edge, edge), :] = acc


def swap(array, axes, count, first):
    pairs = [(i, i + 1) for i in range(first, count - 1, 2)]
    return lax.ppermute(array, axes, pairs + [(j, i) for i, j in pairs])


def local(features, pre_act, upstream, weight, tile_values, tile_list, tile_counts, *, sizes):
    y, z, x = sizes
    rows = y * z * 2
    rows_dev, channels = features.shape
    slot_count, edge = tile_values.shape[:2]
    blocks = rows_dev // edge
    width = x * blocks
    params = pltpu.CompilerParams(vmem_limit_bytes=40 << 20)
    held = [
        pltpu.with_memory_space_constraint(a, pltpu.HBM)
        for a in (tile_list.T, pre_act, upstream, tile_values)
    ]
    cross, chip, own = pl.pallas_call(
        tile_kernel,
        out_shape=(
            jax.ShapeDtypeStruct((width, channels, edge), jnp.bfloat16),
            jax.ShapeDtypeStruct((width, channels, edge), jnp.bfloat16),
            jax.ShapeDtypeStruct((width, channels, edge), jnp.float32),
        ),
        in_specs=[SMEM] + [HBM] * 4,
        out_specs=(VMEM,) * 3,
        scratch_shapes=[
            pltpu.SMEM((3, slot_count), jnp.int32),
            pltpu.VMEM((rows_dev, channels), jnp.bfloat16),
            pltpu.VMEM((rows_dev, channels), jnp.float32),
            pltpu.VMEM((slot_count, edge, edge), jnp.bfloat16),
            pltpu.VMEM((blocks, channels, edge), jnp.bfloat16),
            pltpu.VMEM((3 * width, channels, edge), jnp.float32),
            pltpu.SemaphoreType.DMA((4,)),
        ],
        compiler_params=params,
        name="tile_sums",
    )(tile_counts, *held)
    from_cross = swap(cross, ("y", "z", "core"), rows, 1)
    from_chip = swap(chip, "core", 2, 0)
    summed = own + from_cross.astype(jnp.float32) + from_chip.astype(jnp.float32)
    summed = summed.astype(jnp.bfloat16).reshape(x, blocks, channels, edge)
    parts = lax.all_to_all(summed, "x", 0, 0)
    peers = y * 2 * x
    across = channels // 128
    height = channels * across // peers
    grad_t, term = pl.pallas_call(
        weight_kernel,
        out_shape=(
            jax.ShapeDtypeStruct((blocks, channels, edge), jnp.float32),
            jax.ShapeDtypeStruct((peers, height, 128), jnp.float32),
        ),
        in_specs=[VMEM] * 2,
        out_specs=(VMEM, VMEM),
        compiler_params=params,
        name="weight_term",
    )(parts, features)
    grad_features = pl.pallas_call(
        feature_kernel,
        out_shape=jax.ShapeDtypeStruct((rows_dev, channels), jnp.float32),
        in_specs=[VMEM] * 2,
        out_specs=VMEM,
        compiler_params=params,
        name="feature_grad",
    )(grad_t, weight)
    plane = ("y", "core", "x")
    piece = jnp.sum(lax.all_to_all(term, plane, 0, 0), axis=0)
    copies = jnp.broadcast_to(piece[None], (z,) + piece.shape)
    piece = jnp.sum(lax.all_to_all(copies, "z", 0, 0), axis=0)
    piece = piece / math.sqrt(rows * x * rows_dev)
    copies = jnp.broadcast_to(piece[None], (peers,) + piece.shape)
    pieces = lax.all_to_all(copies, plane, 0, 0).reshape(-1, across, height, 128)
    grad_weight = pieces.transpose(0, 2, 1, 3).reshape(channels, channels)
    return (grad_features, grad_weight)


def solution(mesh):
    rows, x = mesh.devices.shape
    y = math.gcd(rows, 8)
    z = rows // y // 2
    every = ("y", "z", "core", "x")
    fine = Mesh(mesh.devices.reshape(y, z, 2, x), every)
    return jax.shard_map(
        functools.partial(local, sizes=(y, z, x)),
        mesh=fine,
        in_specs=(
            P(every, None),
            P(every, None),
            P(every, None),
            P(),
            P(every, None, None),
            P(every, None),
            P(every),
        ),
        out_specs=(P(every, None), P()),
        check_vma=False,
    )
```

time: 110 us -> 105 us (0.955)
  waiting for transfers between devices: 18.7 us -> 13.2 us
  local copies, waits for them, and re-layouts: 5.91 us -> 1.44 us
  blocking collectives: 60 us -> 63.1 us
  starting transfers between devices: 18.2 us -> 20.7 us
    ppermute x2, waiting for transfers between devices: 8.91 us -> 1.91 us  [swap(): return lax.ppermute(array, axes, pairs + [(j, i) for i, j in pairs])]
    all_to_all x1, blocking collectives: 10.9 us -> 15.9 us  [local(): parts = lax.all_to_all(summed, 'x', 0, 0)]
    unnamed x12 -> x5, local copies, waits for them, and re-layouts: 5.07 us -> 0.71 us
    all_to_all x1, starting transfers between devices: 3.87 us -> 7.53 us  [local(): lax.all_to_all(copies, plane, 0, 0).reshape(-1, across, height, 128)]
    all_to_all x2, blocking collectives: 49.1 us -> 47.2 us  [the longest x1 29.4 us: local(): piece = jnp.sum(lax.all_to_all(term, plane, 0, 0), axis=0)]
    all_to_all x1, waiting for transfers between devices: 9.78 us -> 11.3 us  [local(): lax.all_to_all(copies, plane, 0, 0).reshape(-1, across, height, 128)]
    ppermute x2, starting transfers between devices: 14.3 us -> 13.1 us  [swap(): return lax.ppermute(array, axes, pairs + [(j, i) for i, j in pairs])]
  transfers between devices with their start and end apart: 3 -> 3, of which waited for: 3 -> 2; matrix products, arithmetic and copies ran while one was open for 0% -> 0% of each run, Pallas kernels for 1% -> 1%
where the time goes in v2:
time: 105 us
  blocking collectives  63.1 us (60%)
  starting transfers between devices  20.7 us (20%)
  waiting for transfers between devices  13.2 us (13%)
  Pallas kernels  4.36 us (4%)
  local copies, waits for them, and re-layouts  1.44 us (1%)
  between operations  1.35 us (1%)
    all_to_all x1, blocking collectives, local(): piece = jnp.sum(lax.all_to_all(term, plane, 0, 0), axis=0)  29.4 us
    all_to_all x1, blocking collectives, local(): piece = jnp.sum(lax.all_to_all(copies, 'z', 0, 0), axis=0)  17.8 us
    all_to_all x1, blocking collectives, local(): parts = lax.all_to_all(summed, 'x', 0, 0)  15.9 us
    ppermute x2, starting transfers between devices, swap(): return lax.ppermute(array, axes, pairs + [(j, i) for i, j in pairs])  13.1 us
    all_to_all x1, waiting for transfers between devices, local(): lax.all_to_all(copies, plane, 0, 0).reshape(-1, across, height, 128)  11.3 us
    all_to_all x1, starting transfers between devices, local(): lax.all_to_all(copies, plane, 0, 0).reshape(-1, across, height, 128)  7.53 us
    pallas_call x1, Pallas kernels, local(): pl.pallas_call(tile_kernel, out_shape=(jax.ShapeDtypeStruct((width, chann...  2.78 us
  transfers between devices with their start and end apart: 3, of which 2 were waited for; matrix products, arithmetic and copies ran while one was open for 0% of the time, Pallas kernels for 1%

profile of v2, /device:TPU:1, one launch (start us, length us, event | category | flops | bytes accessed | tf_op | source)
XLA Modules:
  0.0 104.5 jit_solution(3300431251000062332)
XLA Ops:
  1.3 2.8 %tile_sums.1 = (bf16[12,256,128]{2,1,0:T(8,128)(2,1)S(1)}, bf16[12,256,128]{2,1,0:T(8,128)(2,1)S(1)}, f32[12,256,128]{2,1,0:T(8,128)S(1)}) custom-call(s32[1]{0:T(128)S(6)} %copy.10.count, s32[3,72]{1,0:T(4,128)} %bitcast.9, bf16[384,256]{1,0:T(8,128)(2,1)} %pre_hbm.1, f32[384,256]{1,0:T(8,128)} %up_hbm.1, bf16[72,128,128]{2,1,0:T(8,128)(2,1)} %tiles_hbm.1), custom_call_target="tpu_custom_call" | custom-call | tf_op jit(solution)/shard_map/tile_sums/pallas_call | solution.py:114
  4.1 5.4 %collective-permute-start = (bf16[12,256,128]{2,1,0:T(8,128)(2,1)S(1)}, bf16[12,256,128]{2,1,0:T(8,128)(2,1)S(1)}, u32[]{:S(2)}, u32[]{:S(2)}) collective-permute-start(bf16[12,256,128]{2,1,0:T(8,128)(2,1)S(1)} %get-tuple-element.8), channel_id=1, source_target_pairs={{4,8},{12,16},{20,24},{28,32},{36,40},{44,48},{52,56},{60,64},{68,... | collective-permute-start | bytes 2359304 | tf_op jit(solution)/shard_map/ppermute | solution.py:99
  9.5 7.7 %collective-permute-start.1 = (bf16[12,256,128]{2,1,0:T(8,128)(2,1)S(1)}, bf16[12,256,128]{2,1,0:T(8,128)(2,1)S(1)}, u32[]{:S(2)}, u32[]{:S(2)}) collective-permute-start(bf16[12,256,128]{2,1,0:T(8,128)(2,1)S(1)} %get-tuple-element.9), channel_id=1, source_target_pairs={{0,4},{4,0},{1,5},{5,1},{2,6},{6,2},{3,7},{7,3},{8,12},{12,8},{9,1... | collective-permute-start | bytes 2359304 | tf_op jit(solution)/shard_map/ppermute | solution.py:99
  17.2 1.9 %collective-permute-done = bf16[12,256,128]{2,1,0:T(8,128)(2,1)S(1)} collective-permute-done((bf16[12,256,128]{2,1,0:T(8,128)(2,1)S(1)}, bf16[12,256,128]{2,1,0:T(8,128)(2,1)S(1)}, u32[]{:S(2)}, u32[]{:S(2)}) %collective-permute-start) | collective-permute-done | bytes 786464 | tf_op jit(solution)/shard_map/ppermute | solution.py:99
  19.1 0.0 collective-permute-done.1
  19.1 0.3 add_convert_fusion
  19.4 0.0 copy-start
  19.5 15.9 %all_to_all.20.parts = bf16[4,3,256,128]{3,2,1,0:T(8,128)(2,1)S(1)} all-to-all(bf16[4,3,256,128]{3,2,1,0:T(8,128)(2,1)S(1)} %bitcast.7), channel_id=1, replica_groups=mesh['y'=8,'z'=12,'core'=2,'x'=4] {'x'}, dimensions={0} | all-to-all | bytes 1572864 | tf_op jit(solution)/shard_map/all_to_all | solution.py:139
  35.4 0.0 copy-done
  35.4 0.0 copy-start.1
  35.4 0.4 weight_term.1
  35.8 29.4 %all_to_all.21 = f32[64,8,128]{2,1,0:T(8,128)S(1)} all-to-all(f32[64,8,128]{2,1,0:T(8,128)S(1)} %get-tuple-element.11), channel_id=1, replica_groups=mesh['y'=8,'z'=12,'core'=2,'x'=4] {'y','core','x'}, dimensions={0} | all-to-all | bytes 524288 | tf_op jit(solution)/shard_map/all_to_all | solution.py:163
  65.2 0.1 reduce_sum.18
  65.2 17.8 %all_to_all.22 = f32[12,8,128]{2,1,0:T(8,128)S(1)} all-to-all(f32[12,8,128]{2,1,0:T(8,128)S(1)} %broadcast_in_dim.4), channel_id=1, replica_groups=mesh['y'=8,'z'=12,'core'=2,'x'=4] {'z'}, dimensions={0} | all-to-all | bytes 98304 | tf_op jit(solution)/shard_map/all_to_all | solution.py:165
  83.1 0.7 broadcast_in_dim.5
  83.8 7.5 %all-to-all-start.3 = ((f32[64,8,128]{2,1,0:T(8,128)}), f32[64,8,128]{2,1,0:T(8,128)S(1)}, u32[]{:S(2)}, u32[]{:S(2)}) async-start(f32[64,8,128]{2,1,0:T(8,128)} %broadcast_in_dim.5), calls=%async_computation.3 | async-start | bytes 524288 | tf_op jit(solution)/shard_map/all_to_all | solution.py:168
  91.4 0.0 copy-done.1
  91.4 1.1 %feature_grad.1 = f32[384,256]{1,0:T(8,128)} custom-call(f32[3,256,128]{2,1,0:T(8,128)S(1)} %get-tuple-element.10.summed, bf16[256,256]{1,0:T(8,128)(2,1)S(1)} %copy-done.1), custom_call_target="tpu_custom_call" | custom-call | tf_op jit(solution)/shard_map/feature_grad/pallas_call | solution.py:154
  92.5 11.3 %all-to-all-done.3 = f32[64,8,128]{2,1,0:T(8,128)S(1)} async-done(((f32[64,8,128]{2,1,0:T(8,128)}), f32[64,8,128]{2,1,0:T(8,128)S(1)}, u32[]{:S(2)}, u32[]{:S(2)}) %all-to-all-start.3) | async-done | bytes 262176 | tf_op jit(solution)/shard_map/all_to_all | solution.py:168
  103.8 0.7 copy.11
  (3 shorter events, 0.0 us)
Async XLA Ops:
  4.1 15.1 %collective-permute-start = (bf16[12,256,128]{2,1,0:T(8,128)(2,1)S(1)}, bf16[12,256,128]{2,1,0:T(8,128)(2,1)S(1)}, u32[]{:S(2)}, u32[]{:S(2)}) collective-permute-start(bf16[12,256,128]{2,1,0:T(8,128)(2,1)S(1)} %get-tuple-element.8), channel_id=1, source_target_pairs={{4,8},{12,16},{20,24},{28,32},{36,40},{44,48},{52,56},{60,64},{68,... | collective-permute-start | bytes 2359304 | tf_op jit(solution)/shard_map/ppermute | solution.py:99
  9.5 9.7 %collective-permute-start.1 = (bf16[12,256,128]{2,1,0:T(8,128)(2,1)S(1)}, bf16[12,256,128]{2,1,0:T(8,128)(2,1)S(1)}, u32[]{:S(2)}, u32[]{:S(2)}) collective-permute-start(bf16[12,256,128]{2,1,0:T(8,128)(2,1)S(1)} %get-tuple-element.9), channel_id=1, source_target_pairs={{0,4},{4,0},{1,5},{5,1},{2,6},{6,2},{3,7},{7,3},{8,12},{12,8},{9,1... | collective-permute-start | bytes 2359304 | tf_op jit(solution)/shard_map/ppermute | solution.py:99
  19.4 15.9 %copy-start = (bf16[384,256]{1,0:T(8,128)(2,1)S(1)}, bf16[384,256]{1,0:T(8,128)(2,1)}, u32[]{:S(2)}) copy-start(bf16[384,256]{1,0:T(8,128)(2,1)} %features.1) | copy-start | bytes 589828
  35.4 56.0 %copy-start.1 = (bf16[256,256]{1,0:T(8,128)(2,1)S(1)}, bf16[256,256]{1,0:T(8,128)(2,1)}, u32[]{:S(2)}) copy-start(bf16[256,256]{1,0:T(8,128)(2,1)} %weight.1) | copy-start | bytes 393220
  83.8 20.0 %all-to-all-start.3 = ((f32[64,8,128]{2,1,0:T(8,128)}), f32[64,8,128]{2,1,0:T(8,128)S(1)}, u32[]{:S(2)}, u32[]{:S(2)}) async-start(f32[64,8,128]{2,1,0:T(8,128)} %broadcast_in_dim.5), calls=%async_computation.3 | async-start | bytes 524288 | tf_op jit(solution)/shard_map/all_to_all | solution.py:168

commit v3 on v2

--- a/solution.py
+++ b/solution.py
@@ -60,33 +60,79 @@
     return high, (value - high.astype(jnp.float32)).astype(jnp.bfloat16)
 
 
-def weight_kernel(parts, features, summed, term):
-    peers, blocks, _, edge = parts.shape
+def weight_kernel(own, cross, chip, features, packed):
+    blocks, channels, edge = own.shape
+    peers = packed.shape[0]
+    each = blocks // peers
     acc = None
-    for b in range(blocks):
-        g = parts[0, b].astype(jnp.float32)
-        for p in range(1, peers):
-            g = g + parts[p, b].astype(jnp.float32)
-        summed[b] = g
-        feat = features[pl.ds(b * edge, edge), :]
-        for piece in split(g):
+    for b in range(0, blocks, 2):
+        pair = []
+        for i in (b, b + 1):
+            g = own[i] + cross[i].astype(jnp.float32) + chip[i].astype(jnp.float32)
+            packed[i // each, pl.ds(i % each * channels, channels), :] = g.astype(jnp.bfloat16)
+            pair.append(g)
+        feat = features[pl.ds(b * edge, 2 * edge), :]
+        for piece in split(jnp.concatenate(pair, axis=1)):
             prod = jnp.dot(piece, feat, preferred_element_type=jnp.float32)
             acc = prod if acc is None else acc + prod
-    acc = acc.T
-    _, height, breadth = term.shape
-    across = acc.shape[1] // breadth
-    for i in range(acc.shape[0] // height):
-        for j in range(across):
-            term[i * across + j] = acc[
-                i * height : (i + 1) * height, j * breadth : (j + 1) * breadth
-            ]
-
-
-def feature_kernel(summed, weight, grad):
-    blocks, _, edge = summed.shape
-    for b in range(blocks):
+    rows = acc.shape[1] // peers
+    at = each * channels
+    for piece in split(acc.T):
+        for j in range(acc.shape[0] // edge):
+            for c in range(peers):
+                packed[c, pl.ds(at, rows), :] = piece[
+                    c * rows : (c + 1) * rows, j * edge : (j + 1) * edge
+                ]
+            at += rows
+
+
+def term_kernel(halves, packed, term):
+    peers, depth, _ = packed.shape
+    parts, both, _ = term.shape
+    height = both // halves
+    rows = parts * height
+    start = depth - 2 * halves * rows
+    for j in range(halves):
         acc = None
-        for piece in split(summed[b].T):
+        for p in range(peers):
+            for k in range(2):
+                value = packed[p, pl.ds(start + (k * halves + j) * rows, rows), :]
+                value = value.astype(jnp.float32)
+                acc = value if acc is None else acc + value
+        for q in range(parts):
+            term[q, pl.ds(j * height, height), :] = acc[q * height : (q + 1) * height, :]
+
+
+def spread_kernel(scale, got, copies):
+    acc = got[0].astype(jnp.float32)
+    for i in range(1, got.shape[0]):
+        acc = acc + got[i].astype(jnp.float32)
+    value = (acc / scale).astype(copies.dtype)
+    for i in range(copies.shape[0]):
+        copies[i] = value
+
+
+def spread(got, count, scale):
+    return pl.pallas_call(
+        functools.partial(spread_kernel, scale),
+        out_shape=jax.ShapeDtypeStruct((count,) + got.shape[1:], jnp.bfloat16),
+        in_specs=[VMEM],
+        out_specs=VMEM,
+        compiler_params=pltpu.CompilerParams(vmem_limit_bytes=16 << 20),
+        name="spread",
+    )(got)
+
+
+def feature_kernel(packed, weight, grad):
+    peers, _, edge = packed.shape
+    channels = weight.shape[0]
+    for b in range(grad.shape[0] // edge):
+        rows = pl.ds(b * channels, channels)
+        g = packed[0, rows, :].astype(jnp.float32)
+        for p in range(1, peers):
+            g = g + packed[p, rows, :].astype(jnp.float32)
+        acc = None
+        for piece in split(g.T):
             prod = lax.dot_general(
                 piece, weight[...], (((1,), (1,)), ((), ())), preferred_element_type=jnp.float32
             )
@@ -107,6 +153,7 @@
     blocks = rows_dev // edge
     width = x * blocks
     params = pltpu.CompilerParams(vmem_limit_bytes=40 << 20)
+    group = lax.all_to_all(jnp.broadcast_to(features[None], (x,) + features.shape), "x", 0, 0)
     held = [
         pltpu.with_memory_space_constraint(a, pltpu.HBM)
         for a in (tile_list.T, pre_act, upstream, tile_values)
@@ -134,23 +181,27 @@
     )(tile_counts, *held)
     from_cross = swap(cross, ("y", "z", "core"), rows, 1)
     from_chip = swap(chip, "core", 2, 0)
-    summed = own + from_cross.astype(jnp.float32) + from_chip.astype(jnp.float32)
-    summed = summed.astype(jnp.bfloat16).reshape(x, blocks, channels, edge)
-    parts = lax.all_to_all(summed, "x", 0, 0)
-    peers = y * 2 * x
-    across = channels // 128
-    height = channels * across // peers
-    grad_t, term = pl.pallas_call(
+    halves = channels // edge
+    height = channels // (x * y)
+    packed = pl.pallas_call(
         weight_kernel,
-        out_shape=(
-            jax.ShapeDtypeStruct((blocks, channels, edge), jnp.float32),
-            jax.ShapeDtypeStruct((peers, height, 128), jnp.float32),
+        out_shape=jax.ShapeDtypeStruct(
+            (x, blocks * channels + 2 * halves * channels // x, edge), jnp.bfloat16
         ),
-        in_specs=[VMEM] * 2,
-        out_specs=(VMEM, VMEM),
+        in_specs=[VMEM] * 4,
+        out_specs=VMEM,
         compiler_params=params,
         name="weight_term",
-    )(parts, features)
+    )(own, from_cross, from_chip, group.reshape(x * rows_dev, channels))
+    packed = lax.all_to_all(packed, "x", 0, 0)
+    term = pl.pallas_call(
+        functools.partial(term_kernel, halves),
+        out_shape=jax.ShapeDtypeStruct((y, halves * height, edge), jnp.float32),
+        in_specs=[VMEM],
+        out_specs=VMEM,
+        compiler_params=params,
+        name="term_sum",
+    )(packed)
     grad_features = pl.pallas_call(
         feature_kernel,
         out_shape=jax.ShapeDtypeStruct((rows_dev, channels), jnp.float32),
@@ -158,14 +209,13 @@
         out_specs=VMEM,
         compiler_params=params,
         name="feature_grad",
-    )(grad_t, weight)
-    plane = ("y", "core", "x")
-    piece = jnp.sum(lax.all_to_all(term, plane, 0, 0), axis=0)
-    copies = jnp.broadcast_to(piece[None], (z,) + piece.shape)
-    piece = jnp.sum(lax.all_to_all(copies, "z", 0, 0), axis=0)
-    piece = piece / math.sqrt(rows * x * rows_dev)
-    copies = jnp.broadcast_to(piece[None], (peers,) + piece.shape)
-    pieces = lax.all_to_all(copies, plane, 0, 0).reshape(-1, across, height, 128)
+    )(packed, weight)
+    got = lax.all_to_all(term, "y", 0, 0)
+    copies = spread(got, 2 * z, math.sqrt(rows * x * rows_dev))
+    got = lax.all_to_all(copies, ("z", "core"), 0, 0)
+    copies = spread(got, x * y, 1.0)
+    pieces = lax.all_to_all(copies, ("x", "y"), 0, 0).astype(jnp.float32)
+    pieces = pieces.reshape(x * y, halves, height, edge)
     grad_weight = pieces.transpose(0, 2, 1, 3).reshape(channels, channels)
     return (grad_features, grad_weight)
 

time: 105 us -> 102 us (0.971)
  blocking collectives: 63.1 us -> 69.2 us
  waiting for transfers between devices: 13.2 us -> 7.98 us
  starting transfers between devices: 20.7 us -> 16.4 us
  Pallas kernels: 4.36 us -> 5.97 us
  local copies, waits for them, and re-layouts: 1.44 us -> 0.06 us
    all_to_all x3 -> x4, blocking collectives: 63.1 us -> 69.2 us  [the longest x1 20.7 us: local(): got = lax.all_to_all(term, 'y', 0, 0)]
    all_to_all x1, starting transfers between devices: 7.53 us -> 3.86 us  [local(): pieces = lax.all_to_all(copies, ('x', 'y'), 0, 0).astype(jnp.float32)]
    all_to_all x1, waiting for transfers between devices: 11.3 us -> 7.97 us  [local(): pieces = lax.all_to_all(copies, ('x', 'y'), 0, 0).astype(jnp.float32)]
    ppermute x2, waiting for transfers between devices: 1.91 us -> 0.01 us  [swap(): return lax.ppermute(array, axes, pairs + [(j, i) for i, j in pairs])]
  transfers between devices with their start and end apart: 3 -> 3, of which waited for: 2 -> 1; matrix products, arithmetic and copies ran while one was open for 0% -> 0% of each run, Pallas kernels for 1% -> 1%
where the time goes in v3:
time: 102 us
  blocking collectives  69.2 us (68%)
  starting transfers between devices  16.4 us (16%)
  waiting for transfers between devices  7.98 us (8%)
  Pallas kernels  5.97 us (6%)
  between operations  1.4 us (1%)
    all_to_all x1, blocking collectives, local(): got = lax.all_to_all(term, 'y', 0, 0)  20.7 us
    all_to_all x1, blocking collectives, local(): got = lax.all_to_all(copies, ('z', 'core'), 0, 0)  17.4 us
    all_to_all x1, blocking collectives, local(): packed = lax.all_to_all(packed, 'x', 0, 0)  16.6 us
    all_to_all x1, blocking collectives, local(): lax.all_to_all(jnp.broadcast_to(features[None], (x,) + features.shape), '...  14.6 us
    ppermute x2, starting transfers between devices, swap(): return lax.ppermute(array, axes, pairs + [(j, i) for i, j in pairs])  12.5 us
    all_to_all x1, waiting for transfers between devices, local(): pieces = lax.all_to_all(copies, ('x', 'y'), 0, 0).astype(jnp.float32)  7.97 us
    all_to_all x1, starting transfers between devices, local(): pieces = lax.all_to_all(copies, ('x', 'y'), 0, 0).astype(jnp.float32)  3.86 us
    pallas_call x1, Pallas kernels, local(): pl.pallas_call(tile_kernel, out_shape=(jax.ShapeDtypeStruct((width, chann...  3.37 us
  transfers between devices with their start and end apart: 3, of which 1 were waited for; matrix products, arithmetic and copies ran while one was open for 0% of the time, Pallas kernels for 1%

profile of v3, /device:TPU:1, one launch (start us, length us, event | category | flops | bytes accessed | tf_op | source)
XLA Modules:
  0.0 101.8 jit_solution(12527048708545446416)
XLA Ops:
  0.6 0.0 copy-start.1
  1.3 3.4 %tile_sums.1 = (bf16[12,256,128]{2,1,0:T(8,128)(2,1)S(1)}, bf16[12,256,128]{2,1,0:T(8,128)(2,1)S(1)}, f32[12,256,128]{2,1,0:T(8,128)S(1)}) custom-call(s32[1]{0:T(128)S(6)} %copy.9.count, s32[3,72]{1,0:T(4,128)} %bitcast.10, bf16[384,256]{1,0:T(8,128)(2,1)} %pre_hbm.1, f32[384,256]{1,0:T(8,128)} %up_hbm.1, bf16[72,128,128]{2,1,0:T(8,128)(2,1)} %tiles_hbm.1), custom_call_target="tpu_custom_call" | custom-call | tf_op jit(solution)/shard_map/tile_sums/pallas_call | solution.py:161
  4.7 4.8 %collective-permute-start = (bf16[12,256,128]{2,1,0:T(8,128)(2,1)S(1)}, bf16[12,256,128]{2,1,0:T(8,128)(2,1)S(1)}, u32[]{:S(2)}, u32[]{:S(2)}) collective-permute-start(bf16[12,256,128]{2,1,0:T(8,128)(2,1)S(1)} %get-tuple-element.6), channel_id=1, source_target_pairs={{4,8},{12,16},{20,24},{28,32},{36,40},{44,48},{52,56},{60,64},{68,... | collective-permute-start | bytes 2359304 | tf_op jit(solution)/shard_map/ppermute | solution.py:145
  9.5 7.7 %collective-permute-start.1 = (bf16[12,256,128]{2,1,0:T(8,128)(2,1)S(1)}, bf16[12,256,128]{2,1,0:T(8,128)(2,1)S(1)}, u32[]{:S(2)}, u32[]{:S(2)}) collective-permute-start(bf16[12,256,128]{2,1,0:T(8,128)(2,1)S(1)} %get-tuple-element.7), channel_id=1, source_target_pairs={{0,4},{4,0},{1,5},{5,1},{2,6},{6,2},{3,7},{7,3},{8,12},{12,8},{9,1... | collective-permute-start | bytes 2359304 | tf_op jit(solution)/shard_map/ppermute | solution.py:145
  17.3 0.0 copy-done.1
  17.3 0.1 broadcast_in_dim.2
  17.3 14.6 %all_to_all.25 = bf16[4,384,256]{2,1,0:T(8,128)(2,1)S(1)} all-to-all(bf16[4,384,256]{2,1,0:T(8,128)(2,1)S(1)} %broadcast_in_dim.2), channel_id=1, replica_groups=mesh['y'=8,'z'=12,'core'=2,'x'=4] {'x'}, dimensions={0} | all-to-all | bytes 1572864 | tf_op jit(solution)/shard_map/all_to_all | solution.py:156
  31.9 0.0 collective-permute-done.cross
  31.9 0.0 collective-permute-done.1.chip
  31.9 0.7 weight_term.1
  32.6 0.0 copy-start
  32.6 16.6 %all_to_all.26.packed = bf16[4,1024,128]{2,1,0:T(8,128)(2,1)S(1)} all-to-all(bf16[4,1024,128]{2,1,0:T(8,128)(2,1)S(1)} %weight_term.1), channel_id=1, replica_groups=mesh['y'=8,'z'=12,'core'=2,'x'=4] {'x'}, dimensions={0} | all-to-all | bytes 2097152 | tf_op jit(solution)/shard_map/all_to_all | solution.py:196
  49.3 20.7 %all_to_all.27.got = f32[8,16,128]{2,1,0:T(8,128)S(1)} all-to-all(f32[8,16,128]{2,1,0:T(8,128)S(1)} %term_sum.1), channel_id=1, replica_groups=mesh['y'=8,'z'=12,'core'=2,'x'=4] {'y'}, dimensions={0} | all-to-all | bytes 131072 | tf_op jit(solution)/shard_map/all_to_all | solution.py:213
  70.0 17.4 %all_to_all.28.got = bf16[24,16,128]{2,1,0:T(8,128)(2,1)S(1)} all-to-all(bf16[24,16,128]{2,1,0:T(8,128)(2,1)S(1)} %spread.2), channel_id=1, replica_groups=mesh['y'=8,'z'=12,'core'=2,'x'=4] {'z','core'}, dimensions={0} | all-to-all | bytes 196608 | tf_op jit(solution)/shard_map/all_to_all | solution.py:215
  87.3 0.7 spread.3
  88.0 3.9 %all-to-all-start.4 = ((bf16[32,16,128]{2,1,0:T(8,128)(2,1)}), bf16[32,16,128]{2,1,0:T(8,128)(2,1)S(1)}, u32[]{:S(2)}, u32[]{:S(2)}) async-start(bf16[32,16,128]{2,1,0:T(8,128)(2,1)} %spread.3), calls=%async_computation.4 | async-start | bytes 262144 | tf_op jit(solution)/shard_map/all_to_all | solution.py:217
  91.9 0.0 copy-done
  91.9 1.2 %feature_grad.1 = f32[384,256]{1,0:T(8,128)} custom-call(bf16[4,1024,128]{2,1,0:T(8,128)(2,1)S(1)} %all_to_all.26.packed, bf16[256,256]{1,0:T(8,128)(2,1)S(1)} %copy-done), custom_call_target="tpu_custom_call" | custom-call | tf_op jit(solution)/shard_map/feature_grad/pallas_call | solution.py:205
  93.1 8.0 %all-to-all-done.4 = bf16[32,16,128]{2,1,0:T(8,128)(2,1)S(1)} async-done(((bf16[32,16,128]{2,1,0:T(8,128)(2,1)}), bf16[32,16,128]{2,1,0:T(8,128)(2,1)S(1)}, u32[]{:S(2)}, u32[]{:S(2)}) %all-to-all-start.4) | async-done | bytes 131104 | tf_op jit(solution)/shard_map/all_to_all | solution.py:217
  101.0 0.7 convert_bitcast_fusion
  (2 shorter events, 0.1 us)
Async XLA Ops:
  0.6 16.6 %copy-start.1 = (bf16[384,256]{1,0:T(8,128)(2,1)S(1)}, bf16[384,256]{1,0:T(8,128)(2,1)}, u32[]{:S(2)}) copy-start(bf16[384,256]{1,0:T(8,128)(2,1)} %param.7) | copy-start | bytes 589828
  4.7 27.2 %collective-permute-start = (bf16[12,256,128]{2,1,0:T(8,128)(2,1)S(1)}, bf16[12,256,128]{2,1,0:T(8,128)(2,1)S(1)}, u32[]{:S(2)}, u32[]{:S(2)}) collective-permute-start(bf16[12,256,128]{2,1,0:T(8,128)(2,1)S(1)} %get-tuple-element.6), channel_id=1, source_target_pairs={{4,8},{12,16},{20,24},{28,32},{36,40},{44,48},{52,56},{60,64},{68,... | collective-permute-start | bytes 2359304 | tf_op jit(solution)/shard_map/ppermute | solution.py:145
  9.5 22.4 %collective-permute-start.1 = (bf16[12,256,128]{2,1,0:T(8,128)(2,1)S(1)}, bf16[12,256,128]{2,1,0:T(8,128)(2,1)S(1)}, u32[]{:S(2)}, u32[]{:S(2)}) collective-permute-start(bf16[12,256,128]{2,1,0:T(8,128)(2,1)S(1)} %get-tuple-element.7), channel_id=1, source_target_pairs={{0,4},{4,0},{1,5},{5,1},{2,6},{6,2},{3,7},{7,3},{8,12},{12,8},{9,1... | collective-permute-start | bytes 2359304 | tf_op jit(solution)/shard_map/ppermute | solution.py:145
  32.6 59.3 %copy-start = (bf16[256,256]{1,0:T(8,128)(2,1)S(1)}, bf16[256,256]{1,0:T(8,128)(2,1)}, u32[]{:S(2)}) copy-start(bf16[256,256]{1,0:T(8,128)(2,1)} %weight.1) | copy-start | bytes 393220
  88.0 13.0 %all-to-all-start.4 = ((bf16[32,16,128]{2,1,0:T(8,128)(2,1)}), bf16[32,16,128]{2,1,0:T(8,128)(2,1)S(1)}, u32[]{:S(2)}, u32[]{:S(2)}) async-start(bf16[32,16,128]{2,1,0:T(8,128)(2,1)} %spread.3), calls=%async_computation.4 | async-start | bytes 262144 | tf_op jit(solution)/shard_map/all_to_all | solution.py:217

commit v4 on v2

--- a/solution.py
+++ b/solution.py
@@ -50,9 +50,12 @@
 
     lax.fori_loop(0, (live + GROUP - 1) // GROUP, body, 0)
     core = row % 2
-    cross[...] = total[pl.ds(2 * core * width, width)].astype(jnp.bfloat16)
-    chip[...] = total[pl.ds(2 * (1 - core) * width, width)].astype(jnp.bfloat16)
-    own[...] = total[pl.ds(width, width)]
+    col = slots[0, 0] // blocks % (width // blocks)
+    for k in range(width // blocks):
+        to, at = pl.ds(k * blocks, blocks), (k ^ col) * blocks
+        cross[to] = total[pl.ds(2 * core * width + at, blocks)].astype(jnp.bfloat16)
+        chip[to] = total[pl.ds(2 * (1 - core) * width + at, blocks)].astype(jnp.bfloat16)
+        own[to] = total[pl.ds(width + at, blocks)]
 
 
 def split(value):
@@ -60,33 +63,62 @@
     return high, (value - high.astype(jnp.float32)).astype(jnp.bfloat16)
 
 
-def weight_kernel(parts, features, summed, term):
-    peers, blocks, _, edge = parts.shape
+def weight_kernel(own, cross, chip, feat0, feat1, feat32, give, keep0, keep3, term):
+    blocks, channels, edge = keep0.shape
+    held = []
+    for k, (feat, at) in enumerate(((feat0, 0), (feat1, 0), (feat32, blocks), (feat32, 0))):
+        for b in range(blocks):
+            i = k * blocks + b
+            g = own[i] + cross[i].astype(jnp.float32) + chip[i].astype(jnp.float32)
+            if k == 0:
+                keep0[b] = g
+            elif k == 3:
+                keep3[b] = g
+            else:
+                give[(k - 1) * blocks + b] = g.astype(jnp.bfloat16)
+            held.append((g, feat, (at + b) * edge))
     acc = None
-    for b in range(blocks):
-        g = parts[0, b].astype(jnp.float32)
-        for p in range(1, peers):
-            g = g + parts[p, b].astype(jnp.float32)
-        summed[b] = g
-        feat = features[pl.ds(b * edge, edge), :]
-        for piece in split(g):
-            prod = jnp.dot(piece, feat, preferred_element_type=jnp.float32)
+    for (g, feat, at), (g2, feat2, at2) in zip(held[::2], held[1::2]):
+        rows = jnp.concatenate([feat[pl.ds(at, edge), :], feat2[pl.ds(at2, edge), :]], axis=0)
+        for piece in split(jnp.concatenate([g, g2], axis=1)):
+            prod = jnp.dot(piece, rows, preferred_element_type=jnp.float32)
             acc = prod if acc is None else acc + prod
     acc = acc.T
-    _, height, breadth = term.shape
-    across = acc.shape[1] // breadth
-    for i in range(acc.shape[0] // height):
-        for j in range(across):
-            term[i * across + j] = acc[
-                i * height : (i + 1) * height, j * breadth : (j + 1) * breadth
+    parts, both, _ = term.shape
+    height = acc.shape[0] // parts
+    for i in range(parts):
+        for j in range(both // height):
+            term[i, pl.ds(j * height, height), :] = acc[
+                i * height : (i + 1) * height, j * edge : (j + 1) * edge
             ]
 
 
-def feature_kernel(summed, weight, grad):
-    blocks, _, edge = summed.shape
+def spread_kernel(scale, got, copies):
+    acc = got[0].astype(jnp.float32)
+    for i in range(1, got.shape[0]):
+        acc = acc + got[i].astype(jnp.float32)
+    value = (acc / scale).astype(copies.dtype)
+    for i in range(copies.shape[0]):
+        copies[i] = value
+
+
+def spread(got, count, scale):
+    return pl.pallas_call(
+        functools.partial(spread_kernel, scale),
+        out_shape=jax.ShapeDtypeStruct((count,) + got.shape[1:], jnp.bfloat16),
+        in_specs=[VMEM],
+        out_specs=VMEM,
+        compiler_params=pltpu.CompilerParams(vmem_limit_bytes=16 << 20),
+        name="spread",
+    )(got)
+
+
+def feature_kernel(keep, pair, other, weight, grad):
+    blocks, _, edge = keep.shape
     for b in range(blocks):
+        g = keep[b] + pair[b].astype(jnp.float32) + other[b].astype(jnp.float32)
         acc = None
-        for piece in split(summed[b].T):
+        for piece in split(g.T):
             prod = lax.dot_general(
                 piece, weight[...], (((1,), (1,)), ((), ())), preferred_element_type=jnp.float32
             )
@@ -134,38 +166,43 @@
     )(tile_counts, *held)
     from_cross = swap(cross, ("y", "z", "core"), rows, 1)
     from_chip = swap(chip, "core", 2, 0)
-    summed = own + from_cross.astype(jnp.float32) + from_chip.astype(jnp.float32)
-    summed = summed.astype(jnp.bfloat16).reshape(x, blocks, channels, edge)
-    parts = lax.all_to_all(summed, "x", 0, 0)
-    peers = y * 2 * x
-    across = channels // 128
-    height = channels * across // peers
-    grad_t, term = pl.pallas_call(
+    near = [(i, i ^ 1) for i in range(x)]
+    far = [(i, i ^ 3) for i in range(x)]
+    feat1 = lax.ppermute(features, "x", near)
+    feat32 = lax.ppermute(jnp.concatenate([features, feat1], axis=0), "x", far)
+    halves = channels // edge
+    height = channels // (x * y)
+    third = (blocks, channels, edge)
+    give, keep0, keep3, term = pl.pallas_call(
         weight_kernel,
         out_shape=(
-            jax.ShapeDtypeStruct((blocks, channels, edge), jnp.float32),
-            jax.ShapeDtypeStruct((peers, height, 128), jnp.float32),
+            jax.ShapeDtypeStruct((2 * blocks, channels, edge), jnp.bfloat16),
+            jax.ShapeDtypeStruct(third, jnp.float32),
+            jax.ShapeDtypeStruct(third, jnp.float32),
+            jax.ShapeDtypeStruct((x * y, halves * height, edge), jnp.float32),
         ),
-        in_specs=[VMEM] * 2,
-        out_specs=(VMEM, VMEM),
+        in_specs=[VMEM] * 6,
+        out_specs=(VMEM,) * 4,
         compiler_params=params,
         name="weight_term",
-    )(parts, features)
+    )(own, from_cross, from_chip, features, feat1, feat32)
+    from_near = lax.ppermute(give, "x", near)
+    onward = (keep3 + from_near[blocks:].astype(jnp.float32)).astype(jnp.bfloat16)
+    from_far = lax.ppermute(onward, "x", far)
     grad_features = pl.pallas_call(
         feature_kernel,
         out_shape=jax.ShapeDtypeStruct((rows_dev, channels), jnp.float32),
-        in_specs=[VMEM] * 2,
+        in_specs=[VMEM] * 4,
         out_specs=VMEM,
         compiler_params=params,
         name="feature_grad",
-    )(grad_t, weight)
-    plane = ("y", "core", "x")
-    piece = jnp.sum(lax.all_to_all(term, plane, 0, 0), axis=0)
-    copies = jnp.broadcast_to(piece[None], (z,) + piece.shape)
-    piece = jnp.sum(lax.all_to_all(copies, "z", 0, 0), axis=0)
-    piece = piece / math.sqrt(rows * x * rows_dev)
-    copies = jnp.broadcast_to(piece[None], (peers,) + piece.shape)
-    pieces = lax.all_to_all(copies, plane, 0, 0).reshape(-1, across, height, 128)
+    )(keep0, from_near, from_far, weight)
+    got = lax.all_to_all(term, ("x", "y"), 0, 0)
+    copies = spread(got, 2 * z, math.sqrt(rows * x * rows_dev))
+    got = lax.all_to_all(copies, ("z", "core"), 0, 0)
+    copies = spread(got, x * y, 1.0)
+    pieces = lax.all_to_all(copies, ("x", "y"), 0, 0).astype(jnp.float32)
+    pieces = pieces.reshape(x * y, halves, height, edge)
     grad_weight = pieces.transpose(0, 2, 1, 3).reshape(channels, channels)
     return (grad_features, grad_weight)
 

time: 105 us -> 99.2 us (0.945)
  blocking collectives: 63.1 us -> 18.7 us
  starting transfers between devices: 20.7 us -> 41.7 us
  waiting for transfers between devices: 13.2 us -> 29.5 us
  Pallas kernels: 4.36 us -> 6.67 us
  local copies, waits for them, and re-layouts: 1.44 us -> 0.01 us
    all_to_all x3 -> x1, blocking collectives: 63.1 us -> 18.7 us  [local(): got = lax.all_to_all(copies, ('z', 'core'), 0, 0)]
    ppermute x0 -> x4, waiting for transfers between devices: none -> 22.9 us  [the longest x1 11 us: local(): feat32 = lax.ppermute(jnp.concatenate([features, feat1], axis=0), 'x', far)]
    ppermute x0 -> x4, starting transfers between devices: none -> 11.4 us  [the longest x1 4.39 us: local(): from_far = lax.ppermute(onward, 'x', far)]
    all_to_all x1 -> x2, starting transfers between devices: 7.53 us -> 17.2 us  [the longest x1 13.1 us: local(): got = lax.all_to_all(term, ('x', 'y'), 0, 0)]
    all_to_all x1 -> x2, waiting for transfers between devices: 11.3 us -> 6.52 us  [the longest x1 6.51 us: local(): got = lax.all_to_all(term, ('x', 'y'), 0, 0)]
    ppermute x2, waiting for transfers between devices: 1.91 us -> 0.01 us  [swap(): return lax.ppermute(array, axes, pairs + [(j, i) for i, j in pairs])]
    pallas_call x1 -> x3, Pallas kernels: 0.43 us -> 2.14 us  [the longest x1 1.41 us: local(): pl.pallas_call(weight_kernel, out_shape=(jax.ShapeDtypeStruct((2 * blocks...]
  transfers between devices with their start and end apart: 3 -> 8, of which waited for: 2 -> 4; matrix products, arithmetic and copies ran while one was open for 0% -> 0% of each run, Pallas kernels for 1% -> 2%
where the time goes in v4:
time: 99.2 us; the launch traced here: 98.7 us
  starting transfers between devices  41.7 us (42%)
  waiting for transfers between devices  29.5 us (30%)
  blocking collectives  18.7 us (19%)
  Pallas kernels  6.67 us (7%)
  between operations  1.43 us (1%)
    all_to_all x1, blocking collectives, local(): got = lax.all_to_all(copies, ('z', 'core'), 0, 0)  18.7 us
    ppermute x2, starting transfers between devices, swap(): return lax.ppermute(array, axes, pairs + [(j, i) for i, j in pairs])  13.1 us
    all_to_all x1, starting transfers between devices, local(): got = lax.all_to_all(term, ('x', 'y'), 0, 0)  13.1 us
    ppermute x1, waiting for transfers between devices, local(): feat32 = lax.ppermute(jnp.concatenate([features, feat1], axis=0), 'x', far)  11 us
    all_to_all x1, waiting for transfers between devices, local(): got = lax.all_to_all(term, ('x', 'y'), 0, 0)  6.51 us
    ppermute x1, waiting for transfers between devices, local(): feat1 = lax.ppermute(features, 'x', near)  6.49 us
    ppermute x1, waiting for transfers between devices, local(): from_far = lax.ppermute(onward, 'x', far)  5.42 us
    ppermute x1, starting transfers between devices, local(): from_far = lax.ppermute(onward, 'x', far)  4.39 us
  transfers between devices with their start and end apart: 8, of which 4 were waited for; matrix products, arithmetic and copies ran while one was open for 0% of the time, Pallas kernels for 2%

profile of v4, /device:TPU:1, one launch (start us, length us, event | category | flops | bytes accessed | tf_op | source)
XLA Modules:
  0.0 98.7 jit_solution(17177303513866454642)
XLA Ops:
  0.6 0.0 copy-start
  1.3 3.4 %tile_sums.1 = (bf16[12,256,128]{2,1,0:T(8,128)(2,1)S(1)}, bf16[12,256,128]{2,1,0:T(8,128)(2,1)S(1)}, f32[12,256,128]{2,1,0:T(8,128)S(1)}) custom-call(s32[1]{0:T(128)S(6)} %copy.9.count, s32[3,72]{1,0:T(4,128)} %bitcast.8, bf16[384,256]{1,0:T(8,128)(2,1)} %pre_hbm.1, f32[384,256]{1,0:T(8,128)} %up_hbm.1, bf16[72,128,128]{2,1,0:T(8,128)(2,1)} %tiles_hbm.1), custom_call_target="tpu_custom_call" | custom-call | tf_op jit(solution)/shard_map/tile_sums/pallas_call | solution.py:146
  4.7 4.8 %collective-permute-start = (bf16[12,256,128]{2,1,0:T(8,128)(2,1)S(1)}, bf16[12,256,128]{2,1,0:T(8,128)(2,1)S(1)}, u32[]{:S(2)}, u32[]{:S(2)}) collective-permute-start(bf16[12,256,128]{2,1,0:T(8,128)(2,1)S(1)} %get-tuple-element.10), channel_id=1, source_target_pairs={{4,8},{12,16},{20,24},{28,32},{36,40},{44,48},{52,56},{60,64},{68,... | collective-permute-start | bytes 2359304 | tf_op jit(solution)/shard_map/ppermute | solution.py:131
  9.5 8.3 %collective-permute-start.1 = (bf16[12,256,128]{2,1,0:T(8,128)(2,1)S(1)}, bf16[12,256,128]{2,1,0:T(8,128)(2,1)S(1)}, u32[]{:S(2)}, u32[]{:S(2)}) collective-permute-start(bf16[12,256,128]{2,1,0:T(8,128)(2,1)S(1)} %get-tuple-element.11), channel_id=1, source_target_pairs={{0,4},{4,0},{1,5},{5,1},{2,6},{6,2},{3,7},{7,3},{8,12},{12,8},{9,1... | collective-permute-start | bytes 2359304 | tf_op jit(solution)/shard_map/ppermute | solution.py:131
  17.9 0.0 copy-done
  17.9 1.9 %collective-permute-start.2 = (bf16[384,256]{1,0:T(8,128)(2,1)S(1)}, bf16[384,256]{1,0:T(8,128)(2,1)S(1)}, u32[]{:S(2)}, u32[]{:S(2)}) collective-permute-start(bf16[384,256]{1,0:T(8,128)(2,1)S(1)} %copy-done), channel_id=1, source_target_pairs={{0,1},{1,0},{2,3},{3,2},{4,5},{5,4},{6,7},{7,6},{8,9},{9,8},{10,11... | collective-permute-start | bytes 589832 | tf_op jit(solution)/shard_map/ppermute | solution.py:171
  19.8 6.5 %collective-permute-done.2.feat1 = bf16[384,256]{1,0:T(8,128)(2,1)S(1)} collective-permute-done((bf16[384,256]{1,0:T(8,128)(2,1)S(1)}, bf16[384,256]{1,0:T(8,128)(2,1)S(1)}, u32[]{:S(2)}, u32[]{:S(2)}) %collective-permute-start.2) | collective-permute-done | bytes 196640 | tf_op jit(solution)/shard_map/ppermute | solution.py:171
  26.3 1.9 %collective-permute-start.3 = (bf16[768,256]{1,0:T(8,128)(2,1)S(1)}, bf16[768,256]{1,0:T(8,128)(2,1)S(1)}, u32[]{:S(2)}, u32[]{:S(2)}) collective-permute-start(bf16[768,256]{1,0:T(8,128)(2,1)S(1)} %pad_maximum_fusion), channel_id=1, source_target_pairs={{0,3},{1,2},{2,1},{3,0},{4,7},{5,6},{6,5},{7,4},{8,11},{9,10},{10,... | collective-permute-start | bytes 1179656 | tf_op jit(solution)/shard_map/ppermute | solution.py:172
  28.3 11.0 %collective-permute-done.3.feat32 = bf16[768,256]{1,0:T(8,128)(2,1)S(1)} collective-permute-done((bf16[768,256]{1,0:T(8,128)(2,1)S(1)}, bf16[768,256]{1,0:T(8,128)(2,1)S(1)}, u32[]{:S(2)}, u32[]{:S(2)}) %collective-permute-start.3) | collective-permute-done | bytes 393248 | tf_op jit(solution)/shard_map/ppermute | solution.py:172
  39.3 0.0 collective-permute-done.cross
  39.3 0.0 collective-permute-done.1.chip
  39.3 0.0 copy-start.1
  39.3 1.4 %weight_term.1 = (bf16[6,256,128]{2,1,0:T(8,128)(2,1)S(1)}, f32[3,256,128]{2,1,0:T(8,128)S(1)}, f32[3,256,128]{2,1,0:T(8,128)S(1)}, f32[32,16,128]{2,1,0:T(8,128)}) custom-call(f32[12,256,128]{2,1,0:T(8,128)S(1)} %get-tuple-element.9.own, bf16[12,256,128]{2,1,0:T(8,128)(2,1)S(1)} %collective-permute-done.cross, ...), custom_call_target="tpu_custom_call" | custom-call | tf_op jit(solution)/shard_map/weight_term/pallas_call | solution.py:176
  40.7 13.1 %all-to-all-start = ((f32[32,16,128]{2,1,0:T(8,128)}), f32[32,16,128]{2,1,0:T(8,128)S(1)}, u32[]{:S(2)}, u32[]{:S(2)}) async-start(f32[32,16,128]{2,1,0:T(8,128)} %get-tuple-element.15), calls=%async_computation | async-start | bytes 524288 | tf_op jit(solution)/shard_map/all_to_all | solution.py:200
  53.8 3.1 %collective-permute-start.4 = (bf16[6,256,128]{2,1,0:T(8,128)(2,1)S(1)}, bf16[6,256,128]{2,1,0:T(8,128)(2,1)S(1)}, u32[]{:S(2)}, u32[]{:S(2)}) collective-permute-start(bf16[6,256,128]{2,1,0:T(8,128)(2,1)S(1)} %get-tuple-element.13), channel_id=1, source_target_pairs={{0,1},{1,0},{2,3},{3,2},{4,5},{5,4},{6,7},{7,6},{8,9},{9,8},{10,11... | collective-permute-start | bytes 1179656 | tf_op jit(solution)/shard_map/ppermute | solution.py:189
  57.0 6.5 %all-to-all-done.got = f32[32,16,128]{2,1,0:T(8,128)S(1)} async-done(((f32[32,16,128]{2,1,0:T(8,128)}), f32[32,16,128]{2,1,0:T(8,128)S(1)}, u32[]{:S(2)}, u32[]{:S(2)}) %all-to-all-start) | async-done | bytes 262176 | tf_op jit(solution)/shard_map/all_to_all | solution.py:200
  63.5 18.7 %all_to_all.15.got = bf16[24,16,128]{2,1,0:T(8,128)(2,1)S(1)} all-to-all(bf16[24,16,128]{2,1,0:T(8,128)(2,1)S(1)} %spread.2), channel_id=1, replica_groups=mesh['y'=8,'z'=12,'core'=2,'x'=4] {'z','core'}, dimensions={0} | all-to-all | bytes 196608 | tf_op jit(solution)/shard_map/all_to_all | solution.py:202
  82.2 0.7 spread.3
  82.9 4.0 %all-to-all-start.2 = ((bf16[32,16,128]{2,1,0:T(8,128)(2,1)}), bf16[32,16,128]{2,1,0:T(8,128)(2,1)S(1)}, u32[]{:S(2)}, u32[]{:S(2)}) async-start(bf16[32,16,128]{2,1,0:T(8,128)(2,1)} %spread.3), calls=%async_computation.2 | async-start | bytes 262144 | tf_op jit(solution)/shard_map/all_to_all | solution.py:204
  86.9 0.0 collective-permute-done.4.pair
  87.0 4.4 %collective-permute-start.5 = (bf16[3,256,128]{2,1,0:T(8,128)(2,1)S(1)}, bf16[3,256,128]{2,1,0:T(8,128)(2,1)S(1)}, u32[]{:S(2)}, u32[]{:S(2)}) collective-permute-start(bf16[3,256,128]{2,1,0:T(8,128)(2,1)S(1)} %add_convert_fusion), channel_id=1, source_target_pairs={{0,3},{1,2},{2,1},{3,0},{4,7},{5,6},{6,5},{7,4},{8,11},{9,10},{10,... | collective-permute-start | bytes 589832 | tf_op jit(solution)/shard_map/ppermute | solution.py:191
  91.4 5.4 %collective-permute-done.5.other = bf16[3,256,128]{2,1,0:T(8,128)(2,1)S(1)} collective-permute-done((bf16[3,256,128]{2,1,0:T(8,128)(2,1)S(1)}, bf16[3,256,128]{2,1,0:T(8,128)(2,1)S(1)}, u32[]{:S(2)}, u32[]{:S(2)}) %collective-permute-start.5) | collective-permute-done | bytes 196640 | tf_op jit(solution)/shard_map/ppermute | solution.py:191
  96.8 0.0 copy-done.1
  96.8 1.2 %feature_grad.1 = f32[384,256]{1,0:T(8,128)} custom-call(f32[3,256,128]{2,1,0:T(8,128)S(1)} %get-tuple-element.12.keep, bf16[6,256,128]{2,1,0:T(8,128)(2,1)S(1)} %collective-permute-done.4.pair, bf16[3,256,128]{2,1,0:T(8,128)(2,1)S(1)} %collective-permute-done.5.other, bf16[256,256]{1,0:T(8,128)(2,1)S(1)} %copy-done.1), custom_call_target="tpu_custom_call" | custom-call | tf_op jit(solution)/shard_map/feature_grad/pallas_call | solution.py:192
  98.0 0.0 all-to-all-done.2
  98.0 0.7 convert_bitcast_fusion
  (3 shorter events, 0.1 us)
Async XLA Ops:
  0.6 17.2 %copy-start = (bf16[384,256]{1,0:T(8,128)(2,1)S(1)}, bf16[384,256]{1,0:T(8,128)(2,1)}, u32[]{:S(2)}) copy-start(bf16[384,256]{1,0:T(8,128)(2,1)} %feat0.1) | copy-start | bytes 589828
  4.7 34.6 %collective-permute-start = (bf16[12,256,128]{2,1,0:T(8,128)(2,1)S(1)}, bf16[12,256,128]{2,1,0:T(8,128)(2,1)S(1)}, u32[]{:S(2)}, u32[]{:S(2)}) collective-permute-start(bf16[12,256,128]{2,1,0:T(8,128)(2,1)S(1)} %get-tuple-element.10), channel_id=1, source_target_pairs={{4,8},{12,16},{20,24},{28,32},{36,40},{44,48},{52,56},{60,64},{68,... | collective-permute-start | bytes 2359304 | tf_op jit(solution)/shard_map/ppermute | solution.py:131
  9.5 29.8 %collective-permute-start.1 = (bf16[12,256,128]{2,1,0:T(8,128)(2,1)S(1)}, bf16[12,256,128]{2,1,0:T(8,128)(2,1)S(1)}, u32[]{:S(2)}, u32[]{:S(2)}) collective-permute-start(bf16[12,256,128]{2,1,0:T(8,128)(2,1)S(1)} %get-tuple-element.11), channel_id=1, source_target_pairs={{0,4},{4,0},{1,5},{5,1},{2,6},{6,2},{3,7},{7,3},{8,12},{12,8},{9,1... | collective-permute-start | bytes 2359304 | tf_op jit(solution)/shard_map/ppermute | solution.py:131
  17.9 8.4 %collective-permute-start.2 = (bf16[384,256]{1,0:T(8,128)(2,1)S(1)}, bf16[384,256]{1,0:T(8,128)(2,1)S(1)}, u32[]{:S(2)}, u32[]{:S(2)}) collective-permute-start(bf16[384,256]{1,0:T(8,128)(2,1)S(1)} %copy-done), channel_id=1, source_target_pairs={{0,1},{1,0},{2,3},{3,2},{4,5},{5,4},{6,7},{7,6},{8,9},{9,8},{10,11... | collective-permute-start | bytes 589832 | tf_op jit(solution)/shard_map/ppermute | solution.py:171
  26.3 12.9 %collective-permute-start.3 = (bf16[768,256]{1,0:T(8,128)(2,1)S(1)}, bf16[768,256]{1,0:T(8,128)(2,1)S(1)}, u32[]{:S(2)}, u32[]{:S(2)}) collective-permute-start(bf16[768,256]{1,0:T(8,128)(2,1)S(1)} %pad_maximum_fusion), channel_id=1, source_target_pairs={{0,3},{1,2},{2,1},{3,0},{4,7},{5,6},{6,5},{7,4},{8,11},{9,10},{10,... | collective-permute-start | bytes 1179656 | tf_op jit(solution)/shard_map/ppermute | solution.py:172
  39.3 57.5 %copy-start.1 = (bf16[256,256]{1,0:T(8,128)(2,1)S(1)}, bf16[256,256]{1,0:T(8,128)(2,1)}, u32[]{:S(2)}) copy-start(bf16[256,256]{1,0:T(8,128)(2,1)} %weight.1) | copy-start | bytes 393220
  40.7 22.8 %all-to-all-start = ((f32[32,16,128]{2,1,0:T(8,128)}), f32[32,16,128]{2,1,0:T(8,128)S(1)}, u32[]{:S(2)}, u32[]{:S(2)}) async-start(f32[32,16,128]{2,1,0:T(8,128)} %get-tuple-element.15), calls=%async_computation | async-start | bytes 524288 | tf_op jit(solution)/shard_map/all_to_all | solution.py:200
  53.8 33.1 %collective-permute-start.4 = (bf16[6,256,128]{2,1,0:T(8,128)(2,1)S(1)}, bf16[6,256,128]{2,1,0:T(8,128)(2,1)S(1)}, u32[]{:S(2)}, u32[]{:S(2)}) collective-permute-start(bf16[6,256,128]{2,1,0:T(8,128)(2,1)S(1)} %get-tuple-element.13), channel_id=1, source_target_pairs={{0,1},{1,0},{2,3},{3,2},{4,5},{5,4},{6,7},{7,6},{8,9},{9,8},{10,11... | collective-permute-start | bytes 1179656 | tf_op jit(solution)/shard_map/ppermute | solution.py:189
  82.9 15.1 %all-to-all-start.2 = ((bf16[32,16,128]{2,1,0:T(8,128)(2,1)}), bf16[32,16,128]{2,1,0:T(8,128)(2,1)S(1)}, u32[]{:S(2)}, u32[]{:S(2)}) async-start(bf16[32,16,128]{2,1,0:T(8,128)(2,1)} %spread.3), calls=%async_computation.2 | async-start | bytes 262144 | tf_op jit(solution)/shard_map/all_to_all | solution.py:204
  87.0 9.8 %collective-permute-start.5 = (bf16[3,256,128]{2,1,0:T(8,128)(2,1)S(1)}, bf16[3,256,128]{2,1,0:T(8,128)(2,1)S(1)}, u32[]{:S(2)}, u32[]{:S(2)}) collective-permute-start(bf16[3,256,128]{2,1,0:T(8,128)(2,1)S(1)} %add_convert_fusion), channel_id=1, source_target_pairs={{0,3},{1,2},{2,1},{3,0},{4,7},{5,6},{6,5},{7,4},{8,11},{9,10},{10,... | collective-permute-start | bytes 589832 | tf_op jit(solution)/shard_map/ppermute | solution.py:191

commit v5 on v4

--- a/solution.py
+++ b/solution.py
@@ -164,11 +164,12 @@
         compiler_params=params,
         name="tile_sums",
     )(tile_counts, *held)
+    near = [(i, i ^ 1) for i in range(x)]
+    feat1 = lax.ppermute(features, "x", near)
+    chip, feat1 = lax.optimization_barrier((chip, feat1))
     from_cross = swap(cross, ("y", "z", "core"), rows, 1)
     from_chip = swap(chip, "core", 2, 0)
-    near = [(i, i ^ 1) for i in range(x)]
     far = [(i, i ^ 3) for i in range(x)]
-    feat1 = lax.ppermute(features, "x", near)
     feat32 = lax.ppermute(jnp.concatenate([features, feat1], axis=0), "x", far)
     halves = channels // edge
     height = channels // (x * y)
@@ -200,6 +201,7 @@
     got = lax.all_to_all(term, ("x", "y"), 0, 0)
     copies = spread(got, 2 * z, math.sqrt(rows * x * rows_dev))
     got = lax.all_to_all(copies, ("z", "core"), 0, 0)
+    got, from_far = lax.optimization_barrier((got, from_far))
     copies = spread(got, x * y, 1.0)
     pieces = lax.all_to_all(copies, ("x", "y"), 0, 0).astype(jnp.float32)
     pieces = pieces.reshape(x * y, halves, height, edge)

time: 99.2 us -> 93.6 us (0.944)
  blocking collectives: 18.7 us -> 0 us
  starting transfers between devices: 41.7 us -> 48.1 us
  waiting for transfers between devices: 29.5 us -> 34.6 us
  Pallas kernels: 6.67 us -> 7.91 us
    all_to_all x1 -> x0, blocking collectives: 18.7 us -> none  [local(): got = lax.all_to_all(copies, ('z', 'core'), 0, 0)]
    all_to_all x1, waiting for transfers between devices: 0.01 us -> 7.99 us  [local(): pieces = lax.all_to_all(copies, ('x', 'y'), 0, 0).astype(jnp.float32)]
    all_to_all x0 -> x1, starting transfers between devices: none -> 7.19 us  [local(): got = lax.all_to_all(copies, ('z', 'core'), 0, 0)]
    ppermute x1, waiting for transfers between devices: 6.49 us -> 0.01 us  [local(): feat1 = lax.ppermute(features, 'x', near)]
    ppermute x1, starting transfers between devices: 1.92 us -> 4.08 us  [local(): feat1 = lax.ppermute(features, 'x', near)]
    all_to_all x0 -> x1, waiting for transfers between devices: none -> 1.74 us  [local(): got = lax.all_to_all(copies, ('z', 'core'), 0, 0)]
    ppermute x2, starting transfers between devices: 13.1 us -> 11.6 us  [swap(): return lax.ppermute(array, axes, pairs + [(j, i) for i, j in pairs])]
    ppermute x1, starting transfers between devices: 4.39 us -> 2.89 us  [local(): from_far = lax.ppermute(onward, 'x', far)]
  transfers between devices with their start and end apart: 8 -> 9, of which waited for: 4 -> 5; matrix products, arithmetic and copies ran while one was open for 0% -> 0% of each run, Pallas kernels for 2% -> 6%
where the time goes in v5:
time: 93.6 us; the launch traced here: 92.8 us
  starting transfers between devices  48.1 us (51%)
  waiting for transfers between devices  34.6 us (37%)
  Pallas kernels  7.91 us (8%)
  between operations  1.42 us (2%)
    all_to_all x1, starting transfers between devices, local(): got = lax.all_to_all(term, ('x', 'y'), 0, 0)  13.1 us
    ppermute x1, waiting for transfers between devices, local(): feat32 = lax.ppermute(jnp.concatenate([features, feat1], axis=0), 'x', far)  11.9 us
    ppermute x2, starting transfers between devices, swap(): return lax.ppermute(array, axes, pairs + [(j, i) for i, j in pairs])  11.6 us
    all_to_all x1, waiting for transfers between devices, local(): pieces = lax.all_to_all(copies, ('x', 'y'), 0, 0).astype(jnp.float32)  7.99 us
    all_to_all x1, starting transfers between devices, local(): got = lax.all_to_all(copies, ('z', 'core'), 0, 0)  7.19 us
    all_to_all x1, waiting for transfers between devices, local(): got = lax.all_to_all(term, ('x', 'y'), 0, 0)  6.53 us
    ppermute x1, waiting for transfers between devices, local(): from_far = lax.ppermute(onward, 'x', far)  6.41 us
    all_to_all x1, starting transfers between devices, local(): pieces = lax.all_to_all(copies, ('x', 'y'), 0, 0).astype(jnp.float32)  4.22 us
  transfers between devices with their start and end apart: 9, of which 5 were waited for; matrix products, arithmetic and copies ran while one was open for 0% of the time, Pallas kernels for 6%

profile of v5, /device:TPU:1, one launch (start us, length us, event | category | flops | bytes accessed | tf_op | source)
XLA Modules:
  0.0 92.8 jit_solution(3940254627419409637)
XLA Ops:
  0.6 0.0 copy-start
  0.6 4.1 %collective-permute-start.1 = (bf16[384,256]{1,0:T(8,128)(2,1)}, bf16[384,256]{1,0:T(8,128)(2,1)S(1)}, u32[]{:S(2)}, u32[]{:S(2)}) collective-permute-start(bf16[384,256]{1,0:T(8,128)(2,1)} %feat0.1), channel_id=1, source_target_pairs={{0,1},{1,0},{2,3},{3,2},{4,5},{5,4},{6,7},{7,6},{8,9},{9,8},{10,11... | collective-permute-start | bytes 589832 | tf_op jit(solution)/shard_map/ppermute | solution.py:168
  5.4 4.0 %tile_sums.1 = (bf16[12,256,128]{2,1,0:T(8,128)(2,1)S(1)}, bf16[12,256,128]{2,1,0:T(8,128)(2,1)S(1)}, f32[12,256,128]{2,1,0:T(8,128)S(1)}) custom-call(s32[1]{0:T(128)S(6)} %copy.9.count, s32[3,72]{1,0:T(4,128)} %bitcast.8, bf16[384,256]{1,0:T(8,128)(2,1)} %pre_hbm.1, f32[384,256]{1,0:T(8,128)} %up_hbm.1, bf16[72,128,128]{2,1,0:T(8,128)(2,1)} %tiles_hbm.1), custom_call_target="tpu_custom_call" | custom-call | tf_op jit(solution)/shard_map/tile_sums/pallas_call | solution.py:146
  9.4 4.8 %collective-permute-start = (bf16[12,256,128]{2,1,0:T(8,128)(2,1)S(1)}, bf16[12,256,128]{2,1,0:T(8,128)(2,1)S(1)}, u32[]{:S(2)}, u32[]{:S(2)}) collective-permute-start(bf16[12,256,128]{2,1,0:T(8,128)(2,1)S(1)} %get-tuple-element.13), channel_id=1, source_target_pairs={{4,8},{12,16},{20,24},{28,32},{36,40},{44,48},{52,56},{60,64},{68,... | collective-permute-start | bytes 2359304 | tf_op jit(solution)/shard_map/ppermute | solution.py:131
  14.2 0.0 collective-permute-done.1.feat1
  14.2 6.8 %collective-permute-start.2 = (bf16[12,256,128]{2,1,0:T(8,128)(2,1)S(1)}, bf16[12,256,128]{2,1,0:T(8,128)(2,1)S(1)}, u32[]{:S(2)}, u32[]{:S(2)}) collective-permute-start(bf16[12,256,128]{2,1,0:T(8,128)(2,1)S(1)} %get-tuple-element.15), channel_id=1, source_target_pairs={{0,4},{4,0},{1,5},{5,1},{2,6},{6,2},{3,7},{7,3},{8,12},{12,8},{9,1... | collective-permute-start | bytes 2359304 | tf_op jit(solution)/shard_map/ppermute | solution.py:131
  21.0 0.0 copy-done
  21.0 1.9 %collective-permute-start.3 = (bf16[768,256]{1,0:T(8,128)(2,1)S(1)}, bf16[768,256]{1,0:T(8,128)(2,1)S(1)}, u32[]{:S(2)}, u32[]{:S(2)}) collective-permute-start(bf16[768,256]{1,0:T(8,128)(2,1)S(1)} %pad_maximum_fusion), channel_id=1, source_target_pairs={{0,3},{1,2},{2,1},{3,0},{4,7},{5,6},{6,5},{7,4},{8,11},{9,10},{10,... | collective-permute-start | bytes 1179656 | tf_op jit(solution)/shard_map/ppermute | solution.py:173
  22.9 11.9 %collective-permute-done.3.feat32 = bf16[768,256]{1,0:T(8,128)(2,1)S(1)} collective-permute-done((bf16[768,256]{1,0:T(8,128)(2,1)S(1)}, bf16[768,256]{1,0:T(8,128)(2,1)S(1)}, u32[]{:S(2)}, u32[]{:S(2)}) %collective-permute-start.3) | collective-permute-done | bytes 393248 | tf_op jit(solution)/shard_map/ppermute | solution.py:173
  34.9 0.0 collective-permute-done.cross
  34.9 0.0 collective-permute-done.2.chip
  34.9 0.0 copy-start.1
  34.9 1.4 %weight_term.1 = (bf16[6,256,128]{2,1,0:T(8,128)(2,1)S(1)}, f32[3,256,128]{2,1,0:T(8,128)S(1)}, f32[3,256,128]{2,1,0:T(8,128)S(1)}, f32[32,16,128]{2,1,0:T(8,128)}) custom-call(f32[12,256,128]{2,1,0:T(8,128)S(1)} %get-tuple-element.12.own, bf16[12,256,128]{2,1,0:T(8,128)(2,1)S(1)} %collective-permute-done.cross, ...), custom_call_target="tpu_custom_call" | custom-call | tf_op jit(solution)/shard_map/weight_term/pallas_call | solution.py:177
  36.3 13.1 %all-to-all-start = ((f32[32,16,128]{2,1,0:T(8,128)}), f32[32,16,128]{2,1,0:T(8,128)S(1)}, u32[]{:S(2)}, u32[]{:S(2)}) async-start(f32[32,16,128]{2,1,0:T(8,128)} %get-tuple-element.20), calls=%async_computation | async-start | bytes 524288 | tf_op jit(solution)/shard_map/all_to_all | solution.py:201
  49.4 3.1 %collective-permute-start.4 = (bf16[6,256,128]{2,1,0:T(8,128)(2,1)S(1)}, bf16[6,256,128]{2,1,0:T(8,128)(2,1)S(1)}, u32[]{:S(2)}, u32[]{:S(2)}) collective-permute-start(bf16[6,256,128]{2,1,0:T(8,128)(2,1)S(1)} %get-tuple-element.18), channel_id=1, source_target_pairs={{0,1},{1,0},{2,3},{3,2},{4,5},{5,4},{6,7},{7,6},{8,9},{9,8},{10,11... | collective-permute-start | bytes 1179656 | tf_op jit(solution)/shard_map/ppermute | solution.py:190
  52.5 6.5 %all-to-all-done.got = f32[32,16,128]{2,1,0:T(8,128)S(1)} async-done(((f32[32,16,128]{2,1,0:T(8,128)}), f32[32,16,128]{2,1,0:T(8,128)S(1)}, u32[]{:S(2)}, u32[]{:S(2)}) %all-to-all-start) | async-done | bytes 262176 | tf_op jit(solution)/shard_map/all_to_all | solution.py:201
  59.0 0.7 spread.2
  59.7 7.2 %all-to-all-start.1 = ((bf16[24,16,128]{2,1,0:T(8,128)(2,1)}), bf16[24,16,128]{2,1,0:T(8,128)(2,1)S(1)}, u32[]{:S(2)}, u32[]{:S(2)}) async-start(bf16[24,16,128]{2,1,0:T(8,128)(2,1)} %spread.2), calls=%async_computation.1 | async-start | bytes 196608 | tf_op jit(solution)/shard_map/all_to_all | solution.py:203
  66.9 0.0 collective-permute-done.4.pair
  67.0 2.9 %collective-permute-start.5 = (bf16[3,256,128]{2,1,0:T(8,128)(2,1)S(1)}, bf16[3,256,128]{2,1,0:T(8,128)(2,1)S(1)}, u32[]{:S(2)}, u32[]{:S(2)}) collective-permute-start(bf16[3,256,128]{2,1,0:T(8,128)(2,1)S(1)} %add_convert_fusion), channel_id=1, source_target_pairs={{0,3},{1,2},{2,1},{3,0},{4,7},{5,6},{6,5},{7,4},{8,11},{9,10},{10,... | collective-permute-start | bytes 589832 | tf_op jit(solution)/shard_map/ppermute | solution.py:192
  69.9 6.4 %collective-permute-done.5.other = bf16[3,256,128]{2,1,0:T(8,128)(2,1)S(1)} collective-permute-done((bf16[3,256,128]{2,1,0:T(8,128)(2,1)S(1)}, bf16[3,256,128]{2,1,0:T(8,128)(2,1)S(1)}, u32[]{:S(2)}, u32[]{:S(2)}) %collective-permute-start.5) | collective-permute-done | bytes 196640 | tf_op jit(solution)/shard_map/ppermute | solution.py:192
  76.3 1.7 %all-to-all-done.1.got = bf16[24,16,128]{2,1,0:T(8,128)(2,1)S(1)} async-done(((bf16[24,16,128]{2,1,0:T(8,128)(2,1)}), bf16[24,16,128]{2,1,0:T(8,128)(2,1)S(1)}, u32[]{:S(2)}, u32[]{:S(2)}) %all-to-all-start.1) | async-done | bytes 98336 | tf_op jit(solution)/shard_map/all_to_all | solution.py:203
  78.0 0.7 spread.3
  78.7 4.2 %all-to-all-start.2 = ((bf16[32,16,128]{2,1,0:T(8,128)(2,1)}), bf16[32,16,128]{2,1,0:T(8,128)(2,1)S(1)}, u32[]{:S(2)}, u32[]{:S(2)}) async-start(bf16[32,16,128]{2,1,0:T(8,128)(2,1)} %spread.3), calls=%async_computation.2 | async-start | bytes 262144 | tf_op jit(solution)/shard_map/all_to_all | solution.py:206
  82.9 0.0 copy-done.1
  83.0 1.2 %feature_grad.1 = f32[384,256]{1,0:T(8,128)} custom-call(f32[3,256,128]{2,1,0:T(8,128)S(1)} %get-tuple-element.17.keep, bf16[6,256,128]{2,1,0:T(8,128)(2,1)S(1)} %collective-permute-done.4.pair, bf16[3,256,128]{2,1,0:T(8,128)(2,1)S(1)} %collective-permute-done.5.other, bf16[256,256]{1,0:T(8,128)(2,1)S(1)} %copy-done.1), custom_call_target="tpu_custom_call" | custom-call | tf_op jit(solution)/shard_map/feature_grad/pallas_call | solution.py:193
  84.1 8.0 %all-to-all-done.2 = bf16[32,16,128]{2,1,0:T(8,128)(2,1)S(1)} async-done(((bf16[32,16,128]{2,1,0:T(8,128)(2,1)}), bf16[32,16,128]{2,1,0:T(8,128)(2,1)S(1)}, u32[]{:S(2)}, u32[]{:S(2)}) %all-to-all-start.2) | async-done | bytes 131104 | tf_op jit(solution)/shard_map/all_to_all | solution.py:206
  92.1 0.7 convert_bitcast_fusion
  (2 shorter events, 0.1 us)
Async XLA Ops:
  0.6 20.3 %copy-start = (bf16[384,256]{1,0:T(8,128)(2,1)S(1)}, bf16[384,256]{1,0:T(8,128)(2,1)}, u32[]{:S(2)}) copy-start(bf16[384,256]{1,0:T(8,128)(2,1)} %feat0.1) | copy-start | bytes 589828
  0.6 13.6 %collective-permute-start.1 = (bf16[384,256]{1,0:T(8,128)(2,1)}, bf16[384,256]{1,0:T(8,128)(2,1)S(1)}, u32[]{:S(2)}, u32[]{:S(2)}) collective-permute-start(bf16[384,256]{1,0:T(8,128)(2,1)} %feat0.1), channel_id=1, source_target_pairs={{0,1},{1,0},{2,3},{3,2},{4,5},{5,4},{6,7},{7,6},{8,9},{9,8},{10,11... | collective-permute-start | bytes 589832 | tf_op jit(solution)/shard_map/ppermute | solution.py:168
  9.4 25.5 %collective-permute-start = (bf16[12,256,128]{2,1,0:T(8,128)(2,1)S(1)}, bf16[12,256,128]{2,1,0:T(8,128)(2,1)S(1)}, u32[]{:S(2)}, u32[]{:S(2)}) collective-permute-start(bf16[12,256,128]{2,1,0:T(8,128)(2,1)S(1)} %get-tuple-element.13), channel_id=1, source_target_pairs={{4,8},{12,16},{20,24},{28,32},{36,40},{44,48},{52,56},{60,64},{68,... | collective-permute-start | bytes 2359304 | tf_op jit(solution)/shard_map/ppermute | solution.py:131
  14.2 20.6 %collective-permute-start.2 = (bf16[12,256,128]{2,1,0:T(8,128)(2,1)S(1)}, bf16[12,256,128]{2,1,0:T(8,128)(2,1)S(1)}, u32[]{:S(2)}, u32[]{:S(2)}) collective-permute-start(bf16[12,256,128]{2,1,0:T(8,128)(2,1)S(1)} %get-tuple-element.15), channel_id=1, source_target_pairs={{0,4},{4,0},{1,5},{5,1},{2,6},{6,2},{3,7},{7,3},{8,12},{12,8},{9,1... | collective-permute-start | bytes 2359304 | tf_op jit(solution)/shard_map/ppermute | solution.py:131
  21.0 13.8 %collective-permute-start.3 = (bf16[768,256]{1,0:T(8,128)(2,1)S(1)}, bf16[768,256]{1,0:T(8,128)(2,1)S(1)}, u32[]{:S(2)}, u32[]{:S(2)}) collective-permute-start(bf16[768,256]{1,0:T(8,128)(2,1)S(1)} %pad_maximum_fusion), channel_id=1, source_target_pairs={{0,3},{1,2},{2,1},{3,0},{4,7},{5,6},{6,5},{7,4},{8,11},{9,10},{10,... | collective-permute-start | bytes 1179656 | tf_op jit(solution)/shard_map/ppermute | solution.py:173
  34.9 48.1 %copy-start.1 = (bf16[256,256]{1,0:T(8,128)(2,1)S(1)}, bf16[256,256]{1,0:T(8,128)(2,1)}, u32[]{:S(2)}) copy-start(bf16[256,256]{1,0:T(8,128)(2,1)} %weight.1) | copy-start | bytes 393220
  36.3 22.8 %all-to-all-start = ((f32[32,16,128]{2,1,0:T(8,128)}), f32[32,16,128]{2,1,0:T(8,128)S(1)}, u32[]{:S(2)}, u32[]{:S(2)}) async-start(f32[32,16,128]{2,1,0:T(8,128)} %get-tuple-element.20), calls=%async_computation | async-start | bytes 524288 | tf_op jit(solution)/shard_map/all_to_all | solution.py:201
  49.4 17.6 %collective-permute-start.4 = (bf16[6,256,128]{2,1,0:T(8,128)(2,1)S(1)}, bf16[6,256,128]{2,1,0:T(8,128)(2,1)S(1)}, u32[]{:S(2)}, u32[]{:S(2)}) collective-permute-start(bf16[6,256,128]{2,1,0:T(8,128)(2,1)S(1)} %get-tuple-element.18), channel_id=1, source_target_pairs={{0,1},{1,0},{2,3},{3,2},{4,5},{5,4},{6,7},{7,6},{8,9},{9,8},{10,11... | collective-permute-start | bytes 1179656 | tf_op jit(solution)/shard_map/ppermute | solution.py:190
  59.7 18.3 %all-to-all-start.1 = ((bf16[24,16,128]{2,1,0:T(8,128)(2,1)}), bf16[24,16,128]{2,1,0:T(8,128)(2,1)S(1)}, u32[]{:S(2)}, u32[]{:S(2)}) async-start(bf16[24,16,128]{2,1,0:T(8,128)(2,1)} %spread.2), calls=%async_computation.1 | async-start | bytes 196608 | tf_op jit(solution)/shard_map/all_to_all | solution.py:203
  67.0 9.3 %collective-permute-start.5 = (bf16[3,256,128]{2,1,0:T(8,128)(2,1)S(1)}, bf16[3,256,128]{2,1,0:T(8,128)(2,1)S(1)}, u32[]{:S(2)}, u32[]{:S(2)}) collective-permute-start(bf16[3,256,128]{2,1,0:T(8,128)(2,1)S(1)} %add_convert_fusion), channel_id=1, source_target_pairs={{0,3},{1,2},{2,1},{3,0},{4,7},{5,6},{6,5},{7,4},{8,11},{9,10},{10,... | collective-permute-start | bytes 589832 | tf_op jit(solution)/shard_map/ppermute | solution.py:192
  78.7 13.4 %all-to-all-start.2 = ((bf16[32,16,128]{2,1,0:T(8,128)(2,1)}), bf16[32,16,128]{2,1,0:T(8,128)(2,1)S(1)}, u32[]{:S(2)}, u32[]{:S(2)}) async-start(bf16[32,16,128]{2,1,0:T(8,128)(2,1)} %spread.3), calls=%async_computation.2 | async-start | bytes 262144 | tf_op jit(solution)/shard_map/all_to_all | solution.py:206

commit v6 on v5

--- a/solution.py
+++ b/solution.py
@@ -50,12 +50,15 @@
 
     lax.fori_loop(0, (live + GROUP - 1) // GROUP, body, 0)
     core = row % 2
-    col = slots[0, 0] // blocks % (width // blocks)
-    for k in range(width // blocks):
-        to, at = pl.ds(k * blocks, blocks), (k ^ col) * blocks
-        cross[to] = total[pl.ds(2 * core * width + at, blocks)].astype(jnp.bfloat16)
-        chip[to] = total[pl.ds(2 * (1 - core) * width + at, blocks)].astype(jnp.bfloat16)
-        own[to] = total[pl.ds(width + at, blocks)]
+    cols = width // blocks
+    col = slots[0, 0] // blocks % cols
+    for k in range(cols):
+        to = pl.ds(k * blocks, blocks)
+        ahead, back = (k ^ col) * blocks, ((cols - k) % cols ^ col) * blocks
+        mine, other = jnp.where(core == 0, ahead, back), jnp.where(core == 0, back, ahead)
+        cross[to] = total[pl.ds(2 * core * width + other, blocks)].astype(jnp.bfloat16)
+        chip[to] = total[pl.ds(2 * (1 - core) * width + other, blocks)].astype(jnp.bfloat16)
+        own[to] = total[pl.ds(width + mine, blocks)]
 
 
 def split(value):
@@ -124,6 +127,10 @@
             )
             acc = prod if acc is None else acc + prod
         grad[pl.ds(b * edge, edge), :] = acc
+
+
+def hops(cols, flips):
+    return [(c * cols + i, c * cols + (i ^ flip)) for c, flip in enumerate(flips) for i in range(cols)]
 
 
 def swap(array, axes, count, first):
@@ -164,13 +171,12 @@
         compiler_params=params,
         name="tile_sums",
     )(tile_counts, *held)
-    near = [(i, i ^ 1) for i in range(x)]
-    feat1 = lax.ppermute(features, "x", near)
+    near, far = hops(x, (1, 3)), hops(x, (3, 1))
+    feat1 = lax.ppermute(features, ("core", "x"), near)
     chip, feat1 = lax.optimization_barrier((chip, feat1))
     from_cross = swap(cross, ("y", "z", "core"), rows, 1)
     from_chip = swap(chip, "core", 2, 0)
-    far = [(i, i ^ 3) for i in range(x)]
-    feat32 = lax.ppermute(jnp.concatenate([features, feat1], axis=0), "x", far)
+    feat32 = lax.ppermute(jnp.concatenate([features, feat1], axis=0), ("core", "x"), far)
     halves = channels // edge
     height = channels // (x * y)
     third = (blocks, channels, edge)
@@ -187,9 +193,9 @@
         compiler_params=params,
         name="weight_term",
     )(own, from_cross, from_chip, features, feat1, feat32)
-    from_near = lax.ppermute(give, "x", near)
+    from_near = lax.ppermute(give, ("core", "x"), near)
     onward = (keep3 + from_near[blocks:].astype(jnp.float32)).astype(jnp.bfloat16)
-    from_far = lax.ppermute(onward, "x", far)
+    from_far = lax.ppermute(onward, ("core", "x"), far)
     grad_features = pl.pallas_call(
         feature_kernel,
         out_shape=jax.ShapeDtypeStruct((rows_dev, channels), jnp.float32),

time: 93.6 us -> 90 us (0.962)
  waiting for transfers between devices: 34.6 us -> 29.3 us
  starting transfers between devices: 48.1 us -> 51.1 us
  Pallas kernels: 7.91 us -> 6.73 us
    ppermute x4, waiting for transfers between devices: 18.3 us -> 11.6 us  [the longest x1 6.83 us: local(): lax.ppermute(jnp.concatenate([features, feat1], axis=0), ('core', 'x'), far)]
    all_to_all x1, waiting for transfers between devices: 1.74 us -> 4.28 us  [local(): got = lax.all_to_all(copies, ('z', 'core'), 0, 0)]
    all_to_all x1, starting transfers between devices: 7.19 us -> 9.03 us  [local(): got = lax.all_to_all(copies, ('z', 'core'), 0, 0)]
    ppermute x4, starting transfers between devices: 12 us -> 13.7 us  [the longest x1 5.35 us: local(): feat1 = lax.ppermute(features, ('core', 'x'), near)]
    pallas_call x1, Pallas kernels: 3.97 us -> 2.79 us  [local(): pl.pallas_call(tile_kernel, out_shape=(jax.ShapeDtypeStruct((width, chann...]
    all_to_all x1, waiting for transfers between devices: 6.53 us -> 5.37 us  [local(): got = lax.all_to_all(term, ('x', 'y'), 0, 0)]
  transfers between devices with their start and end apart: 9 -> 9, of which waited for: 5 -> 5; matrix products, arithmetic and copies ran while one was open for 0% -> 0% of each run, Pallas kernels for 6% -> 5%
where the time goes in v6:
time: 90 us; the launch traced here: 89.3 us
  starting transfers between devices  51.1 us (57%)
  waiting for transfers between devices  29.3 us (33%)
  Pallas kernels  6.73 us (7%)
  between operations  1.42 us (2%)
    all_to_all x1, starting transfers between devices, local(): got = lax.all_to_all(term, ('x', 'y'), 0, 0)  13 us
    ppermute x2, starting transfers between devices, swap(): return lax.ppermute(array, axes, pairs + [(j, i) for i, j in pairs])  11.5 us
    all_to_all x1, starting transfers between devices, local(): got = lax.all_to_all(copies, ('z', 'core'), 0, 0)  9.03 us
    all_to_all x1, waiting for transfers between devices, local(): pieces = lax.all_to_all(copies, ('x', 'y'), 0, 0).astype(jnp.float32)  8 us
    ppermute x1, waiting for transfers between devices, local(): lax.ppermute(jnp.concatenate([features, feat1], axis=0), ('core', 'x'), far)  6.83 us
    all_to_all x1, waiting for transfers between devices, local(): got = lax.all_to_all(term, ('x', 'y'), 0, 0)  5.37 us
    ppermute x1, starting transfers between devices, local(): feat1 = lax.ppermute(features, ('core', 'x'), near)  5.35 us
    ppermute x1, waiting for transfers between devices, local(): from_far = lax.ppermute(onward, ('core', 'x'), far)  4.77 us
  transfers between devices with their start and end apart: 9, of which 5 were waited for; matrix products, arithmetic and copies ran while one was open for 0% of the time, Pallas kernels for 5%

profile of v6, /device:TPU:1, one launch (start us, length us, event | category | flops | bytes accessed | tf_op | source)
XLA Modules:
  0.0 89.3 jit_solution(10588435267886110269)
XLA Ops:
  0.6 0.0 copy-start
  0.6 5.3 %collective-permute-start.1 = (bf16[384,256]{1,0:T(8,128)(2,1)}, bf16[384,256]{1,0:T(8,128)(2,1)S(1)}, u32[]{:S(2)}, u32[]{:S(2)}) collective-permute-start(bf16[384,256]{1,0:T(8,128)(2,1)} %feat0.1), channel_id=1, source_target_pairs={{0,1},{1,0},{2,3},{3,2},{4,7},{5,6},{6,5},{7,4},{8,9},{9,8},{10,11... | collective-permute-start | bytes 589832 | tf_op jit(solution)/shard_map/ppermute | solution.py:175
  6.6 2.8 %tile_sums.1 = (bf16[12,256,128]{2,1,0:T(8,128)(2,1)S(1)}, bf16[12,256,128]{2,1,0:T(8,128)(2,1)S(1)}, f32[12,256,128]{2,1,0:T(8,128)S(1)}) custom-call(s32[1]{0:T(128)S(6)} %copy.9.count, s32[3,72]{1,0:T(4,128)} %bitcast.8, bf16[384,256]{1,0:T(8,128)(2,1)} %pre_hbm.1, f32[384,256]{1,0:T(8,128)} %up_hbm.1, bf16[72,128,128]{2,1,0:T(8,128)(2,1)} %tiles_hbm.1), custom_call_target="tpu_custom_call" | custom-call | tf_op jit(solution)/shard_map/tile_sums/pallas_call | solution.py:153
  9.4 3.6 %collective-permute-start = (bf16[12,256,128]{2,1,0:T(8,128)(2,1)S(1)}, bf16[12,256,128]{2,1,0:T(8,128)(2,1)S(1)}, u32[]{:S(2)}, u32[]{:S(2)}) collective-permute-start(bf16[12,256,128]{2,1,0:T(8,128)(2,1)S(1)} %get-tuple-element.13), channel_id=1, source_target_pairs={{4,8},{12,16},{20,24},{28,32},{36,40},{44,48},{52,56},{60,64},{68,... | collective-permute-start | bytes 2359304 | tf_op jit(solution)/shard_map/ppermute | solution.py:138
  13.0 0.0 collective-permute-done.1.feat1
  13.0 7.9 %collective-permute-start.2 = (bf16[12,256,128]{2,1,0:T(8,128)(2,1)S(1)}, bf16[12,256,128]{2,1,0:T(8,128)(2,1)S(1)}, u32[]{:S(2)}, u32[]{:S(2)}) collective-permute-start(bf16[12,256,128]{2,1,0:T(8,128)(2,1)S(1)} %get-tuple-element.15), channel_id=1, source_target_pairs={{0,4},{4,0},{1,5},{5,1},{2,6},{6,2},{3,7},{7,3},{8,12},{12,8},{9,1... | collective-permute-start | bytes 2359304 | tf_op jit(solution)/shard_map/ppermute | solution.py:138
  21.0 0.0 copy-done
  21.0 2.0 %collective-permute-start.3 = (bf16[768,256]{1,0:T(8,128)(2,1)S(1)}, bf16[768,256]{1,0:T(8,128)(2,1)S(1)}, u32[]{:S(2)}, u32[]{:S(2)}) collective-permute-start(bf16[768,256]{1,0:T(8,128)(2,1)S(1)} %pad_maximum_fusion), channel_id=1, source_target_pairs={{0,3},{1,2},{2,1},{3,0},{4,5},{5,4},{6,7},{7,6},{8,11},{9,10},{10,... | collective-permute-start | bytes 1179656 | tf_op jit(solution)/shard_map/ppermute | solution.py:179
  23.0 6.8 %collective-permute-done.3.feat32 = bf16[768,256]{1,0:T(8,128)(2,1)S(1)} collective-permute-done((bf16[768,256]{1,0:T(8,128)(2,1)S(1)}, bf16[768,256]{1,0:T(8,128)(2,1)S(1)}, u32[]{:S(2)}, u32[]{:S(2)}) %collective-permute-start.3) | collective-permute-done | bytes 393248 | tf_op jit(solution)/shard_map/ppermute | solution.py:179
  29.8 0.0 collective-permute-done.cross
  29.8 0.0 collective-permute-done.2.chip
  29.8 0.0 copy-start.1
  29.8 1.4 %weight_term.1 = (bf16[6,256,128]{2,1,0:T(8,128)(2,1)S(1)}, f32[3,256,128]{2,1,0:T(8,128)S(1)}, f32[3,256,128]{2,1,0:T(8,128)S(1)}, f32[32,16,128]{2,1,0:T(8,128)}) custom-call(f32[12,256,128]{2,1,0:T(8,128)S(1)} %get-tuple-element.12.own, bf16[12,256,128]{2,1,0:T(8,128)(2,1)S(1)} %collective-permute-done.cross, ...), custom_call_target="tpu_custom_call" | custom-call | tf_op jit(solution)/shard_map/weight_term/pallas_call | solution.py:183
  31.2 13.0 %all-to-all-start = ((f32[32,16,128]{2,1,0:T(8,128)}), f32[32,16,128]{2,1,0:T(8,128)S(1)}, u32[]{:S(2)}, u32[]{:S(2)}) async-start(f32[32,16,128]{2,1,0:T(8,128)} %get-tuple-element.20), calls=%async_computation | async-start | bytes 524288 | tf_op jit(solution)/shard_map/all_to_all | solution.py:207
  44.3 4.4 %collective-permute-start.4 = (bf16[6,256,128]{2,1,0:T(8,128)(2,1)S(1)}, bf16[6,256,128]{2,1,0:T(8,128)(2,1)S(1)}, u32[]{:S(2)}, u32[]{:S(2)}) collective-permute-start(bf16[6,256,128]{2,1,0:T(8,128)(2,1)S(1)} %get-tuple-element.18), channel_id=1, source_target_pairs={{0,1},{1,0},{2,3},{3,2},{4,7},{5,6},{6,5},{7,4},{8,9},{9,8},{10,11... | collective-permute-start | bytes 1179656 | tf_op jit(solution)/shard_map/ppermute | solution.py:196
  48.7 5.4 %all-to-all-done.got = f32[32,16,128]{2,1,0:T(8,128)S(1)} async-done(((f32[32,16,128]{2,1,0:T(8,128)}), f32[32,16,128]{2,1,0:T(8,128)S(1)}, u32[]{:S(2)}, u32[]{:S(2)}) %all-to-all-start) | async-done | bytes 262176 | tf_op jit(solution)/shard_map/all_to_all | solution.py:207
  54.1 0.7 spread.2
  54.7 9.0 %all-to-all-start.1 = ((bf16[24,16,128]{2,1,0:T(8,128)(2,1)}), bf16[24,16,128]{2,1,0:T(8,128)(2,1)S(1)}, u32[]{:S(2)}, u32[]{:S(2)}) async-start(bf16[24,16,128]{2,1,0:T(8,128)(2,1)} %spread.2), calls=%async_computation.1 | async-start | bytes 196608 | tf_op jit(solution)/shard_map/all_to_all | solution.py:209
  63.8 0.0 collective-permute-done.4.pair
  63.8 1.9 %collective-permute-start.5 = (bf16[3,256,128]{2,1,0:T(8,128)(2,1)S(1)}, bf16[3,256,128]{2,1,0:T(8,128)(2,1)S(1)}, u32[]{:S(2)}, u32[]{:S(2)}) collective-permute-start(bf16[3,256,128]{2,1,0:T(8,128)(2,1)S(1)} %add_convert_fusion), channel_id=1, source_target_pairs={{0,3},{1,2},{2,1},{3,0},{4,5},{5,4},{6,7},{7,6},{8,11},{9,10},{10,... | collective-permute-start | bytes 589832 | tf_op jit(solution)/shard_map/ppermute | solution.py:198
  65.8 4.8 %collective-permute-done.5.other = bf16[3,256,128]{2,1,0:T(8,128)(2,1)S(1)} collective-permute-done((bf16[3,256,128]{2,1,0:T(8,128)(2,1)S(1)}, bf16[3,256,128]{2,1,0:T(8,128)(2,1)S(1)}, u32[]{:S(2)}, u32[]{:S(2)}) %collective-permute-start.5) | collective-permute-done | bytes 196640 | tf_op jit(solution)/shard_map/ppermute | solution.py:198
  70.6 4.3 %all-to-all-done.1.got = bf16[24,16,128]{2,1,0:T(8,128)(2,1)S(1)} async-done(((bf16[24,16,128]{2,1,0:T(8,128)(2,1)}), bf16[24,16,128]{2,1,0:T(8,128)(2,1)S(1)}, u32[]{:S(2)}, u32[]{:S(2)}) %all-to-all-start.1) | async-done | bytes 98336 | tf_op jit(solution)/shard_map/all_to_all | solution.py:209
  74.8 0.7 spread.3
  75.5 3.9 %all-to-all-start.2 = ((bf16[32,16,128]{2,1,0:T(8,128)(2,1)}), bf16[32,16,128]{2,1,0:T(8,128)(2,1)S(1)}, u32[]{:S(2)}, u32[]{:S(2)}) async-start(bf16[32,16,128]{2,1,0:T(8,128)(2,1)} %spread.3), calls=%async_computation.2 | async-start | bytes 262144 | tf_op jit(solution)/shard_map/all_to_all | solution.py:212
  79.4 0.0 copy-done.1
  79.4 1.2 %feature_grad.1 = f32[384,256]{1,0:T(8,128)} custom-call(f32[3,256,128]{2,1,0:T(8,128)S(1)} %get-tuple-element.17.keep, bf16[6,256,128]{2,1,0:T(8,128)(2,1)S(1)} %collective-permute-done.4.pair, bf16[3,256,128]{2,1,0:T(8,128)(2,1)S(1)} %collective-permute-done.5.other, bf16[256,256]{1,0:T(8,128)(2,1)S(1)} %copy-done.1), custom_call_target="tpu_custom_call" | custom-call | tf_op jit(solution)/shard_map/feature_grad/pallas_call | solution.py:199
  80.6 8.0 %all-to-all-done.2 = bf16[32,16,128]{2,1,0:T(8,128)(2,1)S(1)} async-done(((bf16[32,16,128]{2,1,0:T(8,128)(2,1)}), bf16[32,16,128]{2,1,0:T(8,128)(2,1)S(1)}, u32[]{:S(2)}, u32[]{:S(2)}) %all-to-all-start.2) | async-done | bytes 131104 | tf_op jit(solution)/shard_map/all_to_all | solution.py:212
  88.6 0.7 convert_bitcast_fusion
  (2 shorter events, 0.1 us)
Async XLA Ops:
  0.6 20.3 %copy-start = (bf16[384,256]{1,0:T(8,128)(2,1)S(1)}, bf16[384,256]{1,0:T(8,128)(2,1)}, u32[]{:S(2)}) copy-start(bf16[384,256]{1,0:T(8,128)(2,1)} %feat0.1) | copy-start | bytes 589828
  0.6 12.4 %collective-permute-start.1 = (bf16[384,256]{1,0:T(8,128)(2,1)}, bf16[384,256]{1,0:T(8,128)(2,1)S(1)}, u32[]{:S(2)}, u32[]{:S(2)}) collective-permute-start(bf16[384,256]{1,0:T(8,128)(2,1)} %feat0.1), channel_id=1, source_target_pairs={{0,1},{1,0},{2,3},{3,2},{4,7},{5,6},{6,5},{7,4},{8,9},{9,8},{10,11... | collective-permute-start | bytes 589832 | tf_op jit(solution)/shard_map/ppermute | solution.py:175
  9.4 20.4 %collective-permute-start = (bf16[12,256,128]{2,1,0:T(8,128)(2,1)S(1)}, bf16[12,256,128]{2,1,0:T(8,128)(2,1)S(1)}, u32[]{:S(2)}, u32[]{:S(2)}) collective-permute-start(bf16[12,256,128]{2,1,0:T(8,128)(2,1)S(1)} %get-tuple-element.13), channel_id=1, source_target_pairs={{4,8},{12,16},{20,24},{28,32},{36,40},{44,48},{52,56},{60,64},{68,... | collective-permute-start | bytes 2359304 | tf_op jit(solution)/shard_map/ppermute | solution.py:138
  13.0 16.8 %collective-permute-start.2 = (bf16[12,256,128]{2,1,0:T(8,128)(2,1)S(1)}, bf16[12,256,128]{2,1,0:T(8,128)(2,1)S(1)}, u32[]{:S(2)}, u32[]{:S(2)}) collective-permute-start(bf16[12,256,128]{2,1,0:T(8,128)(2,1)S(1)} %get-tuple-element.15), channel_id=1, source_target_pairs={{0,4},{4,0},{1,5},{5,1},{2,6},{6,2},{3,7},{7,3},{8,12},{12,8},{9,1... | collective-permute-start | bytes 2359304 | tf_op jit(solution)/shard_map/ppermute | solution.py:138
  21.0 8.8 %collective-permute-start.3 = (bf16[768,256]{1,0:T(8,128)(2,1)S(1)}, bf16[768,256]{1,0:T(8,128)(2,1)S(1)}, u32[]{:S(2)}, u32[]{:S(2)}) collective-permute-start(bf16[768,256]{1,0:T(8,128)(2,1)S(1)} %pad_maximum_fusion), channel_id=1, source_target_pairs={{0,3},{1,2},{2,1},{3,0},{4,5},{5,4},{6,7},{7,6},{8,11},{9,10},{10,... | collective-permute-start | bytes 1179656 | tf_op jit(solution)/shard_map/ppermute | solution.py:179
  29.8 49.6 %copy-start.1 = (bf16[256,256]{1,0:T(8,128)(2,1)S(1)}, bf16[256,256]{1,0:T(8,128)(2,1)}, u32[]{:S(2)}) copy-start(bf16[256,256]{1,0:T(8,128)(2,1)} %weight.1) | copy-start | bytes 393220
  31.2 22.8 %all-to-all-start = ((f32[32,16,128]{2,1,0:T(8,128)}), f32[32,16,128]{2,1,0:T(8,128)S(1)}, u32[]{:S(2)}, u32[]{:S(2)}) async-start(f32[32,16,128]{2,1,0:T(8,128)} %get-tuple-element.20), calls=%async_computation | async-start | bytes 524288 | tf_op jit(solution)/shard_map/all_to_all | solution.py:207
  44.3 19.5 %collective-permute-start.4 = (bf16[6,256,128]{2,1,0:T(8,128)(2,1)S(1)}, bf16[6,256,128]{2,1,0:T(8,128)(2,1)S(1)}, u32[]{:S(2)}, u32[]{:S(2)}) collective-permute-start(bf16[6,256,128]{2,1,0:T(8,128)(2,1)S(1)} %get-tuple-element.18), channel_id=1, source_target_pairs={{0,1},{1,0},{2,3},{3,2},{4,7},{5,6},{6,5},{7,4},{8,9},{9,8},{10,11... | collective-permute-start | bytes 1179656 | tf_op jit(solution)/shard_map/ppermute | solution.py:196
  54.7 20.1 %all-to-all-start.1 = ((bf16[24,16,128]{2,1,0:T(8,128)(2,1)}), bf16[24,16,128]{2,1,0:T(8,128)(2,1)S(1)}, u32[]{:S(2)}, u32[]{:S(2)}) async-start(bf16[24,16,128]{2,1,0:T(8,128)(2,1)} %spread.2), calls=%async_computation.1 | async-start | bytes 196608 | tf_op jit(solution)/shard_map/all_to_all | solution.py:209
  63.8 6.7 %collective-permute-start.5 = (bf16[3,256,128]{2,1,0:T(8,128)(2,1)S(1)}, bf16[3,256,128]{2,1,0:T(8,128)(2,1)S(1)}, u32[]{:S(2)}, u32[]{:S(2)}) collective-permute-start(bf16[3,256,128]{2,1,0:T(8,128)(2,1)S(1)} %add_convert_fusion), channel_id=1, source_target_pairs={{0,3},{1,2},{2,1},{3,0},{4,5},{5,4},{6,7},{7,6},{8,11},{9,10},{10,... | collective-permute-start | bytes 589832 | tf_op jit(solution)/shard_map/ppermute | solution.py:198
  75.5 13.0 %all-to-all-start.2 = ((bf16[32,16,128]{2,1,0:T(8,128)(2,1)}), bf16[32,16,128]{2,1,0:T(8,128)(2,1)S(1)}, u32[]{:S(2)}, u32[]{:S(2)}) async-start(bf16[32,16,128]{2,1,0:T(8,128)(2,1)} %spread.3), calls=%async_computation.2 | async-start | bytes 262144 | tf_op jit(solution)/shard_map/all_to_all | solution.py:212

commit v7 on v6

--- a/solution.py
+++ b/solution.py
@@ -90,10 +90,11 @@
     parts, both, _ = term.shape
     height = acc.shape[0] // parts
     for i in range(parts):
-        for j in range(both // height):
-            term[i, pl.ds(j * height, height), :] = acc[
-                i * height : (i + 1) * height, j * edge : (j + 1) * edge
-            ]
+        halves = [
+            acc[i * height : (i + 1) * height, j * edge : (j + 1) * edge]
+            for j in range(both // height)
+        ]
+        term[i] = jnp.concatenate(halves, axis=0).astype(term.dtype)
 
 
 def spread_kernel(scale, got, copies):
@@ -186,7 +187,7 @@
             jax.ShapeDtypeStruct((2 * blocks, channels, edge), jnp.bfloat16),
             jax.ShapeDtypeStruct(third, jnp.float32),
             jax.ShapeDtypeStruct(third, jnp.float32),
-            jax.ShapeDtypeStruct((x * y, halves * height, edge), jnp.float32),
+            jax.ShapeDtypeStruct((x * y, halves * height, edge), jnp.bfloat16),
         ),
         in_specs=[VMEM] * 6,
         out_specs=(VMEM,) * 4,
@@ -207,7 +208,6 @@
     got = lax.all_to_all(term, ("x", "y"), 0, 0)
     copies = spread(got, 2 * z, math.sqrt(rows * x * rows_dev))
     got = lax.all_to_all(copies, ("z", "core"), 0, 0)
-    got, from_far = lax.optimization_barrier((got, from_far))
     copies = spread(got, x * y, 1.0)
     pieces = lax.all_to_all(copies, ("x", "y"), 0, 0).astype(jnp.float32)
     pieces = pieces.reshape(x * y, halves, height, edge)

time: 90 us -> 87.9 us (0.977)
  blocking collectives: 0 us -> 19.2 us
  waiting for transfers between devices: 29.3 us -> 16.5 us
  starting transfers between devices: 51.1 us -> 43 us
    all_to_all x0 -> x1, blocking collectives: none -> 19.2 us  [local(): got = lax.all_to_all(copies, ('z', 'core'), 0, 0)]
    all_to_all x1 -> x0, starting transfers between devices: 9.03 us -> none  [local(): got = lax.all_to_all(copies, ('z', 'core'), 0, 0)]
    all_to_all x1, waiting for transfers between devices: 8 us -> 0.52 us  [local(): pieces = lax.all_to_all(copies, ('x', 'y'), 0, 0).astype(jnp.float32)]
    all_to_all x1 -> x0, waiting for transfers between devices: 4.28 us -> none  [local(): got = lax.all_to_all(copies, ('z', 'core'), 0, 0)]
    ppermute x1, starting transfers between devices: 1.93 us -> 3.07 us  [local(): from_far = lax.ppermute(onward, ('core', 'x'), far)]
  transfers between devices with their start and end apart: 9 -> 8, of which waited for: 5 -> 4; matrix products, arithmetic and copies ran while one was open for 0% -> 0% of each run, Pallas kernels for 5% -> 5%
where the time goes in v7:
time: 87.9 us; the launch traced here: 86.8 us
  starting transfers between devices  43 us (49%)
  blocking collectives  19.2 us (22%)
  waiting for transfers between devices  16.5 us (19%)
  Pallas kernels  6.04 us (7%)
  between operations  1.4 us (2%)
    all_to_all x1, blocking collectives, local(): got = lax.all_to_all(copies, ('z', 'core'), 0, 0)  19.2 us
    all_to_all x1, starting transfers between devices, local(): got = lax.all_to_all(term, ('x', 'y'), 0, 0)  12.8 us
    ppermute x2, starting transfers between devices, swap(): return lax.ppermute(array, axes, pairs + [(j, i) for i, j in pairs])  11.5 us
    ppermute x1, waiting for transfers between devices, local(): lax.ppermute(jnp.concatenate([features, feat1], axis=0), ('core', 'x'), far)  6.83 us
    ppermute x1, starting transfers between devices, local(): feat1 = lax.ppermute(features, ('core', 'x'), near)  5.35 us
    all_to_all x1, waiting for transfers between devices, local(): got = lax.all_to_all(term, ('x', 'y'), 0, 0)  4.77 us
    ppermute x1, starting transfers between devices, local(): from_near = lax.ppermute(give, ('core', 'x'), near)  4.39 us
    ppermute x1, waiting for transfers between devices, local(): from_far = lax.ppermute(onward, ('core', 'x'), far)  4.33 us
  transfers between devices with their start and end apart: 8, of which 4 were waited for; matrix products, arithmetic and copies ran while one was open for 0% of the time, Pallas kernels for 5%

profile of v7, /device:TPU:1, one launch (start us, length us, event | category | flops | bytes accessed | tf_op | source)
XLA Modules:
  0.0 86.8 jit_solution(5797733173108730253)
XLA Ops:
  0.6 0.0 copy-start
  0.6 5.3 %collective-permute-start.1 = (bf16[384,256]{1,0:T(8,128)(2,1)}, bf16[384,256]{1,0:T(8,128)(2,1)S(1)}, u32[]{:S(2)}, u32[]{:S(2)}) collective-permute-start(bf16[384,256]{1,0:T(8,128)(2,1)} %feat0.1), channel_id=1, source_target_pairs={{0,1},{1,0},{2,3},{3,2},{4,7},{5,6},{6,5},{7,4},{8,9},{9,8},{10,11... | collective-permute-start | bytes 589832 | tf_op jit(solution)/shard_map/ppermute | solution.py:176
  6.6 2.8 %tile_sums.1 = (bf16[12,256,128]{2,1,0:T(8,128)(2,1)S(1)}, bf16[12,256,128]{2,1,0:T(8,128)(2,1)S(1)}, f32[12,256,128]{2,1,0:T(8,128)S(1)}) custom-call(s32[1]{0:T(128)S(6)} %copy.9.count, s32[3,72]{1,0:T(4,128)} %bitcast.8, bf16[384,256]{1,0:T(8,128)(2,1)} %pre_hbm.1, f32[384,256]{1,0:T(8,128)} %up_hbm.1, bf16[72,128,128]{2,1,0:T(8,128)(2,1)} %tiles_hbm.1), custom_call_target="tpu_custom_call" | custom-call | tf_op jit(solution)/shard_map/tile_sums/pallas_call | solution.py:154
  9.4 3.6 %collective-permute-start = (bf16[12,256,128]{2,1,0:T(8,128)(2,1)S(1)}, bf16[12,256,128]{2,1,0:T(8,128)(2,1)S(1)}, u32[]{:S(2)}, u32[]{:S(2)}) collective-permute-start(bf16[12,256,128]{2,1,0:T(8,128)(2,1)S(1)} %get-tuple-element.12), channel_id=1, source_target_pairs={{4,8},{12,16},{20,24},{28,32},{36,40},{44,48},{52,56},{60,64},{68,... | collective-permute-start | bytes 2359304 | tf_op jit(solution)/shard_map/ppermute | solution.py:139
  13.0 0.0 collective-permute-done.1.feat1
  13.0 7.9 %collective-permute-start.2 = (bf16[12,256,128]{2,1,0:T(8,128)(2,1)S(1)}, bf16[12,256,128]{2,1,0:T(8,128)(2,1)S(1)}, u32[]{:S(2)}, u32[]{:S(2)}) collective-permute-start(bf16[12,256,128]{2,1,0:T(8,128)(2,1)S(1)} %get-tuple-element.14), channel_id=1, source_target_pairs={{0,4},{4,0},{1,5},{5,1},{2,6},{6,2},{3,7},{7,3},{8,12},{12,8},{9,1... | collective-permute-start | bytes 2359304 | tf_op jit(solution)/shard_map/ppermute | solution.py:139
  21.0 0.0 copy-done
  21.0 2.0 %collective-permute-start.3 = (bf16[768,256]{1,0:T(8,128)(2,1)S(1)}, bf16[768,256]{1,0:T(8,128)(2,1)S(1)}, u32[]{:S(2)}, u32[]{:S(2)}) collective-permute-start(bf16[768,256]{1,0:T(8,128)(2,1)S(1)} %pad_maximum_fusion), channel_id=1, source_target_pairs={{0,3},{1,2},{2,1},{3,0},{4,5},{5,4},{6,7},{7,6},{8,11},{9,10},{10,... | collective-permute-start | bytes 1179656 | tf_op jit(solution)/shard_map/ppermute | solution.py:180
  23.0 6.8 %collective-permute-done.3.feat32 = bf16[768,256]{1,0:T(8,128)(2,1)S(1)} collective-permute-done((bf16[768,256]{1,0:T(8,128)(2,1)S(1)}, bf16[768,256]{1,0:T(8,128)(2,1)S(1)}, u32[]{:S(2)}, u32[]{:S(2)}) %collective-permute-start.3) | collective-permute-done | bytes 393248 | tf_op jit(solution)/shard_map/ppermute | solution.py:180
  29.8 0.0 collective-permute-done.cross
  29.8 0.0 collective-permute-done.2.chip
  29.8 0.0 copy-start.1
  29.8 1.4 %weight_term.1 = (bf16[6,256,128]{2,1,0:T(8,128)(2,1)S(1)}, f32[3,256,128]{2,1,0:T(8,128)S(1)}, f32[3,256,128]{2,1,0:T(8,128)S(1)}, bf16[32,16,128]{2,1,0:T(8,128)(2,1)}) custom-call(f32[12,256,128]{2,1,0:T(8,128)S(1)} %get-tuple-element.11.own, bf16[12,256,128]{2,1,0:T(8,128)(2,1)S(1)} %collective-permute-done.cross, ...), custom_call_target="tpu_custom_call" | custom-call | tf_op jit(solution)/shard_map/weight_term/pallas_call | solution.py:184
  31.2 12.8 %all-to-all-start = ((bf16[32,16,128]{2,1,0:T(8,128)(2,1)}), bf16[32,16,128]{2,1,0:T(8,128)(2,1)S(1)}, u32[]{:S(2)}, u32[]{:S(2)}) async-start(bf16[32,16,128]{2,1,0:T(8,128)(2,1)} %get-tuple-element.19), calls=%async_computation | async-start | bytes 262144 | tf_op jit(solution)/shard_map/all_to_all | solution.py:208
  44.0 4.4 %collective-permute-start.4 = (bf16[6,256,128]{2,1,0:T(8,128)(2,1)S(1)}, bf16[6,256,128]{2,1,0:T(8,128)(2,1)S(1)}, u32[]{:S(2)}, u32[]{:S(2)}) collective-permute-start(bf16[6,256,128]{2,1,0:T(8,128)(2,1)S(1)} %get-tuple-element.17), channel_id=1, source_target_pairs={{0,1},{1,0},{2,3},{3,2},{4,7},{5,6},{6,5},{7,4},{8,9},{9,8},{10,11... | collective-permute-start | bytes 1179656 | tf_op jit(solution)/shard_map/ppermute | solution.py:197
  48.4 4.8 %all-to-all-done.got = bf16[32,16,128]{2,1,0:T(8,128)(2,1)S(1)} async-done(((bf16[32,16,128]{2,1,0:T(8,128)(2,1)}), bf16[32,16,128]{2,1,0:T(8,128)(2,1)S(1)}, u32[]{:S(2)}, u32[]{:S(2)}) %all-to-all-start) | async-done | bytes 131104 | tf_op jit(solution)/shard_map/all_to_all | solution.py:208
  53.2 19.2 %all_to_all.15.got = bf16[24,16,128]{2,1,0:T(8,128)(2,1)S(1)} all-to-all(bf16[24,16,128]{2,1,0:T(8,128)(2,1)S(1)} %spread.2), channel_id=1, replica_groups=mesh['y'=8,'z'=12,'core'=2,'x'=4] {'z','core'}, dimensions={0} | all-to-all | bytes 196608 | tf_op jit(solution)/shard_map/all_to_all | solution.py:210
  72.4 0.7 spread.3
  73.1 3.9 %all-to-all-start.2 = ((bf16[32,16,128]{2,1,0:T(8,128)(2,1)}), bf16[32,16,128]{2,1,0:T(8,128)(2,1)S(1)}, u32[]{:S(2)}, u32[]{:S(2)}) async-start(bf16[32,16,128]{2,1,0:T(8,128)(2,1)} %spread.3), calls=%async_computation.2 | async-start | bytes 262144 | tf_op jit(solution)/shard_map/all_to_all | solution.py:212
  77.0 0.0 collective-permute-done.4.pair
  77.0 3.1 %collective-permute-start.5 = (bf16[3,256,128]{2,1,0:T(8,128)(2,1)S(1)}, bf16[3,256,128]{2,1,0:T(8,128)(2,1)S(1)}, u32[]{:S(2)}, u32[]{:S(2)}) collective-permute-start(bf16[3,256,128]{2,1,0:T(8,128)(2,1)S(1)} %add_convert_fusion), channel_id=1, source_target_pairs={{0,3},{1,2},{2,1},{3,0},{4,5},{5,4},{6,7},{7,6},{8,11},{9,10},{10,... | collective-permute-start | bytes 589832 | tf_op jit(solution)/shard_map/ppermute | solution.py:199
  80.1 4.3 %collective-permute-done.5.other = bf16[3,256,128]{2,1,0:T(8,128)(2,1)S(1)} collective-permute-done((bf16[3,256,128]{2,1,0:T(8,128)(2,1)S(1)}, bf16[3,256,128]{2,1,0:T(8,128)(2,1)S(1)}, u32[]{:S(2)}, u32[]{:S(2)}) %collective-permute-start.5) | collective-permute-done | bytes 196640 | tf_op jit(solution)/shard_map/ppermute | solution.py:199
  84.4 0.0 copy-done.1
  84.4 1.2 %feature_grad.1 = f32[384,256]{1,0:T(8,128)} custom-call(f32[3,256,128]{2,1,0:T(8,128)S(1)} %get-tuple-element.16.keep, bf16[6,256,128]{2,1,0:T(8,128)(2,1)S(1)} %collective-permute-done.4.pair, bf16[3,256,128]{2,1,0:T(8,128)(2,1)S(1)} %collective-permute-done.5.other, bf16[256,256]{1,0:T(8,128)(2,1)S(1)} %copy-done.1), custom_call_target="tpu_custom_call" | custom-call | tf_op jit(solution)/shard_map/feature_grad/pallas_call | solution.py:200
  85.6 0.5 all-to-all-done.2
  86.1 0.7 convert_bitcast_fusion
  (3 shorter events, 0.1 us)
Async XLA Ops:
  0.6 20.3 %copy-start = (bf16[384,256]{1,0:T(8,128)(2,1)S(1)}, bf16[384,256]{1,0:T(8,128)(2,1)}, u32[]{:S(2)}) copy-start(bf16[384,256]{1,0:T(8,128)(2,1)} %feat0.1) | copy-start | bytes 589828
  0.6 12.4 %collective-permute-start.1 = (bf16[384,256]{1,0:T(8,128)(2,1)}, bf16[384,256]{1,0:T(8,128)(2,1)S(1)}, u32[]{:S(2)}, u32[]{:S(2)}) collective-permute-start(bf16[384,256]{1,0:T(8,128)(2,1)} %feat0.1), channel_id=1, source_target_pairs={{0,1},{1,0},{2,3},{3,2},{4,7},{5,6},{6,5},{7,4},{8,9},{9,8},{10,11... | collective-permute-start | bytes 589832 | tf_op jit(solution)/shard_map/ppermute | solution.py:176
  9.4 20.4 %collective-permute-start = (bf16[12,256,128]{2,1,0:T(8,128)(2,1)S(1)}, bf16[12,256,128]{2,1,0:T(8,128)(2,1)S(1)}, u32[]{:S(2)}, u32[]{:S(2)}) collective-permute-start(bf16[12,256,128]{2,1,0:T(8,128)(2,1)S(1)} %get-tuple-element.12), channel_id=1, source_target_pairs={{4,8},{12,16},{20,24},{28,32},{36,40},{44,48},{52,56},{60,64},{68,... | collective-permute-start | bytes 2359304 | tf_op jit(solution)/shard_map/ppermute | solution.py:139
  13.0 16.8 %collective-permute-start.2 = (bf16[12,256,128]{2,1,0:T(8,128)(2,1)S(1)}, bf16[12,256,128]{2,1,0:T(8,128)(2,1)S(1)}, u32[]{:S(2)}, u32[]{:S(2)}) collective-permute-start(bf16[12,256,128]{2,1,0:T(8,128)(2,1)S(1)} %get-tuple-element.14), channel_id=1, source_target_pairs={{0,4},{4,0},{1,5},{5,1},{2,6},{6,2},{3,7},{7,3},{8,12},{12,8},{9,1... | collective-permute-start | bytes 2359304 | tf_op jit(solution)/shard_map/ppermute | solution.py:139
  21.0 8.8 %collective-permute-start.3 = (bf16[768,256]{1,0:T(8,128)(2,1)S(1)}, bf16[768,256]{1,0:T(8,128)(2,1)S(1)}, u32[]{:S(2)}, u32[]{:S(2)}) collective-permute-start(bf16[768,256]{1,0:T(8,128)(2,1)S(1)} %pad_maximum_fusion), channel_id=1, source_target_pairs={{0,3},{1,2},{2,1},{3,0},{4,5},{5,4},{6,7},{7,6},{8,11},{9,10},{10,... | collective-permute-start | bytes 1179656 | tf_op jit(solution)/shard_map/ppermute | solution.py:180
  29.8 54.6 %copy-start.1 = (bf16[256,256]{1,0:T(8,128)(2,1)S(1)}, bf16[256,256]{1,0:T(8,128)(2,1)}, u32[]{:S(2)}) copy-start(bf16[256,256]{1,0:T(8,128)(2,1)} %weight.1) | copy-start | bytes 393220
  31.2 22.0 %all-to-all-start = ((bf16[32,16,128]{2,1,0:T(8,128)(2,1)}), bf16[32,16,128]{2,1,0:T(8,128)(2,1)S(1)}, u32[]{:S(2)}, u32[]{:S(2)}) async-start(bf16[32,16,128]{2,1,0:T(8,128)(2,1)} %get-tuple-element.19), calls=%async_computation | async-start | bytes 262144 | tf_op jit(solution)/shard_map/all_to_all | solution.py:208
  44.0 32.9 %collective-permute-start.4 = (bf16[6,256,128]{2,1,0:T(8,128)(2,1)S(1)}, bf16[6,256,128]{2,1,0:T(8,128)(2,1)S(1)}, u32[]{:S(2)}, u32[]{:S(2)}) collective-permute-start(bf16[6,256,128]{2,1,0:T(8,128)(2,1)S(1)} %get-tuple-element.17), channel_id=1, source_target_pairs={{0,1},{1,0},{2,3},{3,2},{4,7},{5,6},{6,5},{7,4},{8,9},{9,8},{10,11... | collective-permute-start | bytes 1179656 | tf_op jit(solution)/shard_map/ppermute | solution.py:197
  73.1 13.0 %all-to-all-start.2 = ((bf16[32,16,128]{2,1,0:T(8,128)(2,1)}), bf16[32,16,128]{2,1,0:T(8,128)(2,1)S(1)}, u32[]{:S(2)}, u32[]{:S(2)}) async-start(bf16[32,16,128]{2,1,0:T(8,128)(2,1)} %spread.3), calls=%async_computation.2 | async-start | bytes 262144 | tf_op jit(solution)/shard_map/all_to_all | solution.py:212
  77.0 7.4 %collective-permute-start.5 = (bf16[3,256,128]{2,1,0:T(8,128)(2,1)S(1)}, bf16[3,256,128]{2,1,0:T(8,128)(2,1)S(1)}, u32[]{:S(2)}, u32[]{:S(2)}) collective-permute-start(bf16[3,256,128]{2,1,0:T(8,128)(2,1)S(1)} %add_convert_fusion), channel_id=1, source_target_pairs={{0,3},{1,2},{2,1},{3,0},{4,5},{5,4},{6,7},{7,6},{8,11},{9,10},{10,... | collective-permute-start | bytes 589832 | tf_op jit(solution)/shard_map/ppermute | solution.py:199

commit v8 on v7

--- a/solution.py
+++ b/solution.py
@@ -66,10 +66,10 @@
     return high, (value - high.astype(jnp.float32)).astype(jnp.bfloat16)
 
 
-def weight_kernel(own, cross, chip, feat0, feat1, feat32, give, keep0, keep3, term):
+def weight_kernel(own, cross, chip, feat0, feat1, feat2, feat3, give1, give2, keep0, keep3, term):
     blocks, channels, edge = keep0.shape
     held = []
-    for k, (feat, at) in enumerate(((feat0, 0), (feat1, 0), (feat32, blocks), (feat32, 0))):
+    for k, feat in enumerate((feat0, feat1, feat2, feat3)):
         for b in range(blocks):
             i = k * blocks + b
             g = own[i] + cross[i].astype(jnp.float32) + chip[i].astype(jnp.float32)
@@ -78,8 +78,8 @@
             elif k == 3:
                 keep3[b] = g
             else:
-                give[(k - 1) * blocks + b] = g.astype(jnp.bfloat16)
-            held.append((g, feat, (at + b) * edge))
+                (give1 if k == 1 else give2)[b] = g.astype(jnp.bfloat16)
+            held.append((g, feat, b * edge))
     acc = None
     for (g, feat, at), (g2, feat2, at2) in zip(held[::2], held[1::2]):
         rows = jnp.concatenate([feat[pl.ds(at, edge), :], feat2[pl.ds(at2, edge), :]], axis=0)
@@ -177,26 +177,34 @@
     chip, feat1 = lax.optimization_barrier((chip, feat1))
     from_cross = swap(cross, ("y", "z", "core"), rows, 1)
     from_chip = swap(chip, "core", 2, 0)
-    feat32 = lax.ppermute(jnp.concatenate([features, feat1], axis=0), ("core", "x"), far)
+    feat3 = lax.ppermute(features, ("core", "x"), far)
+    feat2 = lax.ppermute(feat1, ("core", "x"), far)
     halves = channels // edge
     height = channels // (x * y)
     third = (blocks, channels, edge)
-    give, keep0, keep3, term = pl.pallas_call(
+    give1, give2, keep0, keep3, term = pl.pallas_call(
         weight_kernel,
         out_shape=(
-            jax.ShapeDtypeStruct((2 * blocks, channels, edge), jnp.bfloat16),
+            jax.ShapeDtypeStruct(third, jnp.bfloat16),
+            jax.ShapeDtypeStruct(third, jnp.bfloat16),
             jax.ShapeDtypeStruct(third, jnp.float32),
             jax.ShapeDtypeStruct(third, jnp.float32),
             jax.ShapeDtypeStruct((x * y, halves * height, edge), jnp.bfloat16),
         ),
-        in_specs=[VMEM] * 6,
-        out_specs=(VMEM,) * 4,
+        in_specs=[VMEM] * 7,
+        out_specs=(VMEM,) * 5,
         compiler_params=params,
         name="weight_term",
-    )(own, from_cross, from_chip, features, feat1, feat32)
-    from_near = lax.ppermute(give, ("core", "x"), near)
-    onward = (keep3 + from_near[blocks:].astype(jnp.float32)).astype(jnp.bfloat16)
+    )(own, from_cross, from_chip, features, feat1, feat2, feat3)
+    passing = lax.ppermute(give2, ("core", "x"), near)
+    onward = (keep3 + passing.astype(jnp.float32)).astype(jnp.bfloat16)
     from_far = lax.ppermute(onward, ("core", "x"), far)
+    got = lax.all_to_all(term, ("x", "y"), 0, 0)
+    got, give1 = lax.optimization_barrier((got, give1))
+    from_near = lax.ppermute(give1, ("core", "x"), near)
+    copies = spread(got, 2 * z, math.sqrt(rows * x * rows_dev))
+    got = lax.all_to_all(copies, ("z", "core"), 0, 0)
+    got, from_near, from_far = lax.optimization_barrier((got, from_near, from_far))
     grad_features = pl.pallas_call(
         feature_kernel,
         out_shape=jax.ShapeDtypeStruct((rows_dev, channels), jnp.float32),
@@ -205,9 +213,6 @@
         compiler_params=params,
         name="feature_grad",
     )(keep0, from_near, from_far, weight)
-    got = lax.all_to_all(term, ("x", "y"), 0, 0)
-    copies = spread(got, 2 * z, math.sqrt(rows * x * rows_dev))
-    got = lax.all_to_all(copies, ("z", "core"), 0, 0)
     copies = spread(got, x * y, 1.0)
     pieces = lax.all_to_all(copies, ("x", "y"), 0, 0).astype(jnp.float32)
     pieces = pieces.reshape(x * y, halves, height, edge)

time: 87.9 us -> 89.3 us (1.016)
  blocking collectives: 19.2 us -> 0 us
  starting transfers between devices: 43 us -> 56.6 us
  waiting for transfers between devices: 16.5 us -> 23.1 us
    all_to_all x1 -> x0, blocking collectives: 19.2 us -> none  [local(): got = lax.all_to_all(copies, ('z', 'core'), 0, 0)]
    all_to_all x0 -> x1, starting transfers between devices: none -> 8.26 us  [local(): got = lax.all_to_all(copies, ('z', 'core'), 0, 0)]
    all_to_all x1, waiting for transfers between devices: 0.52 us -> 7.98 us  [local(): pieces = lax.all_to_all(copies, ('x', 'y'), 0, 0).astype(jnp.float32)]
    ppermute x2 -> x4, starting transfers between devices: 6.38 us -> 12.6 us  [the longest x1 4.39 us: local(): passing = lax.ppermute(give2, ('core', 'x'), near)]
    ppermute x1, waiting for transfers between devices: 4.33 us -> 1.52 us  [local(): from_far = lax.ppermute(onward, ('core', 'x'), far)]
    ppermute x2 -> x4, waiting for transfers between devices: 6.83 us -> 8.54 us  [the longest x1 3.96 us: local(): from_near = lax.ppermute(give1, ('core', 'x'), near)]
  transfers between devices with their start and end apart: 8 -> 11, of which waited for: 4 -> 7; matrix products, arithmetic and copies ran while one was open for 0% -> 0% of each run, Pallas kernels for 5% -> 5%
where the time goes in v8:
time: 89.3 us; the launch traced here: 88.6 us
  starting transfers between devices  56.6 us (63%)
  waiting for transfers between devices  23.1 us (26%)
  Pallas kernels  6.69 us (7%)
  between operations  1.43 us (2%)
    all_to_all x1, starting transfers between devices, local(): got = lax.all_to_all(term, ('x', 'y'), 0, 0)  12.8 us
    ppermute x2, starting transfers between devices, swap(): return lax.ppermute(array, axes, pairs + [(j, i) for i, j in pairs])  11.5 us
    all_to_all x1, starting transfers between devices, local(): got = lax.all_to_all(copies, ('z', 'core'), 0, 0)  8.26 us
    all_to_all x1, waiting for transfers between devices, local(): pieces = lax.all_to_all(copies, ('x', 'y'), 0, 0).astype(jnp.float32)  7.98 us
    ppermute x1, starting transfers between devices, local(): feat1 = lax.ppermute(features, ('core', 'x'), near)  5.35 us
    all_to_all x1, waiting for transfers between devices, local(): got = lax.all_to_all(term, ('x', 'y'), 0, 0)  4.75 us
    ppermute x1, starting transfers between devices, local(): passing = lax.ppermute(give2, ('core', 'x'), near)  4.39 us
    ppermute x1, waiting for transfers between devices, local(): from_near = lax.ppermute(give1, ('core', 'x'), near)  3.96 us
  transfers between devices with their start and end apart: 11, of which 7 were waited for; matrix products, arithmetic and copies ran while one was open for 0% of the time, Pallas kernels for 5%

profile of v8, /device:TPU:1, one launch (start us, length us, event | category | flops | bytes accessed | tf_op | source)
XLA Modules:
  0.0 88.6 jit_solution(16206360620892561529)
XLA Ops:
  0.6 0.0 copy-start
  0.6 5.3 %collective-permute-start.1 = (bf16[384,256]{1,0:T(8,128)(2,1)}, bf16[384,256]{1,0:T(8,128)(2,1)S(1)}, u32[]{:S(2)}, u32[]{:S(2)}) collective-permute-start(bf16[384,256]{1,0:T(8,128)(2,1)} %feat0.1), channel_id=1, source_target_pairs={{0,1},{1,0},{2,3},{3,2},{4,7},{5,6},{6,5},{7,4},{8,9},{9,8},{10,11... | collective-permute-start | bytes 589832 | tf_op jit(solution)/shard_map/ppermute | solution.py:176
  6.6 2.8 %tile_sums.1 = (bf16[12,256,128]{2,1,0:T(8,128)(2,1)S(1)}, bf16[12,256,128]{2,1,0:T(8,128)(2,1)S(1)}, f32[12,256,128]{2,1,0:T(8,128)S(1)}) custom-call(s32[1]{0:T(128)S(6)} %copy.9.count, s32[3,72]{1,0:T(4,128)} %bitcast.8, bf16[384,256]{1,0:T(8,128)(2,1)} %pre_hbm.1, f32[384,256]{1,0:T(8,128)} %up_hbm.1, bf16[72,128,128]{2,1,0:T(8,128)(2,1)} %tiles_hbm.1), custom_call_target="tpu_custom_call" | custom-call | tf_op jit(solution)/shard_map/tile_sums/pallas_call | solution.py:154
  9.4 4.2 %collective-permute-start = (bf16[12,256,128]{2,1,0:T(8,128)(2,1)S(1)}, bf16[12,256,128]{2,1,0:T(8,128)(2,1)S(1)}, u32[]{:S(2)}, u32[]{:S(2)}) collective-permute-start(bf16[12,256,128]{2,1,0:T(8,128)(2,1)S(1)} %get-tuple-element.18), channel_id=1, source_target_pairs={{4,8},{12,16},{20,24},{28,32},{36,40},{44,48},{52,56},{60,64},{68,... | collective-permute-start | bytes 2359304 | tf_op jit(solution)/shard_map/ppermute | solution.py:139
  13.6 0.0 collective-permute-done.1.feat1
  13.6 7.3 %collective-permute-start.2 = (bf16[12,256,128]{2,1,0:T(8,128)(2,1)S(1)}, bf16[12,256,128]{2,1,0:T(8,128)(2,1)S(1)}, u32[]{:S(2)}, u32[]{:S(2)}) collective-permute-start(bf16[12,256,128]{2,1,0:T(8,128)(2,1)S(1)} %get-tuple-element.20), channel_id=1, source_target_pairs={{0,4},{4,0},{1,5},{5,1},{2,6},{6,2},{3,7},{7,3},{8,12},{12,8},{9,1... | collective-permute-start | bytes 2359304 | tf_op jit(solution)/shard_map/ppermute | solution.py:139
  21.0 0.0 copy-done
  21.0 3.2 %collective-permute-start.4 = (bf16[384,256]{1,0:T(8,128)(2,1)S(1)}, bf16[384,256]{1,0:T(8,128)(2,1)S(1)}, u32[]{:S(2)}, u32[]{:S(2)}) collective-permute-start(bf16[384,256]{1,0:T(8,128)(2,1)S(1)} %copy-done), channel_id=1, source_target_pairs={{0,3},{1,2},{2,1},{3,0},{4,5},{5,4},{6,7},{7,6},{8,11},{9,10},{10,... | collective-permute-start | bytes 589832 | tf_op jit(solution)/shard_map/ppermute | solution.py:180
  24.1 2.1 %collective-permute-start.3 = (bf16[384,256]{1,0:T(8,128)(2,1)S(1)}, bf16[384,256]{1,0:T(8,128)(2,1)S(1)}, u32[]{:S(2)}, u32[]{:S(2)}) collective-permute-start(bf16[384,256]{1,0:T(8,128)(2,1)S(1)} %collective-permute-done.1.feat1), channel_id=1, source_target_pairs={{0,3},{1,2},{2,1},{3,0},{4,5},{5,4},{6,7},{7,6},{8,11},{9,10},{10,... | collective-permute-start | bytes 589832 | tf_op jit(solution)/shard_map/ppermute | solution.py:181
  26.3 1.4 %collective-permute-done.4.feat3 = bf16[384,256]{1,0:T(8,128)(2,1)S(1)} collective-permute-done((bf16[384,256]{1,0:T(8,128)(2,1)S(1)}, bf16[384,256]{1,0:T(8,128)(2,1)S(1)}, u32[]{:S(2)}, u32[]{:S(2)}) %collective-permute-start.4) | collective-permute-done | bytes 196640 | tf_op jit(solution)/shard_map/ppermute | solution.py:180
  27.7 3.2 %collective-permute-done.3.feat2 = bf16[384,256]{1,0:T(8,128)(2,1)S(1)} collective-permute-done((bf16[384,256]{1,0:T(8,128)(2,1)S(1)}, bf16[384,256]{1,0:T(8,128)(2,1)S(1)}, u32[]{:S(2)}, u32[]{:S(2)}) %collective-permute-start.3) | collective-permute-done | bytes 196640 | tf_op jit(solution)/shard_map/ppermute | solution.py:181
  30.9 0.0 collective-permute-done.cross
  30.9 0.0 collective-permute-done.2.chip
  30.9 0.0 copy-start.1
  30.9 1.4 %weight_term.1 = (bf16[3,256,128]{2,1,0:T(8,128)(2,1)S(1)}, bf16[3,256,128]{2,1,0:T(8,128)(2,1)S(1)}, f32[3,256,128]{2,1,0:T(8,128)S(1)}, f32[3,256,128]{2,1,0:T(8,128)S(1)}, bf16[32,16,128]{2,1,0:T(8,128)(2,1)}) custom-call(f32[12,256,128]{2,1,0:T(8,128)S(1)} %get-tuple-element.17.own, bf16[12,256,128]{2,1,0:T(8,128)(2,1)S(1)} %collective-permute-done.cross, ...), custom_call_target="tpu_custom_call" | custom-call | tf_op jit(solution)/shard_map/weight_term/pallas_call | solution.py:185
  32.2 12.8 %all-to-all-start = ((bf16[32,16,128]{2,1,0:T(8,128)(2,1)}), bf16[32,16,128]{2,1,0:T(8,128)(2,1)S(1)}, u32[]{:S(2)}, u32[]{:S(2)}) async-start(bf16[32,16,128]{2,1,0:T(8,128)(2,1)} %get-tuple-element.23), calls=%async_computation | async-start | bytes 262144 | tf_op jit(solution)/shard_map/all_to_all | solution.py:202
  45.0 4.4 %collective-permute-start.6 = (bf16[3,256,128]{2,1,0:T(8,128)(2,1)S(1)}, bf16[3,256,128]{2,1,0:T(8,128)(2,1)S(1)}, u32[]{:S(2)}, u32[]{:S(2)}) collective-permute-start(bf16[3,256,128]{2,1,0:T(8,128)(2,1)S(1)} %get-tuple-element.28), channel_id=1, source_target_pairs={{0,1},{1,0},{2,3},{3,2},{4,7},{5,6},{6,5},{7,4},{8,9},{9,8},{10,11... | collective-permute-start | bytes 589832 | tf_op jit(solution)/shard_map/ppermute | solution.py:199
  49.4 4.7 %all-to-all-done.got = bf16[32,16,128]{2,1,0:T(8,128)(2,1)S(1)} async-done(((bf16[32,16,128]{2,1,0:T(8,128)(2,1)}), bf16[32,16,128]{2,1,0:T(8,128)(2,1)S(1)}, u32[]{:S(2)}, u32[]{:S(2)}) %all-to-all-start) | async-done | bytes 131104 | tf_op jit(solution)/shard_map/all_to_all | solution.py:202
  54.1 0.7 spread.2
  54.8 8.3 %all-to-all-start.1 = ((bf16[24,16,128]{2,1,0:T(8,128)(2,1)}), bf16[24,16,128]{2,1,0:T(8,128)(2,1)S(1)}, u32[]{:S(2)}, u32[]{:S(2)}) async-start(bf16[24,16,128]{2,1,0:T(8,128)(2,1)} %spread.2), calls=%async_computation.1 | async-start | bytes 196608 | tf_op jit(solution)/shard_map/all_to_all | solution.py:206
  63.1 0.0 collective-permute-done.6
  63.1 2.2 %collective-permute-start.7 = (bf16[3,256,128]{2,1,0:T(8,128)(2,1)S(1)}, bf16[3,256,128]{2,1,0:T(8,128)(2,1)S(1)}, u32[]{:S(2)}, u32[]{:S(2)}) collective-permute-start(bf16[3,256,128]{2,1,0:T(8,128)(2,1)S(1)} %add_convert_fusion), channel_id=1, source_target_pairs={{0,3},{1,2},{2,1},{3,0},{4,5},{5,4},{6,7},{7,6},{8,11},{9,10},{10,... | collective-permute-start | bytes 589832 | tf_op jit(solution)/shard_map/ppermute | solution.py:201
  65.4 2.9 %collective-permute-start.5 = (bf16[3,256,128]{2,1,0:T(8,128)(2,1)S(1)}, bf16[3,256,128]{2,1,0:T(8,128)(2,1)S(1)}, u32[]{:S(2)}, u32[]{:S(2)}) collective-permute-start(bf16[3,256,128]{2,1,0:T(8,128)(2,1)S(1)} %get-tuple-element.26), channel_id=1, source_target_pairs={{0,1},{1,0},{2,3},{3,2},{4,7},{5,6},{6,5},{7,4},{8,9},{9,8},{10,11... | collective-permute-start | bytes 589832 | tf_op jit(solution)/shard_map/ppermute | solution.py:204
  68.3 1.5 %collective-permute-done.7.other = bf16[3,256,128]{2,1,0:T(8,128)(2,1)S(1)} collective-permute-done((bf16[3,256,128]{2,1,0:T(8,128)(2,1)S(1)}, bf16[3,256,128]{2,1,0:T(8,128)(2,1)S(1)}, u32[]{:S(2)}, u32[]{:S(2)}) %collective-permute-start.7) | collective-permute-done | bytes 196640 | tf_op jit(solution)/shard_map/ppermute | solution.py:201
  69.9 4.0 %collective-permute-done.5.pair = bf16[3,256,128]{2,1,0:T(8,128)(2,1)S(1)} collective-permute-done((bf16[3,256,128]{2,1,0:T(8,128)(2,1)S(1)}, bf16[3,256,128]{2,1,0:T(8,128)(2,1)S(1)}, u32[]{:S(2)}, u32[]{:S(2)}) %collective-permute-start.5) | collective-permute-done | bytes 196640 | tf_op jit(solution)/shard_map/ppermute | solution.py:204
  73.8 0.3 all-to-all-done.1.got
  74.1 0.7 spread.3
  74.8 3.9 %all-to-all-start.2 = ((bf16[32,16,128]{2,1,0:T(8,128)(2,1)}), bf16[32,16,128]{2,1,0:T(8,128)(2,1)S(1)}, u32[]{:S(2)}, u32[]{:S(2)}) async-start(bf16[32,16,128]{2,1,0:T(8,128)(2,1)} %spread.3), calls=%async_computation.2 | async-start | bytes 262144 | tf_op jit(solution)/shard_map/all_to_all | solution.py:217
  78.7 0.0 copy-done.1
  78.7 1.2 %feature_grad.1 = f32[384,256]{1,0:T(8,128)} custom-call(f32[3,256,128]{2,1,0:T(8,128)S(1)} %get-tuple-element.22.keep, bf16[3,256,128]{2,1,0:T(8,128)(2,1)S(1)} %collective-permute-done.5.pair, bf16[3,256,128]{2,1,0:T(8,128)(2,1)S(1)} %collective-permute-done.7.other, bf16[256,256]{1,0:T(8,128)(2,1)S(1)} %copy-done.1), custom_call_target="tpu_custom_call" | custom-call | tf_op jit(solution)/shard_map/feature_grad/pallas_call | solution.py:208
  79.9 8.0 %all-to-all-done.2 = bf16[32,16,128]{2,1,0:T(8,128)(2,1)S(1)} async-done(((bf16[32,16,128]{2,1,0:T(8,128)(2,1)}), bf16[32,16,128]{2,1,0:T(8,128)(2,1)S(1)}, u32[]{:S(2)}, u32[]{:S(2)}) %all-to-all-start.2) | async-done | bytes 131104 | tf_op jit(solution)/shard_map/all_to_all | solution.py:217
  87.8 0.7 convert_bitcast_fusion
  (1 shorter events, 0.0 us)
Async XLA Ops:
  0.6 20.3 %copy-start = (bf16[384,256]{1,0:T(8,128)(2,1)S(1)}, bf16[384,256]{1,0:T(8,128)(2,1)}, u32[]{:S(2)}) copy-start(bf16[384,256]{1,0:T(8,128)(2,1)} %feat0.1) | copy-start | bytes 589828
  0.6 13.0 %collective-permute-start.1 = (bf16[384,256]{1,0:T(8,128)(2,1)}, bf16[384,256]{1,0:T(8,128)(2,1)S(1)}, u32[]{:S(2)}, u32[]{:S(2)}) collective-permute-start(bf16[384,256]{1,0:T(8,128)(2,1)} %feat0.1), channel_id=1, source_target_pairs={{0,1},{1,0},{2,3},{3,2},{4,7},{5,6},{6,5},{7,4},{8,9},{9,8},{10,11... | collective-permute-start | bytes 589832 | tf_op jit(solution)/shard_map/ppermute | solution.py:176
  9.4 21.4 %collective-permute-start = (bf16[12,256,128]{2,1,0:T(8,128)(2,1)S(1)}, bf16[12,256,128]{2,1,0:T(8,128)(2,1)S(1)}, u32[]{:S(2)}, u32[]{:S(2)}) collective-permute-start(bf16[12,256,128]{2,1,0:T(8,128)(2,1)S(1)} %get-tuple-element.18), channel_id=1, source_target_pairs={{4,8},{12,16},{20,24},{28,32},{36,40},{44,48},{52,56},{60,64},{68,... | collective-permute-start | bytes 2359304 | tf_op jit(solution)/shard_map/ppermute | solution.py:139
  13.6 17.2 %collective-permute-start.2 = (bf16[12,256,128]{2,1,0:T(8,128)(2,1)S(1)}, bf16[12,256,128]{2,1,0:T(8,128)(2,1)S(1)}, u32[]{:S(2)}, u32[]{:S(2)}) collective-permute-start(bf16[12,256,128]{2,1,0:T(8,128)(2,1)S(1)} %get-tuple-element.20), channel_id=1, source_target_pairs={{0,4},{4,0},{1,5},{5,1},{2,6},{6,2},{3,7},{7,3},{8,12},{12,8},{9,1... | collective-permute-start | bytes 2359304 | tf_op jit(solution)/shard_map/ppermute | solution.py:139
  21.0 6.7 %collective-permute-start.4 = (bf16[384,256]{1,0:T(8,128)(2,1)S(1)}, bf16[384,256]{1,0:T(8,128)(2,1)S(1)}, u32[]{:S(2)}, u32[]{:S(2)}) collective-permute-start(bf16[384,256]{1,0:T(8,128)(2,1)S(1)} %copy-done), channel_id=1, source_target_pairs={{0,3},{1,2},{2,1},{3,0},{4,5},{5,4},{6,7},{7,6},{8,11},{9,10},{10,... | collective-permute-start | bytes 589832 | tf_op jit(solution)/shard_map/ppermute | solution.py:180
  24.1 6.7 %collective-permute-start.3 = (bf16[384,256]{1,0:T(8,128)(2,1)S(1)}, bf16[384,256]{1,0:T(8,128)(2,1)S(1)}, u32[]{:S(2)}, u32[]{:S(2)}) collective-permute-start(bf16[384,256]{1,0:T(8,128)(2,1)S(1)} %collective-permute-done.1.feat1), channel_id=1, source_target_pairs={{0,3},{1,2},{2,1},{3,0},{4,5},{5,4},{6,7},{7,6},{8,11},{9,10},{10,... | collective-permute-start | bytes 589832 | tf_op jit(solution)/shard_map/ppermute | solution.py:181
  30.9 47.8 %copy-start.1 = (bf16[256,256]{1,0:T(8,128)(2,1)S(1)}, bf16[256,256]{1,0:T(8,128)(2,1)}, u32[]{:S(2)}) copy-start(bf16[256,256]{1,0:T(8,128)(2,1)} %weight.1) | copy-start | bytes 393220
  32.2 21.9 %all-to-all-start = ((bf16[32,16,128]{2,1,0:T(8,128)(2,1)}), bf16[32,16,128]{2,1,0:T(8,128)(2,1)S(1)}, u32[]{:S(2)}, u32[]{:S(2)}) async-start(bf16[32,16,128]{2,1,0:T(8,128)(2,1)} %get-tuple-element.23), calls=%async_computation | async-start | bytes 262144 | tf_op jit(solution)/shard_map/all_to_all | solution.py:202
  45.0 18.1 %collective-permute-start.6 = (bf16[3,256,128]{2,1,0:T(8,128)(2,1)S(1)}, bf16[3,256,128]{2,1,0:T(8,128)(2,1)S(1)}, u32[]{:S(2)}, u32[]{:S(2)}) collective-permute-start(bf16[3,256,128]{2,1,0:T(8,128)(2,1)S(1)} %get-tuple-element.28), channel_id=1, source_target_pairs={{0,1},{1,0},{2,3},{3,2},{4,7},{5,6},{6,5},{7,4},{8,9},{9,8},{10,11... | collective-permute-start | bytes 589832 | tf_op jit(solution)/shard_map/ppermute | solution.py:199
  54.8 19.3 %all-to-all-start.1 = ((bf16[24,16,128]{2,1,0:T(8,128)(2,1)}), bf16[24,16,128]{2,1,0:T(8,128)(2,1)S(1)}, u32[]{:S(2)}, u32[]{:S(2)}) async-start(bf16[24,16,128]{2,1,0:T(8,128)(2,1)} %spread.2), calls=%async_computation.1 | async-start | bytes 196608 | tf_op jit(solution)/shard_map/all_to_all | solution.py:206
  63.1 6.7 %collective-permute-start.7 = (bf16[3,256,128]{2,1,0:T(8,128)(2,1)S(1)}, bf16[3,256,128]{2,1,0:T(8,128)(2,1)S(1)}, u32[]{:S(2)}, u32[]{:S(2)}) collective-permute-start(bf16[3,256,128]{2,1,0:T(8,128)(2,1)S(1)} %add_convert_fusion), channel_id=1, source_target_pairs={{0,3},{1,2},{2,1},{3,0},{4,5},{5,4},{6,7},{7,6},{8,11},{9,10},{10,... | collective-permute-start | bytes 589832 | tf_op jit(solution)/shard_map/ppermute | solution.py:201
  65.4 8.4 %collective-permute-start.5 = (bf16[3,256,128]{2,1,0:T(8,128)(2,1)S(1)}, bf16[3,256,128]{2,1,0:T(8,128)(2,1)S(1)}, u32[]{:S(2)}, u32[]{:S(2)}) collective-permute-start(bf16[3,256,128]{2,1,0:T(8,128)(2,1)S(1)} %get-tuple-element.26), channel_id=1, source_target_pairs={{0,1},{1,0},{2,3},{3,2},{4,7},{5,6},{6,5},{7,4},{8,9},{9,8},{10,11... | collective-permute-start | bytes 589832 | tf_op jit(solution)/shard_map/ppermute | solution.py:204
  74.8 13.0 %all-to-all-start.2 = ((bf16[32,16,128]{2,1,0:T(8,128)(2,1)}), bf16[32,16,128]{2,1,0:T(8,128)(2,1)S(1)}, u32[]{:S(2)}, u32[]{:S(2)}) async-start(bf16[32,16,128]{2,1,0:T(8,128)(2,1)} %spread.3), calls=%async_computation.2 | async-start | bytes 262144 | tf_op jit(solution)/shard_map/all_to_all | solution.py:217

commit v9 on v7

--- a/solution.py
+++ b/solution.py
@@ -66,10 +66,10 @@
     return high, (value - high.astype(jnp.float32)).astype(jnp.bfloat16)
 
 
-def weight_kernel(own, cross, chip, feat0, feat1, feat32, give, keep0, keep3, term):
+def weight_kernel(own, cross, chip, feat0, feat1, feat2, feat3, give, keep0, keep3, term):
     blocks, channels, edge = keep0.shape
     held = []
-    for k, (feat, at) in enumerate(((feat0, 0), (feat1, 0), (feat32, blocks), (feat32, 0))):
+    for k, feat in enumerate((feat0, feat1, feat2, feat3)):
         for b in range(blocks):
             i = k * blocks + b
             g = own[i] + cross[i].astype(jnp.float32) + chip[i].astype(jnp.float32)
@@ -79,7 +79,7 @@
                 keep3[b] = g
             else:
                 give[(k - 1) * blocks + b] = g.astype(jnp.bfloat16)
-            held.append((g, feat, (at + b) * edge))
+            held.append((g, feat, b * edge))
     acc = None
     for (g, feat, at), (g2, feat2, at2) in zip(held[::2], held[1::2]):
         rows = jnp.concatenate([feat[pl.ds(at, edge), :], feat2[pl.ds(at2, edge), :]], axis=0)
@@ -174,10 +174,10 @@
     )(tile_counts, *held)
     near, far = hops(x, (1, 3)), hops(x, (3, 1))
     feat1 = lax.ppermute(features, ("core", "x"), near)
-    chip, feat1 = lax.optimization_barrier((chip, feat1))
     from_cross = swap(cross, ("y", "z", "core"), rows, 1)
     from_chip = swap(chip, "core", 2, 0)
-    feat32 = lax.ppermute(jnp.concatenate([features, feat1], axis=0), ("core", "x"), far)
+    feat3 = lax.ppermute(features, ("core", "x"), far)
+    feat2 = lax.ppermute(feat1, ("core", "x"), far)
     halves = channels // edge
     height = channels // (x * y)
     third = (blocks, channels, edge)
@@ -189,11 +189,11 @@
             jax.ShapeDtypeStruct(third, jnp.float32),
             jax.ShapeDtypeStruct((x * y, halves * height, edge), jnp.bfloat16),
         ),
-        in_specs=[VMEM] * 6,
+        in_specs=[VMEM] * 7,
         out_specs=(VMEM,) * 4,
         compiler_params=params,
         name="weight_term",
-    )(own, from_cross, from_chip, features, feat1, feat32)
+    )(own, from_cross, from_chip, features, feat1, feat2, feat3)
     from_near = lax.ppermute(give, ("core", "x"), near)
     onward = (keep3 + from_near[blocks:].astype(jnp.float32)).astype(jnp.bfloat16)
     from_far = lax.ppermute(onward, ("core", "x"), far)

time: 87.9 us -> 91.3 us (1.039)
  starting transfers between devices: 43 us -> 44.4 us
  waiting for transfers between devices: 16.5 us -> 17.8 us
    ppermute x1, waiting for transfers between devices: 0.01 us -> 3.77 us  [local(): feat1 = lax.ppermute(features, ('core', 'x'), near)]
    ppermute x1, starting transfers between devices: 5.35 us -> 1.92 us  [local(): feat1 = lax.ppermute(features, ('core', 'x'), near)]
    ppermute x1 -> x2, waiting for transfers between devices: 6.83 us -> 4.48 us  [the longest x1 4.48 us: local(): feat2 = lax.ppermute(feat1, ('core', 'x'), far)]
    ppermute x1 -> x2, starting transfers between devices: 1.98 us -> 3.83 us  [the longest x1 1.92 us: local(): feat3 = lax.ppermute(features, ('core', 'x'), far)]
    ppermute x2, starting transfers between devices: 11.5 us -> 13.1 us  [swap(): return lax.ppermute(array, axes, pairs + [(j, i) for i, j in pairs])]
    all_to_all x1, starting transfers between devices: 12.8 us -> 14.2 us  [local(): got = lax.all_to_all(term, ('x', 'y'), 0, 0)]
  transfers between devices with their start and end apart: 8 -> 9, of which waited for: 4 -> 5; matrix products, arithmetic and copies ran while one was open for 0% -> 0% of each run, Pallas kernels for 5% -> 2%
where the time goes in v9:
time: 91.3 us; the launch traced here: 90.2 us
  starting transfers between devices  44.4 us (49%)
  blocking collectives  19.7 us (22%)
  waiting for transfers between devices  17.8 us (19%)
  Pallas kernels  6.04 us (7%)
  between operations  1.44 us (2%)
    all_to_all x1, blocking collectives, local(): got = lax.all_to_all(copies, ('z', 'core'), 0, 0)  19.7 us
    all_to_all x1, starting transfers between devices, local(): got = lax.all_to_all(term, ('x', 'y'), 0, 0)  14.2 us
    ppermute x2, starting transfers between devices, swap(): return lax.ppermute(array, axes, pairs + [(j, i) for i, j in pairs])  13.1 us
    all_to_all x1, waiting for transfers between devices, local(): got = lax.all_to_all(term, ('x', 'y'), 0, 0)  4.75 us
    ppermute x1, waiting for transfers between devices, local(): feat2 = lax.ppermute(feat1, ('core', 'x'), far)  4.48 us
    ppermute x1, starting transfers between devices, local(): from_near = lax.ppermute(give, ('core', 'x'), near)  4.39 us
    ppermute x1, waiting for transfers between devices, local(): from_far = lax.ppermute(onward, ('core', 'x'), far)  4.33 us
    all_to_all x1, starting transfers between devices, local(): pieces = lax.all_to_all(copies, ('x', 'y'), 0, 0).astype(jnp.float32)  3.86 us
  transfers between devices with their start and end apart: 9, of which 5 were waited for; matrix products, arithmetic and copies ran while one was open for 0% of the time, Pallas kernels for 2%

profile of v9, /device:TPU:1, one launch (start us, length us, event | category | flops | bytes accessed | tf_op | source)
XLA Modules:
  0.0 90.2 jit_solution(6337852053249934330)
XLA Ops:
  0.6 0.0 copy-start
  1.3 2.8 %tile_sums.1 = (bf16[12,256,128]{2,1,0:T(8,128)(2,1)S(1)}, bf16[12,256,128]{2,1,0:T(8,128)(2,1)S(1)}, f32[12,256,128]{2,1,0:T(8,128)S(1)}) custom-call(s32[1]{0:T(128)S(6)} %copy.9.count, s32[3,72]{1,0:T(4,128)} %bitcast.8, bf16[384,256]{1,0:T(8,128)(2,1)} %pre_hbm.1, f32[384,256]{1,0:T(8,128)} %up_hbm.1, bf16[72,128,128]{2,1,0:T(8,128)(2,1)} %tiles_hbm.1), custom_call_target="tpu_custom_call" | custom-call | tf_op jit(solution)/shard_map/tile_sums/pallas_call | solution.py:154
  4.1 5.4 %collective-permute-start = (bf16[12,256,128]{2,1,0:T(8,128)(2,1)S(1)}, bf16[12,256,128]{2,1,0:T(8,128)(2,1)S(1)}, u32[]{:S(2)}, u32[]{:S(2)}) collective-permute-start(bf16[12,256,128]{2,1,0:T(8,128)(2,1)S(1)} %get-tuple-element.10), channel_id=1, source_target_pairs={{4,8},{12,16},{20,24},{28,32},{36,40},{44,48},{52,56},{60,64},{68,... | collective-permute-start | bytes 2359304 | tf_op jit(solution)/shard_map/ppermute | solution.py:139
  9.5 7.7 %collective-permute-start.1 = (bf16[12,256,128]{2,1,0:T(8,128)(2,1)S(1)}, bf16[12,256,128]{2,1,0:T(8,128)(2,1)S(1)}, u32[]{:S(2)}, u32[]{:S(2)}) collective-permute-start(bf16[12,256,128]{2,1,0:T(8,128)(2,1)S(1)} %get-tuple-element.11), channel_id=1, source_target_pairs={{0,4},{4,0},{1,5},{5,1},{2,6},{6,2},{3,7},{7,3},{8,12},{12,8},{9,1... | collective-permute-start | bytes 2359304 | tf_op jit(solution)/shard_map/ppermute | solution.py:139
  17.3 0.0 copy-done
  17.3 1.9 %collective-permute-start.2 = (bf16[384,256]{1,0:T(8,128)(2,1)S(1)}, bf16[384,256]{1,0:T(8,128)(2,1)S(1)}, u32[]{:S(2)}, u32[]{:S(2)}) collective-permute-start(bf16[384,256]{1,0:T(8,128)(2,1)S(1)} %copy-done), channel_id=1, source_target_pairs={{0,1},{1,0},{2,3},{3,2},{4,7},{5,6},{6,5},{7,4},{8,9},{9,8},{10,11... | collective-permute-start | bytes 589832 | tf_op jit(solution)/shard_map/ppermute | solution.py:176
  19.2 1.9 %collective-permute-start.4 = (bf16[384,256]{1,0:T(8,128)(2,1)S(1)}, bf16[384,256]{1,0:T(8,128)(2,1)S(1)}, u32[]{:S(2)}, u32[]{:S(2)}) collective-permute-start(bf16[384,256]{1,0:T(8,128)(2,1)S(1)} %copy-done), channel_id=1, source_target_pairs={{0,3},{1,2},{2,1},{3,0},{4,5},{5,4},{6,7},{7,6},{8,11},{9,10},{10,... | collective-permute-start | bytes 589832 | tf_op jit(solution)/shard_map/ppermute | solution.py:179
  21.1 3.8 %collective-permute-done.2.feat1 = bf16[384,256]{1,0:T(8,128)(2,1)S(1)} collective-permute-done((bf16[384,256]{1,0:T(8,128)(2,1)S(1)}, bf16[384,256]{1,0:T(8,128)(2,1)S(1)}, u32[]{:S(2)}, u32[]{:S(2)}) %collective-permute-start.2) | collective-permute-done | bytes 196640 | tf_op jit(solution)/shard_map/ppermute | solution.py:176
  24.9 1.9 %collective-permute-start.3 = (bf16[384,256]{1,0:T(8,128)(2,1)S(1)}, bf16[384,256]{1,0:T(8,128)(2,1)S(1)}, u32[]{:S(2)}, u32[]{:S(2)}) collective-permute-start(bf16[384,256]{1,0:T(8,128)(2,1)S(1)} %collective-permute-done.2.feat1), channel_id=1, source_target_pairs={{0,3},{1,2},{2,1},{3,0},{4,5},{5,4},{6,7},{7,6},{8,11},{9,10},{10,... | collective-permute-start | bytes 589832 | tf_op jit(solution)/shard_map/ppermute | solution.py:180
  26.8 0.0 collective-permute-done.4.feat3
  26.8 4.5 %collective-permute-done.3.feat2 = bf16[384,256]{1,0:T(8,128)(2,1)S(1)} collective-permute-done((bf16[384,256]{1,0:T(8,128)(2,1)S(1)}, bf16[384,256]{1,0:T(8,128)(2,1)S(1)}, u32[]{:S(2)}, u32[]{:S(2)}) %collective-permute-start.3) | collective-permute-done | bytes 196640 | tf_op jit(solution)/shard_map/ppermute | solution.py:180
  31.3 0.0 collective-permute-done.cross
  31.3 0.0 collective-permute-done.1.chip
  31.3 0.0 copy-start.1
  31.3 1.4 %weight_term.1 = (bf16[6,256,128]{2,1,0:T(8,128)(2,1)S(1)}, f32[3,256,128]{2,1,0:T(8,128)S(1)}, f32[3,256,128]{2,1,0:T(8,128)S(1)}, bf16[32,16,128]{2,1,0:T(8,128)(2,1)}) custom-call(f32[12,256,128]{2,1,0:T(8,128)S(1)} %get-tuple-element.9.own, bf16[12,256,128]{2,1,0:T(8,128)(2,1)S(1)} %collective-permute-done.cross, ...), custom_call_target="tpu_custom_call" | custom-call | tf_op jit(solution)/shard_map/weight_term/pallas_call | solution.py:184
  32.7 14.2 %all-to-all-start = ((bf16[32,16,128]{2,1,0:T(8,128)(2,1)}), bf16[32,16,128]{2,1,0:T(8,128)(2,1)S(1)}, u32[]{:S(2)}, u32[]{:S(2)}) async-start(bf16[32,16,128]{2,1,0:T(8,128)(2,1)} %get-tuple-element.15), calls=%async_computation | async-start | bytes 262144 | tf_op jit(solution)/shard_map/all_to_all | solution.py:208
  46.9 4.4 %collective-permute-start.5 = (bf16[6,256,128]{2,1,0:T(8,128)(2,1)S(1)}, bf16[6,256,128]{2,1,0:T(8,128)(2,1)S(1)}, u32[]{:S(2)}, u32[]{:S(2)}) collective-permute-start(bf16[6,256,128]{2,1,0:T(8,128)(2,1)S(1)} %get-tuple-element.13), channel_id=1, source_target_pairs={{0,1},{1,0},{2,3},{3,2},{4,7},{5,6},{6,5},{7,4},{8,9},{9,8},{10,11... | collective-permute-start | bytes 1179656 | tf_op jit(solution)/shard_map/ppermute | solution.py:197
  51.3 4.7 %all-to-all-done.got = bf16[32,16,128]{2,1,0:T(8,128)(2,1)S(1)} async-done(((bf16[32,16,128]{2,1,0:T(8,128)(2,1)}), bf16[32,16,128]{2,1,0:T(8,128)(2,1)S(1)}, u32[]{:S(2)}, u32[]{:S(2)}) %all-to-all-start) | async-done | bytes 131104 | tf_op jit(solution)/shard_map/all_to_all | solution.py:208
  56.1 19.7 %all_to_all.15.got = bf16[24,16,128]{2,1,0:T(8,128)(2,1)S(1)} all-to-all(bf16[24,16,128]{2,1,0:T(8,128)(2,1)S(1)} %spread.2), channel_id=1, replica_groups=mesh['y'=8,'z'=12,'core'=2,'x'=4] {'z','core'}, dimensions={0} | all-to-all | bytes 196608 | tf_op jit(solution)/shard_map/all_to_all | solution.py:210
  75.8 0.7 spread.3
  76.5 3.9 %all-to-all-start.2 = ((bf16[32,16,128]{2,1,0:T(8,128)(2,1)}), bf16[32,16,128]{2,1,0:T(8,128)(2,1)S(1)}, u32[]{:S(2)}, u32[]{:S(2)}) async-start(bf16[32,16,128]{2,1,0:T(8,128)(2,1)} %spread.3), calls=%async_computation.2 | async-start | bytes 262144 | tf_op jit(solution)/shard_map/all_to_all | solution.py:212
  80.3 0.0 collective-permute-done.5.pair
  80.4 3.1 %collective-permute-start.6 = (bf16[3,256,128]{2,1,0:T(8,128)(2,1)S(1)}, bf16[3,256,128]{2,1,0:T(8,128)(2,1)S(1)}, u32[]{:S(2)}, u32[]{:S(2)}) collective-permute-start(bf16[3,256,128]{2,1,0:T(8,128)(2,1)S(1)} %add_convert_fusion), channel_id=1, source_target_pairs={{0,3},{1,2},{2,1},{3,0},{4,5},{5,4},{6,7},{7,6},{8,11},{9,10},{10,... | collective-permute-start | bytes 589832 | tf_op jit(solution)/shard_map/ppermute | solution.py:199
  83.5 4.3 %collective-permute-done.6.other = bf16[3,256,128]{2,1,0:T(8,128)(2,1)S(1)} collective-permute-done((bf16[3,256,128]{2,1,0:T(8,128)(2,1)S(1)}, bf16[3,256,128]{2,1,0:T(8,128)(2,1)S(1)}, u32[]{:S(2)}, u32[]{:S(2)}) %collective-permute-start.6) | collective-permute-done | bytes 196640 | tf_op jit(solution)/shard_map/ppermute | solution.py:199
  87.8 0.0 copy-done.1
  87.8 1.2 %feature_grad.1 = f32[384,256]{1,0:T(8,128)} custom-call(f32[3,256,128]{2,1,0:T(8,128)S(1)} %get-tuple-element.12.keep, bf16[6,256,128]{2,1,0:T(8,128)(2,1)S(1)} %collective-permute-done.5.pair, bf16[3,256,128]{2,1,0:T(8,128)(2,1)S(1)} %collective-permute-done.6.other, bf16[256,256]{1,0:T(8,128)(2,1)S(1)} %copy-done.1), custom_call_target="tpu_custom_call" | custom-call | tf_op jit(solution)/shard_map/feature_grad/pallas_call | solution.py:200
  89.0 0.5 all-to-all-done.2
  89.5 0.7 convert_bitcast_fusion
  (2 shorter events, 0.1 us)
Async XLA Ops:
  0.6 16.6 %copy-start = (bf16[384,256]{1,0:T(8,128)(2,1)S(1)}, bf16[384,256]{1,0:T(8,128)(2,1)}, u32[]{:S(2)}) copy-start(bf16[384,256]{1,0:T(8,128)(2,1)} %feat0.1) | copy-start | bytes 589828
  4.1 27.2 %collective-permute-start = (bf16[12,256,128]{2,1,0:T(8,128)(2,1)S(1)}, bf16[12,256,128]{2,1,0:T(8,128)(2,1)S(1)}, u32[]{:S(2)}, u32[]{:S(2)}) collective-permute-start(bf16[12,256,128]{2,1,0:T(8,128)(2,1)S(1)} %get-tuple-element.10), channel_id=1, source_target_pairs={{4,8},{12,16},{20,24},{28,32},{36,40},{44,48},{52,56},{60,64},{68,... | collective-permute-start | bytes 2359304 | tf_op jit(solution)/shard_map/ppermute | solution.py:139
  9.5 21.8 %collective-permute-start.1 = (bf16[12,256,128]{2,1,0:T(8,128)(2,1)S(1)}, bf16[12,256,128]{2,1,0:T(8,128)(2,1)S(1)}, u32[]{:S(2)}, u32[]{:S(2)}) collective-permute-start(bf16[12,256,128]{2,1,0:T(8,128)(2,1)S(1)} %get-tuple-element.11), channel_id=1, source_target_pairs={{0,4},{4,0},{1,5},{5,1},{2,6},{6,2},{3,7},{7,3},{8,12},{12,8},{9,1... | collective-permute-start | bytes 2359304 | tf_op jit(solution)/shard_map/ppermute | solution.py:139
  17.3 7.6 %collective-permute-start.2 = (bf16[384,256]{1,0:T(8,128)(2,1)S(1)}, bf16[384,256]{1,0:T(8,128)(2,1)S(1)}, u32[]{:S(2)}, u32[]{:S(2)}) collective-permute-start(bf16[384,256]{1,0:T(8,128)(2,1)S(1)} %copy-done), channel_id=1, source_target_pairs={{0,1},{1,0},{2,3},{3,2},{4,7},{5,6},{6,5},{7,4},{8,9},{9,8},{10,11... | collective-permute-start | bytes 589832 | tf_op jit(solution)/shard_map/ppermute | solution.py:176
  19.2 7.6 %collective-permute-start.4 = (bf16[384,256]{1,0:T(8,128)(2,1)S(1)}, bf16[384,256]{1,0:T(8,128)(2,1)S(1)}, u32[]{:S(2)}, u32[]{:S(2)}) collective-permute-start(bf16[384,256]{1,0:T(8,128)(2,1)S(1)} %copy-done), channel_id=1, source_target_pairs={{0,3},{1,2},{2,1},{3,0},{4,5},{5,4},{6,7},{7,6},{8,11},{9,10},{10,... | collective-permute-start | bytes 589832 | tf_op jit(solution)/shard_map/ppermute | solution.py:179
  24.9 6.4 %collective-permute-start.3 = (bf16[384,256]{1,0:T(8,128)(2,1)S(1)}, bf16[384,256]{1,0:T(8,128)(2,1)S(1)}, u32[]{:S(2)}, u32[]{:S(2)}) collective-permute-start(bf16[384,256]{1,0:T(8,128)(2,1)S(1)} %collective-permute-done.2.feat1), channel_id=1, source_target_pairs={{0,3},{1,2},{2,1},{3,0},{4,5},{5,4},{6,7},{7,6},{8,11},{9,10},{10,... | collective-permute-start | bytes 589832 | tf_op jit(solution)/shard_map/ppermute | solution.py:180
  31.3 56.5 %copy-start.1 = (bf16[256,256]{1,0:T(8,128)(2,1)S(1)}, bf16[256,256]{1,0:T(8,128)(2,1)}, u32[]{:S(2)}) copy-start(bf16[256,256]{1,0:T(8,128)(2,1)} %weight.1) | copy-start | bytes 393220
  32.7 23.4 %all-to-all-start = ((bf16[32,16,128]{2,1,0:T(8,128)(2,1)}), bf16[32,16,128]{2,1,0:T(8,128)(2,1)S(1)}, u32[]{:S(2)}, u32[]{:S(2)}) async-start(bf16[32,16,128]{2,1,0:T(8,128)(2,1)} %get-tuple-element.15), calls=%async_computation | async-start | bytes 262144 | tf_op jit(solution)/shard_map/all_to_all | solution.py:208
  46.9 33.4 %collective-permute-start.5 = (bf16[6,256,128]{2,1,0:T(8,128)(2,1)S(1)}, bf16[6,256,128]{2,1,0:T(8,128)(2,1)S(1)}, u32[]{:S(2)}, u32[]{:S(2)}) collective-permute-start(bf16[6,256,128]{2,1,0:T(8,128)(2,1)S(1)} %get-tuple-element.13), channel_id=1, source_target_pairs={{0,1},{1,0},{2,3},{3,2},{4,7},{5,6},{6,5},{7,4},{8,9},{9,8},{10,11... | collective-permute-start | bytes 1179656 | tf_op jit(solution)/shard_map/ppermute | solution.py:197
  76.5 13.0 %all-to-all-start.2 = ((bf16[32,16,128]{2,1,0:T(8,128)(2,1)}), bf16[32,16,128]{2,1,0:T(8,128)(2,1)S(1)}, u32[]{:S(2)}, u32[]{:S(2)}) async-start(bf16[32,16,128]{2,1,0:T(8,128)(2,1)} %spread.3), calls=%async_computation.2 | async-start | bytes 262144 | tf_op jit(solution)/shard_map/all_to_all | solution.py:212
  80.4 7.4 %collective-permute-start.6 = (bf16[3,256,128]{2,1,0:T(8,128)(2,1)S(1)}, bf16[3,256,128]{2,1,0:T(8,128)(2,1)S(1)}, u32[]{:S(2)}, u32[]{:S(2)}) collective-permute-start(bf16[3,256,128]{2,1,0:T(8,128)(2,1)S(1)} %add_convert_fusion), channel_id=1, source_target_pairs={{0,3},{1,2},{2,1},{3,0},{4,5},{5,4},{6,7},{7,6},{8,11},{9,10},{10,... | collective-permute-start | bytes 589832 | tf_op jit(solution)/shard_map/ppermute | solution.py:199

commit v10 on v7

--- a/solution.py
+++ b/solution.py
@@ -97,24 +97,48 @@
         term[i] = jnp.concatenate(halves, axis=0).astype(term.dtype)
 
 
-def spread_kernel(scale, got, copies):
+def sum_kernel(scale, got, total):
     acc = got[0].astype(jnp.float32)
     for i in range(1, got.shape[0]):
         acc = acc + got[i].astype(jnp.float32)
-    value = (acc / scale).astype(copies.dtype)
-    for i in range(copies.shape[0]):
-        copies[i] = value
-
-
-def spread(got, count, scale):
+    total[...] = acc / scale
+
+
+def sum_of(got, scale):
     return pl.pallas_call(
-        functools.partial(spread_kernel, scale),
-        out_shape=jax.ShapeDtypeStruct((count,) + got.shape[1:], jnp.bfloat16),
+        functools.partial(sum_kernel, scale),
+        out_shape=jax.ShapeDtypeStruct(got.shape[1:], jnp.float32),
         in_specs=[VMEM],
         out_specs=VMEM,
         compiler_params=pltpu.CompilerParams(vmem_limit_bytes=16 << 20),
+        name="piece_sum",
+    )(got)
+
+
+def spread_kernel(got, copies):
+    acc = got[0].astype(jnp.float32)
+    for i in range(1, got.shape[0]):
+        acc = acc + got[i].astype(jnp.float32)
+    value = acc.astype(copies.dtype)
+    for i in range(copies.shape[0]):
+        copies[i] = value
+
+
+def spread_pair_kernel(mine, other, copies):
+    value = (mine[...] + other[...]).astype(copies.dtype)
+    for i in range(copies.shape[0]):
+        copies[i] = value
+
+
+def spread(kernel, count, shape, *parts):
+    return pl.pallas_call(
+        kernel,
+        out_shape=jax.ShapeDtypeStruct((count,) + shape, jnp.bfloat16),
+        in_specs=[VMEM] * len(parts),
+        out_specs=VMEM,
+        compiler_params=pltpu.CompilerParams(vmem_limit_bytes=16 << 20),
         name="spread",
-    )(got)
+    )(*parts)
 
 
 def feature_kernel(keep, pair, other, weight, grad):
@@ -206,9 +230,11 @@
         name="feature_grad",
     )(keep0, from_near, from_far, weight)
     got = lax.all_to_all(term, ("x", "y"), 0, 0)
-    copies = spread(got, 2 * z, math.sqrt(rows * x * rows_dev))
-    got = lax.all_to_all(copies, ("z", "core"), 0, 0)
-    copies = spread(got, x * y, 1.0)
+    mine = sum_of(got, math.sqrt(rows * x * rows_dev))
+    other = swap(mine, "core", 2, 0)
+    copies = spread(spread_pair_kernel, z, mine.shape, mine, other)
+    got = lax.all_to_all(copies, "z", 0, 0)
+    copies = spread(spread_kernel, x * y, mine.shape, got)
     pieces = lax.all_to_all(copies, ("x", "y"), 0, 0).astype(jnp.float32)
     pieces = pieces.reshape(x * y, halves, height, edge)
     grad_weight = pieces.transpose(0, 2, 1, 3).reshape(channels, channels)

time: 87.9 us -> 90 us (1.024)
  the two profiles are of different devices: /device:TPU:1 before, /device:TPU:8 now
where the time goes in v10:
time: 90 us; the launch traced here: 89.5 us
  starting transfers between devices  44.9 us (50%)
  waiting for transfers between devices  20.4 us (23%)
  blocking collectives  15.4 us (17%)
  Pallas kernels  6.61 us (7%)
  between operations  1.42 us (2%)
    ppermute x3, starting transfers between devices, swap(): return lax.ppermute(array, axes, pairs + [(j, i) for i, j in pairs])  18.2 us
    all_to_all x1, blocking collectives, local(): got = lax.all_to_all(copies, 'z', 0, 0)  15.4 us
    ppermute x1, waiting for transfers between devices, local(): lax.ppermute(jnp.concatenate([features, feat1], axis=0), ('core', 'x'), far)  8.49 us
    all_to_all x1, starting transfers between devices, local(): got = lax.all_to_all(term, ('x', 'y'), 0, 0)  8.21 us
    all_to_all x1, waiting for transfers between devices, local(): got = lax.all_to_all(term, ('x', 'y'), 0, 0)  6.29 us
    ppermute x1, starting transfers between devices, local(): from_far = lax.ppermute(onward, ('core', 'x'), far)  4.75 us
    all_to_all x1, starting transfers between devices, local(): pieces = lax.all_to_all(copies, ('x', 'y'), 0, 0).astype(jnp.float32)  4.49 us
    ppermute x1, waiting for transfers between devices, local(): from_far = lax.ppermute(onward, ('core', 'x'), far)  4.44 us
  transfers between devices with their start and end apart: 9, of which 4 were waited for; matrix products, arithmetic and copies ran while one was open for 0% of the time, Pallas kernels for 6%

profile of v10, /device:TPU:8, one launch (start us, length us, event | category | flops | bytes accessed | tf_op | source)
XLA Modules:
  0.0 89.5 jit_solution(4298754127164492919)
XLA Ops:
  0.6 0.0 copy-start
  0.6 3.5 %collective-permute-start.1 = (bf16[384,256]{1,0:T(8,128)(2,1)}, bf16[384,256]{1,0:T(8,128)(2,1)S(1)}, u32[]{:S(2)}, u32[]{:S(2)}) collective-permute-start(bf16[384,256]{1,0:T(8,128)(2,1)} %feat0.1), channel_id=1, source_target_pairs={{0,1},{1,0},{2,3},{3,2},{4,7},{5,6},{6,5},{7,4},{8,9},{9,8},{10,11... | collective-permute-start | bytes 589832 | tf_op jit(solution)/shard_map/ppermute | solution.py:200
  4.8 3.4 %tile_sums.1 = (bf16[12,256,128]{2,1,0:T(8,128)(2,1)S(1)}, bf16[12,256,128]{2,1,0:T(8,128)(2,1)S(1)}, f32[12,256,128]{2,1,0:T(8,128)S(1)}) custom-call(s32[1]{0:T(128)S(6)} %copy.9.count, s32[3,72]{1,0:T(4,128)} %bitcast.8, bf16[384,256]{1,0:T(8,128)(2,1)} %pre_hbm.1, f32[384,256]{1,0:T(8,128)} %up_hbm.1, bf16[72,128,128]{2,1,0:T(8,128)(2,1)} %tiles_hbm.1), custom_call_target="tpu_custom_call" | custom-call | tf_op jit(solution)/shard_map/tile_sums/pallas_call | solution.py:178
  8.2 14.3 %collective-permute-start = (bf16[12,256,128]{2,1,0:T(8,128)(2,1)S(1)}, bf16[12,256,128]{2,1,0:T(8,128)(2,1)S(1)}, u32[]{:S(2)}, u32[]{:S(2)}) collective-permute-start(bf16[12,256,128]{2,1,0:T(8,128)(2,1)S(1)} %get-tuple-element.12), channel_id=1, source_target_pairs={{4,8},{12,16},{20,24},{28,32},{36,40},{44,48},{52,56},{60,64},{68,... | collective-permute-start | bytes 2359304 | tf_op jit(solution)/shard_map/ppermute | solution.py:163
  22.5 0.0 collective-permute-done.1.feat1
  22.5 1.9 %collective-permute-start.2 = (bf16[12,256,128]{2,1,0:T(8,128)(2,1)S(1)}, bf16[12,256,128]{2,1,0:T(8,128)(2,1)S(1)}, u32[]{:S(2)}, u32[]{:S(2)}) collective-permute-start(bf16[12,256,128]{2,1,0:T(8,128)(2,1)S(1)} %get-tuple-element.14), channel_id=1, source_target_pairs={{0,4},{4,0},{1,5},{5,1},{2,6},{6,2},{3,7},{7,3},{8,12},{12,8},{9,1... | collective-permute-start | bytes 2359304 | tf_op jit(solution)/shard_map/ppermute | solution.py:163
  24.5 0.0 copy-done
  24.5 2.4 %collective-permute-start.3 = (bf16[768,256]{1,0:T(8,128)(2,1)S(1)}, bf16[768,256]{1,0:T(8,128)(2,1)S(1)}, u32[]{:S(2)}, u32[]{:S(2)}) collective-permute-start(bf16[768,256]{1,0:T(8,128)(2,1)S(1)} %pad_maximum_fusion), channel_id=1, source_target_pairs={{0,3},{1,2},{2,1},{3,0},{4,5},{5,4},{6,7},{7,6},{8,11},{9,10},{10,... | collective-permute-start | bytes 1179656 | tf_op jit(solution)/shard_map/ppermute | solution.py:204
  26.9 8.5 %collective-permute-done.3.feat32 = bf16[768,256]{1,0:T(8,128)(2,1)S(1)} collective-permute-done((bf16[768,256]{1,0:T(8,128)(2,1)S(1)}, bf16[768,256]{1,0:T(8,128)(2,1)S(1)}, u32[]{:S(2)}, u32[]{:S(2)}) %collective-permute-start.3) | collective-permute-done | bytes 393248 | tf_op jit(solution)/shard_map/ppermute | solution.py:204
  35.4 0.0 collective-permute-done.cross
  35.4 0.0 collective-permute-done.2.chip
  35.4 0.0 copy-start.1
  35.4 1.4 %weight_term.1 = (bf16[6,256,128]{2,1,0:T(8,128)(2,1)S(1)}, f32[3,256,128]{2,1,0:T(8,128)S(1)}, f32[3,256,128]{2,1,0:T(8,128)S(1)}, bf16[32,16,128]{2,1,0:T(8,128)(2,1)}) custom-call(f32[12,256,128]{2,1,0:T(8,128)S(1)} %get-tuple-element.11.own, bf16[12,256,128]{2,1,0:T(8,128)(2,1)S(1)} %collective-permute-done.cross, ...), custom_call_target="tpu_custom_call" | custom-call | tf_op jit(solution)/shard_map/weight_term/pallas_call | solution.py:208
  36.8 8.2 %all-to-all-start = ((bf16[32,16,128]{2,1,0:T(8,128)(2,1)}), bf16[32,16,128]{2,1,0:T(8,128)(2,1)S(1)}, u32[]{:S(2)}, u32[]{:S(2)}) async-start(bf16[32,16,128]{2,1,0:T(8,128)(2,1)} %get-tuple-element.19), calls=%async_computation | async-start | bytes 262144 | tf_op jit(solution)/shard_map/all_to_all | solution.py:232
  45.0 3.4 %collective-permute-start.4 = (bf16[6,256,128]{2,1,0:T(8,128)(2,1)S(1)}, bf16[6,256,128]{2,1,0:T(8,128)(2,1)S(1)}, u32[]{:S(2)}, u32[]{:S(2)}) collective-permute-start(bf16[6,256,128]{2,1,0:T(8,128)(2,1)S(1)} %get-tuple-element.17), channel_id=1, source_target_pairs={{0,1},{1,0},{2,3},{3,2},{4,7},{5,6},{6,5},{7,4},{8,9},{9,8},{10,11... | collective-permute-start | bytes 1179656 | tf_op jit(solution)/shard_map/ppermute | solution.py:221
  48.4 6.3 %all-to-all-done.got = bf16[32,16,128]{2,1,0:T(8,128)(2,1)S(1)} async-done(((bf16[32,16,128]{2,1,0:T(8,128)(2,1)}), bf16[32,16,128]{2,1,0:T(8,128)(2,1)S(1)}, u32[]{:S(2)}, u32[]{:S(2)}) %all-to-all-start) | async-done | bytes 131104 | tf_op jit(solution)/shard_map/all_to_all | solution.py:232
  54.7 1.9 %collective-permute-start.6 = (f32[16,128]{1,0:T(8,128)S(1)}, f32[16,128]{1,0:T(8,128)S(1)}, u32[]{:S(2)}, u32[]{:S(2)}) collective-permute-start(f32[16,128]{1,0:T(8,128)S(1)} %piece_sum.1.mine), channel_id=1, source_target_pairs={{0,4},{4,0},{1,5},{5,1},{2,6},{6,2},{3,7},{7,3},{8,12},{12,8},{9,1... | collective-permute-start | bytes 24584 | tf_op jit(solution)/shard_map/ppermute | solution.py:163
  56.6 1.1 %collective-permute-done.6.other = f32[16,128]{1,0:T(8,128)S(1)} collective-permute-done((f32[16,128]{1,0:T(8,128)S(1)}, f32[16,128]{1,0:T(8,128)S(1)}, u32[]{:S(2)}, u32[]{:S(2)}) %collective-permute-start.6) | collective-permute-done | bytes 8224 | tf_op jit(solution)/shard_map/ppermute | solution.py:163
  57.8 15.4 %all_to_all.15.got = bf16[12,16,128]{2,1,0:T(8,128)(2,1)S(1)} all-to-all(bf16[12,16,128]{2,1,0:T(8,128)(2,1)S(1)} %spread.2), channel_id=1, replica_groups=mesh['y'=8,'z'=12,'core'=2,'x'=4] {'z'}, dimensions={0} | all-to-all | bytes 98304 | tf_op jit(solution)/shard_map/all_to_all | solution.py:236
  73.2 0.7 spread.3
  73.9 4.5 %all-to-all-start.2 = ((bf16[32,16,128]{2,1,0:T(8,128)(2,1)}), bf16[32,16,128]{2,1,0:T(8,128)(2,1)S(1)}, u32[]{:S(2)}, u32[]{:S(2)}) async-start(bf16[32,16,128]{2,1,0:T(8,128)(2,1)} %spread.3), calls=%async_computation.2 | async-start | bytes 262144 | tf_op jit(solution)/shard_map/all_to_all | solution.py:238
  78.4 0.0 collective-permute-done.4.pair
  78.4 4.7 %collective-permute-start.5 = (bf16[3,256,128]{2,1,0:T(8,128)(2,1)S(1)}, bf16[3,256,128]{2,1,0:T(8,128)(2,1)S(1)}, u32[]{:S(2)}, u32[]{:S(2)}) collective-permute-start(bf16[3,256,128]{2,1,0:T(8,128)(2,1)S(1)} %add_convert_fusion), channel_id=1, source_target_pairs={{0,3},{1,2},{2,1},{3,0},{4,5},{5,4},{6,7},{7,6},{8,11},{9,10},{10,... | collective-permute-start | bytes 589832 | tf_op jit(solution)/shard_map/ppermute | solution.py:223
  83.2 4.4 %collective-permute-done.5.other = bf16[3,256,128]{2,1,0:T(8,128)(2,1)S(1)} collective-permute-done((bf16[3,256,128]{2,1,0:T(8,128)(2,1)S(1)}, bf16[3,256,128]{2,1,0:T(8,128)(2,1)S(1)}, u32[]{:S(2)}, u32[]{:S(2)}) %collective-permute-start.5) | collective-permute-done | bytes 196640 | tf_op jit(solution)/shard_map/ppermute | solution.py:223
  87.6 0.0 copy-done.1
  87.6 1.2 %feature_grad.1 = f32[384,256]{1,0:T(8,128)} custom-call(f32[3,256,128]{2,1,0:T(8,128)S(1)} %get-tuple-element.16.keep, bf16[6,256,128]{2,1,0:T(8,128)(2,1)S(1)} %collective-permute-done.4.pair, bf16[3,256,128]{2,1,0:T(8,128)(2,1)S(1)} %collective-permute-done.5.other, bf16[256,256]{1,0:T(8,128)(2,1)S(1)} %copy-done.1), custom_call_target="tpu_custom_call" | custom-call | tf_op jit(solution)/shard_map/feature_grad/pallas_call | solution.py:224
  88.8 0.0 all-to-all-done.2
  88.8 0.7 convert_bitcast_fusion
  (4 shorter events, 0.1 us)
Async XLA Ops:
  0.6 23.8 %copy-start = (bf16[384,256]{1,0:T(8,128)(2,1)S(1)}, bf16[384,256]{1,0:T(8,128)(2,1)}, u32[]{:S(2)}) copy-start(bf16[384,256]{1,0:T(8,128)(2,1)} %feat0.1) | copy-start | bytes 589828
  0.6 21.9 %collective-permute-start.1 = (bf16[384,256]{1,0:T(8,128)(2,1)}, bf16[384,256]{1,0:T(8,128)(2,1)S(1)}, u32[]{:S(2)}, u32[]{:S(2)}) collective-permute-start(bf16[384,256]{1,0:T(8,128)(2,1)} %feat0.1), channel_id=1, source_target_pairs={{0,1},{1,0},{2,3},{3,2},{4,7},{5,6},{6,5},{7,4},{8,9},{9,8},{10,11... | collective-permute-start | bytes 589832 | tf_op jit(solution)/shard_map/ppermute | solution.py:200
  8.2 27.2 %collective-permute-start = (bf16[12,256,128]{2,1,0:T(8,128)(2,1)S(1)}, bf16[12,256,128]{2,1,0:T(8,128)(2,1)S(1)}, u32[]{:S(2)}, u32[]{:S(2)}) collective-permute-start(bf16[12,256,128]{2,1,0:T(8,128)(2,1)S(1)} %get-tuple-element.12), channel_id=1, source_target_pairs={{4,8},{12,16},{20,24},{28,32},{36,40},{44,48},{52,56},{60,64},{68,... | collective-permute-start | bytes 2359304 | tf_op jit(solution)/shard_map/ppermute | solution.py:163
  22.5 12.9 %collective-permute-start.2 = (bf16[12,256,128]{2,1,0:T(8,128)(2,1)S(1)}, bf16[12,256,128]{2,1,0:T(8,128)(2,1)S(1)}, u32[]{:S(2)}, u32[]{:S(2)}) collective-permute-start(bf16[12,256,128]{2,1,0:T(8,128)(2,1)S(1)} %get-tuple-element.14), channel_id=1, source_target_pairs={{0,4},{4,0},{1,5},{5,1},{2,6},{6,2},{3,7},{7,3},{8,12},{12,8},{9,1... | collective-permute-start | bytes 2359304 | tf_op jit(solution)/shard_map/ppermute | solution.py:163
  24.5 10.9 %collective-permute-start.3 = (bf16[768,256]{1,0:T(8,128)(2,1)S(1)}, bf16[768,256]{1,0:T(8,128)(2,1)S(1)}, u32[]{:S(2)}, u32[]{:S(2)}) collective-permute-start(bf16[768,256]{1,0:T(8,128)(2,1)S(1)} %pad_maximum_fusion), channel_id=1, source_target_pairs={{0,3},{1,2},{2,1},{3,0},{4,5},{5,4},{6,7},{7,6},{8,11},{9,10},{10,... | collective-permute-start | bytes 1179656 | tf_op jit(solution)/shard_map/ppermute | solution.py:204
  35.4 52.2 %copy-start.1 = (bf16[256,256]{1,0:T(8,128)(2,1)S(1)}, bf16[256,256]{1,0:T(8,128)(2,1)}, u32[]{:S(2)}) copy-start(bf16[256,256]{1,0:T(8,128)(2,1)} %weight.1) | copy-start | bytes 393220
  36.8 17.9 %all-to-all-start = ((bf16[32,16,128]{2,1,0:T(8,128)(2,1)}), bf16[32,16,128]{2,1,0:T(8,128)(2,1)S(1)}, u32[]{:S(2)}, u32[]{:S(2)}) async-start(bf16[32,16,128]{2,1,0:T(8,128)(2,1)} %get-tuple-element.19), calls=%async_computation | async-start | bytes 262144 | tf_op jit(solution)/shard_map/all_to_all | solution.py:232
  45.0 33.4 %collective-permute-start.4 = (bf16[6,256,128]{2,1,0:T(8,128)(2,1)S(1)}, bf16[6,256,128]{2,1,0:T(8,128)(2,1)S(1)}, u32[]{:S(2)}, u32[]{:S(2)}) collective-permute-start(bf16[6,256,128]{2,1,0:T(8,128)(2,1)S(1)} %get-tuple-element.17), channel_id=1, source_target_pairs={{0,1},{1,0},{2,3},{3,2},{4,7},{5,6},{6,5},{7,4},{8,9},{9,8},{10,11... | collective-permute-start | bytes 1179656 | tf_op jit(solution)/shard_map/ppermute | solution.py:221
  54.7 3.1 %collective-permute-start.6 = (f32[16,128]{1,0:T(8,128)S(1)}, f32[16,128]{1,0:T(8,128)S(1)}, u32[]{:S(2)}, u32[]{:S(2)}) collective-permute-start(f32[16,128]{1,0:T(8,128)S(1)} %piece_sum.1.mine), channel_id=1, source_target_pairs={{0,4},{4,0},{1,5},{5,1},{2,6},{6,2},{3,7},{7,3},{8,12},{12,8},{9,1... | collective-permute-start | bytes 24584 | tf_op jit(solution)/shard_map/ppermute | solution.py:163
  73.9 14.9 %all-to-all-start.2 = ((bf16[32,16,128]{2,1,0:T(8,128)(2,1)}), bf16[32,16,128]{2,1,0:T(8,128)(2,1)S(1)}, u32[]{:S(2)}, u32[]{:S(2)}) async-start(bf16[32,16,128]{2,1,0:T(8,128)(2,1)} %spread.3), calls=%async_computation.2 | async-start | bytes 262144 | tf_op jit(solution)/shard_map/all_to_all | solution.py:238
  78.4 9.2 %collective-permute-start.5 = (bf16[3,256,128]{2,1,0:T(8,128)(2,1)S(1)}, bf16[3,256,128]{2,1,0:T(8,128)(2,1)S(1)}, u32[]{:S(2)}, u32[]{:S(2)}) collective-permute-start(bf16[3,256,128]{2,1,0:T(8,128)(2,1)S(1)} %add_convert_fusion), channel_id=1, source_target_pairs={{0,3},{1,2},{2,1},{3,0},{4,5},{5,4},{6,7},{7,6},{8,11},{9,10},{10,... | collective-permute-start | bytes 589832 | tf_op jit(solution)/shard_map/ppermute | solution.py:223

commit v11 on v8

--- a/solution.py
+++ b/solution.py
@@ -66,10 +66,10 @@
     return high, (value - high.astype(jnp.float32)).astype(jnp.bfloat16)
 
 
-def weight_kernel(own, cross, chip, feat0, feat1, feat2, feat3, give1, give2, keep0, keep3, term):
+def weight_kernel(own, cross, chip, feat0, feat1, feat32, give1, give2, keep0, keep3, term):
     blocks, channels, edge = keep0.shape
     held = []
-    for k, feat in enumerate((feat0, feat1, feat2, feat3)):
+    for k, (feat, at) in enumerate(((feat0, 0), (feat1, 0), (feat32, blocks), (feat32, 0))):
         for b in range(blocks):
             i = k * blocks + b
             g = own[i] + cross[i].astype(jnp.float32) + chip[i].astype(jnp.float32)
@@ -79,7 +79,7 @@
                 keep3[b] = g
             else:
                 (give1 if k == 1 else give2)[b] = g.astype(jnp.bfloat16)
-            held.append((g, feat, b * edge))
+            held.append((g, feat, (at + b) * edge))
     acc = None
     for (g, feat, at), (g2, feat2, at2) in zip(held[::2], held[1::2]):
         rows = jnp.concatenate([feat[pl.ds(at, edge), :], feat2[pl.ds(at2, edge), :]], axis=0)
@@ -177,8 +177,7 @@
     chip, feat1 = lax.optimization_barrier((chip, feat1))
     from_cross = swap(cross, ("y", "z", "core"), rows, 1)
     from_chip = swap(chip, "core", 2, 0)
-    feat3 = lax.ppermute(features, ("core", "x"), far)
-    feat2 = lax.ppermute(feat1, ("core", "x"), far)
+    feat32 = lax.ppermute(jnp.concatenate([features, feat1], axis=0), ("core", "x"), far)
     halves = channels // edge
     height = channels // (x * y)
     third = (blocks, channels, edge)
@@ -191,11 +190,11 @@
             jax.ShapeDtypeStruct(third, jnp.float32),
             jax.ShapeDtypeStruct((x * y, halves * height, edge), jnp.bfloat16),
         ),
-        in_specs=[VMEM] * 7,
+        in_specs=[VMEM] * 6,
         out_specs=(VMEM,) * 5,
         compiler_params=params,
         name="weight_term",
-    )(own, from_cross, from_chip, features, feat1, feat2, feat3)
+    )(own, from_cross, from_chip, features, feat1, feat32)
     passing = lax.ppermute(give2, ("core", "x"), near)
     onward = (keep3 + passing.astype(jnp.float32)).astype(jnp.bfloat16)
     from_far = lax.ppermute(onward, ("core", "x"), far)

time: 89.3 us -> 88.5 us (level)
  starting transfers between devices: 56.6 us -> 52.8 us
  waiting for transfers between devices: 23.1 us -> 25.4 us
    ppermute x2 -> x1, starting transfers between devices: 5.28 us -> 1.98 us  [local(): lax.ppermute(jnp.concatenate([features, feat1], axis=0), ('core', 'x'), far)]
    ppermute x2 -> x1, waiting for transfers between devices: 4.58 us -> 6.83 us  [local(): lax.ppermute(jnp.concatenate([features, feat1], axis=0), ('core', 'x'), far)]
  transfers between devices with their start and end apart: 11 -> 10, of which waited for: 7 -> 6; matrix products, arithmetic and copies ran while one was open for 0% -> 0% of each run, Pallas kernels for 5% -> 6%
where the time goes in v11:
time: 88.5 us; the launch traced here: 87.7 us
  starting transfers between devices  52.8 us (60%)
  waiting for transfers between devices  25.4 us (29%)
  Pallas kernels  7.27 us (8%)
  between operations  1.43 us (2%)
    all_to_all x1, starting transfers between devices, local(): got = lax.all_to_all(term, ('x', 'y'), 0, 0)  13.2 us
    ppermute x2, starting transfers between devices, swap(): return lax.ppermute(array, axes, pairs + [(j, i) for i, j in pairs])  10.9 us
    all_to_all x1, starting transfers between devices, local(): got = lax.all_to_all(copies, ('z', 'core'), 0, 0)  8.05 us
    all_to_all x1, waiting for transfers between devices, local(): pieces = lax.all_to_all(copies, ('x', 'y'), 0, 0).astype(jnp.float32)  7.98 us
    ppermute x1, waiting for transfers between devices, local(): lax.ppermute(jnp.concatenate([features, feat1], axis=0), ('core', 'x'), far)  6.83 us
    ppermute x1, starting transfers between devices, local(): feat1 = lax.ppermute(features, ('core', 'x'), near)  5.35 us
    all_to_all x1, waiting for transfers between devices, local(): got = lax.all_to_all(term, ('x', 'y'), 0, 0)  4.75 us
    ppermute x1, starting transfers between devices, local(): passing = lax.ppermute(give2, ('core', 'x'), near)  4.39 us
  transfers between devices with their start and end apart: 10, of which 6 were waited for; matrix products, arithmetic and copies ran while one was open for 0% of the time, Pallas kernels for 6%

profile of v11, /device:TPU:1, one launch (start us, length us, event | category | flops | bytes accessed | tf_op | source)
XLA Modules:
  0.0 87.7 jit_solution(5152843133715523610)
XLA Ops:
  0.6 0.0 copy-start
  0.6 5.3 %collective-permute-start.1 = (bf16[384,256]{1,0:T(8,128)(2,1)}, bf16[384,256]{1,0:T(8,128)(2,1)S(1)}, u32[]{:S(2)}, u32[]{:S(2)}) collective-permute-start(bf16[384,256]{1,0:T(8,128)(2,1)} %feat0.1), channel_id=1, source_target_pairs={{0,1},{1,0},{2,3},{3,2},{4,7},{5,6},{6,5},{7,4},{8,9},{9,8},{10,11... | collective-permute-start | bytes 589832 | tf_op jit(solution)/shard_map/ppermute | solution.py:176
  6.6 3.4 %tile_sums.1 = (bf16[12,256,128]{2,1,0:T(8,128)(2,1)S(1)}, bf16[12,256,128]{2,1,0:T(8,128)(2,1)S(1)}, f32[12,256,128]{2,1,0:T(8,128)S(1)}) custom-call(s32[1]{0:T(128)S(6)} %copy.9.count, s32[3,72]{1,0:T(4,128)} %bitcast.8, bf16[384,256]{1,0:T(8,128)(2,1)} %pre_hbm.1, f32[384,256]{1,0:T(8,128)} %up_hbm.1, bf16[72,128,128]{2,1,0:T(8,128)(2,1)} %tiles_hbm.1), custom_call_target="tpu_custom_call" | custom-call | tf_op jit(solution)/shard_map/tile_sums/pallas_call | solution.py:154
  10.0 3.0 %collective-permute-start = (bf16[12,256,128]{2,1,0:T(8,128)(2,1)S(1)}, bf16[12,256,128]{2,1,0:T(8,128)(2,1)S(1)}, u32[]{:S(2)}, u32[]{:S(2)}) collective-permute-start(bf16[12,256,128]{2,1,0:T(8,128)(2,1)S(1)} %get-tuple-element.18), channel_id=1, source_target_pairs={{4,8},{12,16},{20,24},{28,32},{36,40},{44,48},{52,56},{60,64},{68,... | collective-permute-start | bytes 2359304 | tf_op jit(solution)/shard_map/ppermute | solution.py:139
  13.0 0.0 collective-permute-done.1.feat1
  13.0 7.9 %collective-permute-start.2 = (bf16[12,256,128]{2,1,0:T(8,128)(2,1)S(1)}, bf16[12,256,128]{2,1,0:T(8,128)(2,1)S(1)}, u32[]{:S(2)}, u32[]{:S(2)}) collective-permute-start(bf16[12,256,128]{2,1,0:T(8,128)(2,1)S(1)} %get-tuple-element.20), channel_id=1, source_target_pairs={{0,4},{4,0},{1,5},{5,1},{2,6},{6,2},{3,7},{7,3},{8,12},{12,8},{9,1... | collective-permute-start | bytes 2359304 | tf_op jit(solution)/shard_map/ppermute | solution.py:139
  21.0 0.0 copy-done
  21.0 2.0 %collective-permute-start.3 = (bf16[768,256]{1,0:T(8,128)(2,1)S(1)}, bf16[768,256]{1,0:T(8,128)(2,1)S(1)}, u32[]{:S(2)}, u32[]{:S(2)}) collective-permute-start(bf16[768,256]{1,0:T(8,128)(2,1)S(1)} %pad_maximum_fusion), channel_id=1, source_target_pairs={{0,3},{1,2},{2,1},{3,0},{4,5},{5,4},{6,7},{7,6},{8,11},{9,10},{10,... | collective-permute-start | bytes 1179656 | tf_op jit(solution)/shard_map/ppermute | solution.py:180
  23.0 6.8 %collective-permute-done.3.feat32 = bf16[768,256]{1,0:T(8,128)(2,1)S(1)} collective-permute-done((bf16[768,256]{1,0:T(8,128)(2,1)S(1)}, bf16[768,256]{1,0:T(8,128)(2,1)S(1)}, u32[]{:S(2)}, u32[]{:S(2)}) %collective-permute-start.3) | collective-permute-done | bytes 393248 | tf_op jit(solution)/shard_map/ppermute | solution.py:180
  29.8 0.0 collective-permute-done.cross
  29.8 0.0 collective-permute-done.2.chip
  29.8 0.0 copy-start.1
  29.8 1.4 %weight_term.1 = (bf16[3,256,128]{2,1,0:T(8,128)(2,1)S(1)}, bf16[3,256,128]{2,1,0:T(8,128)(2,1)S(1)}, f32[3,256,128]{2,1,0:T(8,128)S(1)}, f32[3,256,128]{2,1,0:T(8,128)S(1)}, bf16[32,16,128]{2,1,0:T(8,128)(2,1)}) custom-call(f32[12,256,128]{2,1,0:T(8,128)S(1)} %get-tuple-element.17.own, bf16[12,256,128]{2,1,0:T(8,128)(2,1)S(1)} %collective-permute-done.cross, ...), custom_call_target="tpu_custom_call" | custom-call | tf_op jit(solution)/shard_map/weight_term/pallas_call | solution.py:184
  31.2 13.2 %all-to-all-start = ((bf16[32,16,128]{2,1,0:T(8,128)(2,1)}), bf16[32,16,128]{2,1,0:T(8,128)(2,1)S(1)}, u32[]{:S(2)}, u32[]{:S(2)}) async-start(bf16[32,16,128]{2,1,0:T(8,128)(2,1)} %get-tuple-element.23), calls=%async_computation | async-start | bytes 262144 | tf_op jit(solution)/shard_map/all_to_all | solution.py:201
  44.4 4.4 %collective-permute-start.5 = (bf16[3,256,128]{2,1,0:T(8,128)(2,1)S(1)}, bf16[3,256,128]{2,1,0:T(8,128)(2,1)S(1)}, u32[]{:S(2)}, u32[]{:S(2)}) collective-permute-start(bf16[3,256,128]{2,1,0:T(8,128)(2,1)S(1)} %get-tuple-element.28), channel_id=1, source_target_pairs={{0,1},{1,0},{2,3},{3,2},{4,7},{5,6},{6,5},{7,4},{8,9},{9,8},{10,11... | collective-permute-start | bytes 589832 | tf_op jit(solution)/shard_map/ppermute | solution.py:198
  48.8 4.7 %all-to-all-done.got = bf16[32,16,128]{2,1,0:T(8,128)(2,1)S(1)} async-done(((bf16[32,16,128]{2,1,0:T(8,128)(2,1)}), bf16[32,16,128]{2,1,0:T(8,128)(2,1)S(1)}, u32[]{:S(2)}, u32[]{:S(2)}) %all-to-all-start) | async-done | bytes 131104 | tf_op jit(solution)/shard_map/all_to_all | solution.py:201
  53.5 0.7 spread.2
  54.2 8.0 %all-to-all-start.1 = ((bf16[24,16,128]{2,1,0:T(8,128)(2,1)}), bf16[24,16,128]{2,1,0:T(8,128)(2,1)S(1)}, u32[]{:S(2)}, u32[]{:S(2)}) async-start(bf16[24,16,128]{2,1,0:T(8,128)(2,1)} %spread.2), calls=%async_computation.1 | async-start | bytes 196608 | tf_op jit(solution)/shard_map/all_to_all | solution.py:205
  62.3 0.0 collective-permute-done.5
  62.3 2.2 %collective-permute-start.6 = (bf16[3,256,128]{2,1,0:T(8,128)(2,1)S(1)}, bf16[3,256,128]{2,1,0:T(8,128)(2,1)S(1)}, u32[]{:S(2)}, u32[]{:S(2)}) collective-permute-start(bf16[3,256,128]{2,1,0:T(8,128)(2,1)S(1)} %add_convert_fusion), channel_id=1, source_target_pairs={{0,3},{1,2},{2,1},{3,0},{4,5},{5,4},{6,7},{7,6},{8,11},{9,10},{10,... | collective-permute-start | bytes 589832 | tf_op jit(solution)/shard_map/ppermute | solution.py:200
  64.6 2.9 %collective-permute-start.4 = (bf16[3,256,128]{2,1,0:T(8,128)(2,1)S(1)}, bf16[3,256,128]{2,1,0:T(8,128)(2,1)S(1)}, u32[]{:S(2)}, u32[]{:S(2)}) collective-permute-start(bf16[3,256,128]{2,1,0:T(8,128)(2,1)S(1)} %get-tuple-element.26), channel_id=1, source_target_pairs={{0,1},{1,0},{2,3},{3,2},{4,7},{5,6},{6,5},{7,4},{8,9},{9,8},{10,11... | collective-permute-start | bytes 589832 | tf_op jit(solution)/shard_map/ppermute | solution.py:203
  67.4 1.6 %collective-permute-done.6.other = bf16[3,256,128]{2,1,0:T(8,128)(2,1)S(1)} collective-permute-done((bf16[3,256,128]{2,1,0:T(8,128)(2,1)S(1)}, bf16[3,256,128]{2,1,0:T(8,128)(2,1)S(1)}, u32[]{:S(2)}, u32[]{:S(2)}) %collective-permute-start.6) | collective-permute-done | bytes 196640 | tf_op jit(solution)/shard_map/ppermute | solution.py:200
  69.0 4.0 %collective-permute-done.4.pair = bf16[3,256,128]{2,1,0:T(8,128)(2,1)S(1)} collective-permute-done((bf16[3,256,128]{2,1,0:T(8,128)(2,1)S(1)}, bf16[3,256,128]{2,1,0:T(8,128)(2,1)S(1)}, u32[]{:S(2)}, u32[]{:S(2)}) %collective-permute-start.4) | collective-permute-done | bytes 196640 | tf_op jit(solution)/shard_map/ppermute | solution.py:203
  73.0 0.3 all-to-all-done.1.got
  73.3 0.7 spread.3
  74.0 3.9 %all-to-all-start.2 = ((bf16[32,16,128]{2,1,0:T(8,128)(2,1)}), bf16[32,16,128]{2,1,0:T(8,128)(2,1)S(1)}, u32[]{:S(2)}, u32[]{:S(2)}) async-start(bf16[32,16,128]{2,1,0:T(8,128)(2,1)} %spread.3), calls=%async_computation.2 | async-start | bytes 262144 | tf_op jit(solution)/shard_map/all_to_all | solution.py:216
  77.9 0.0 copy-done.1
  77.9 1.2 %feature_grad.1 = f32[384,256]{1,0:T(8,128)} custom-call(f32[3,256,128]{2,1,0:T(8,128)S(1)} %get-tuple-element.22.keep, bf16[3,256,128]{2,1,0:T(8,128)(2,1)S(1)} %collective-permute-done.4.pair, bf16[3,256,128]{2,1,0:T(8,128)(2,1)S(1)} %collective-permute-done.6.other, bf16[256,256]{1,0:T(8,128)(2,1)S(1)} %copy-done.1), custom_call_target="tpu_custom_call" | custom-call | tf_op jit(solution)/shard_map/feature_grad/pallas_call | solution.py:207
  79.0 8.0 %all-to-all-done.2 = bf16[32,16,128]{2,1,0:T(8,128)(2,1)S(1)} async-done(((bf16[32,16,128]{2,1,0:T(8,128)(2,1)}), bf16[32,16,128]{2,1,0:T(8,128)(2,1)S(1)}, u32[]{:S(2)}, u32[]{:S(2)}) %all-to-all-start.2) | async-done | bytes 131104 | tf_op jit(solution)/shard_map/all_to_all | solution.py:216
  87.0 0.7 convert_bitcast_fusion
  (2 shorter events, 0.1 us)
Async XLA Ops:
  0.6 20.3 %copy-start = (bf16[384,256]{1,0:T(8,128)(2,1)S(1)}, bf16[384,256]{1,0:T(8,128)(2,1)}, u32[]{:S(2)}) copy-start(bf16[384,256]{1,0:T(8,128)(2,1)} %feat0.1) | copy-start | bytes 589828
  0.6 12.4 %collective-permute-start.1 = (bf16[384,256]{1,0:T(8,128)(2,1)}, bf16[384,256]{1,0:T(8,128)(2,1)S(1)}, u32[]{:S(2)}, u32[]{:S(2)}) collective-permute-start(bf16[384,256]{1,0:T(8,128)(2,1)} %feat0.1), channel_id=1, source_target_pairs={{0,1},{1,0},{2,3},{3,2},{4,7},{5,6},{6,5},{7,4},{8,9},{9,8},{10,11... | collective-permute-start | bytes 589832 | tf_op jit(solution)/shard_map/ppermute | solution.py:176
  10.0 19.8 %collective-permute-start = (bf16[12,256,128]{2,1,0:T(8,128)(2,1)S(1)}, bf16[12,256,128]{2,1,0:T(8,128)(2,1)S(1)}, u32[]{:S(2)}, u32[]{:S(2)}) collective-permute-start(bf16[12,256,128]{2,1,0:T(8,128)(2,1)S(1)} %get-tuple-element.18), channel_id=1, source_target_pairs={{4,8},{12,16},{20,24},{28,32},{36,40},{44,48},{52,56},{60,64},{68,... | collective-permute-start | bytes 2359304 | tf_op jit(solution)/shard_map/ppermute | solution.py:139
  13.0 16.8 %collective-permute-start.2 = (bf16[12,256,128]{2,1,0:T(8,128)(2,1)S(1)}, bf16[12,256,128]{2,1,0:T(8,128)(2,1)S(1)}, u32[]{:S(2)}, u32[]{:S(2)}) collective-permute-start(bf16[12,256,128]{2,1,0:T(8,128)(2,1)S(1)} %get-tuple-element.20), channel_id=1, source_target_pairs={{0,4},{4,0},{1,5},{5,1},{2,6},{6,2},{3,7},{7,3},{8,12},{12,8},{9,1... | collective-permute-start | bytes 2359304 | tf_op jit(solution)/shard_map/ppermute | solution.py:139
  21.0 8.8 %collective-permute-start.3 = (bf16[768,256]{1,0:T(8,128)(2,1)S(1)}, bf16[768,256]{1,0:T(8,128)(2,1)S(1)}, u32[]{:S(2)}, u32[]{:S(2)}) collective-permute-start(bf16[768,256]{1,0:T(8,128)(2,1)S(1)} %pad_maximum_fusion), channel_id=1, source_target_pairs={{0,3},{1,2},{2,1},{3,0},{4,5},{5,4},{6,7},{7,6},{8,11},{9,10},{10,... | collective-permute-start | bytes 1179656 | tf_op jit(solution)/shard_map/ppermute | solution.py:180
  29.8 48.0 %copy-start.1 = (bf16[256,256]{1,0:T(8,128)(2,1)S(1)}, bf16[256,256]{1,0:T(8,128)(2,1)}, u32[]{:S(2)}) copy-start(bf16[256,256]{1,0:T(8,128)(2,1)} %weight.1) | copy-start | bytes 393220
  31.2 22.3 %all-to-all-start = ((bf16[32,16,128]{2,1,0:T(8,128)(2,1)}), bf16[32,16,128]{2,1,0:T(8,128)(2,1)S(1)}, u32[]{:S(2)}, u32[]{:S(2)}) async-start(bf16[32,16,128]{2,1,0:T(8,128)(2,1)} %get-tuple-element.23), calls=%async_computation | async-start | bytes 262144 | tf_op jit(solution)/shard_map/all_to_all | solution.py:201
  44.4 17.9 %collective-permute-start.5 = (bf16[3,256,128]{2,1,0:T(8,128)(2,1)S(1)}, bf16[3,256,128]{2,1,0:T(8,128)(2,1)S(1)}, u32[]{:S(2)}, u32[]{:S(2)}) collective-permute-start(bf16[3,256,128]{2,1,0:T(8,128)(2,1)S(1)} %get-tuple-element.28), channel_id=1, source_target_pairs={{0,1},{1,0},{2,3},{3,2},{4,7},{5,6},{6,5},{7,4},{8,9},{9,8},{10,11... | collective-permute-start | bytes 589832 | tf_op jit(solution)/shard_map/ppermute | solution.py:198
  54.2 19.1 %all-to-all-start.1 = ((bf16[24,16,128]{2,1,0:T(8,128)(2,1)}), bf16[24,16,128]{2,1,0:T(8,128)(2,1)S(1)}, u32[]{:S(2)}, u32[]{:S(2)}) async-start(bf16[24,16,128]{2,1,0:T(8,128)(2,1)} %spread.2), calls=%async_computation.1 | async-start | bytes 196608 | tf_op jit(solution)/shard_map/all_to_all | solution.py:205
  62.3 6.7 %collective-permute-start.6 = (bf16[3,256,128]{2,1,0:T(8,128)(2,1)S(1)}, bf16[3,256,128]{2,1,0:T(8,128)(2,1)S(1)}, u32[]{:S(2)}, u32[]{:S(2)}) collective-permute-start(bf16[3,256,128]{2,1,0:T(8,128)(2,1)S(1)} %add_convert_fusion), channel_id=1, source_target_pairs={{0,3},{1,2},{2,1},{3,0},{4,5},{5,4},{6,7},{7,6},{8,11},{9,10},{10,... | collective-permute-start | bytes 589832 | tf_op jit(solution)/shard_map/ppermute | solution.py:200
  64.6 8.4 %collective-permute-start.4 = (bf16[3,256,128]{2,1,0:T(8,128)(2,1)S(1)}, bf16[3,256,128]{2,1,0:T(8,128)(2,1)S(1)}, u32[]{:S(2)}, u32[]{:S(2)}) collective-permute-start(bf16[3,256,128]{2,1,0:T(8,128)(2,1)S(1)} %get-tuple-element.26), channel_id=1, source_target_pairs={{0,1},{1,0},{2,3},{3,2},{4,7},{5,6},{6,5},{7,4},{8,9},{9,8},{10,11... | collective-permute-start | bytes 589832 | tf_op jit(solution)/shard_map/ppermute | solution.py:203
  74.0 13.0 %all-to-all-start.2 = ((bf16[32,16,128]{2,1,0:T(8,128)(2,1)}), bf16[32,16,128]{2,1,0:T(8,128)(2,1)S(1)}, u32[]{:S(2)}, u32[]{:S(2)}) async-start(bf16[32,16,128]{2,1,0:T(8,128)(2,1)} %spread.3), calls=%async_computation.2 | async-start | bytes 262144 | tf_op jit(solution)/shard_map/all_to_all | solution.py:216

commit v12 on v11

--- a/solution.py
+++ b/solution.py
@@ -196,11 +196,10 @@
         name="weight_term",
     )(own, from_cross, from_chip, features, feat1, feat32)
     passing = lax.ppermute(give2, ("core", "x"), near)
+    from_near = lax.ppermute(give1, ("core", "x"), near)
     onward = (keep3 + passing.astype(jnp.float32)).astype(jnp.bfloat16)
     from_far = lax.ppermute(onward, ("core", "x"), far)
     got = lax.all_to_all(term, ("x", "y"), 0, 0)
-    got, give1 = lax.optimization_barrier((got, give1))
-    from_near = lax.ppermute(give1, ("core", "x"), near)
     copies = spread(got, 2 * z, math.sqrt(rows * x * rows_dev))
     got = lax.all_to_all(copies, ("z", "core"), 0, 0)
     got, from_near, from_far = lax.optimization_barrier((got, from_near, from_far))

time: 88.5 us -> 90.8 us (1.026)
  starting transfers between devices: 52.8 us -> 54.2 us
    all_to_all x1, waiting for transfers between devices: 0.32 us -> 4.28 us  [local(): got = lax.all_to_all(copies, ('z', 'core'), 0, 0)]
    ppermute x1, waiting for transfers between devices: 3.96 us -> 0.01 us  [local(): from_near = lax.ppermute(give1, ('core', 'x'), near)]
    ppermute x1, waiting for transfers between devices: 1.58 us -> 4.44 us  [local(): from_far = lax.ppermute(onward, ('core', 'x'), far)]
    all_to_all x1, waiting for transfers between devices: 4.75 us -> 2.66 us  [local(): got = lax.all_to_all(term, ('x', 'y'), 0, 0)]
    all_to_all x1, starting transfers between devices: 8.05 us -> 9.32 us  [local(): got = lax.all_to_all(copies, ('z', 'core'), 0, 0)]
    all_to_all x1, starting transfers between devices: 3.86 us -> 4.98 us  [local(): pieces = lax.all_to_all(copies, ('x', 'y'), 0, 0).astype(jnp.float32)]
  transfers between devices with their start and end apart: 10 -> 10, of which waited for: 6 -> 5; matrix products, arithmetic and copies ran while one was open for 0% -> 0% of each run, Pallas kernels for 6% -> 6%
where the time goes in v12:
time: 90.8 us; the launch traced here: 90 us
  starting transfers between devices  54.2 us (60%)
  waiting for transfers between devices  26.2 us (29%)
  Pallas kernels  7.27 us (8%)
  between operations  1.44 us (2%)
    all_to_all x1, starting transfers between devices, local(): got = lax.all_to_all(term, ('x', 'y'), 0, 0)  12.9 us
    ppermute x2, starting transfers between devices, swap(): return lax.ppermute(array, axes, pairs + [(j, i) for i, j in pairs])  10.9 us
    all_to_all x1, starting transfers between devices, local(): got = lax.all_to_all(copies, ('z', 'core'), 0, 0)  9.32 us
    all_to_all x1, waiting for transfers between devices, local(): pieces = lax.all_to_all(copies, ('x', 'y'), 0, 0).astype(jnp.float32)  7.99 us
    ppermute x1, waiting for transfers between devices, local(): lax.ppermute(jnp.concatenate([features, feat1], axis=0), ('core', 'x'), far)  6.83 us
    ppermute x1, starting transfers between devices, local(): feat1 = lax.ppermute(features, ('core', 'x'), near)  5.35 us
    all_to_all x1, starting transfers between devices, local(): pieces = lax.all_to_all(copies, ('x', 'y'), 0, 0).astype(jnp.float32)  4.98 us
    ppermute x1, waiting for transfers between devices, local(): from_far = lax.ppermute(onward, ('core', 'x'), far)  4.44 us
  transfers between devices with their start and end apart: 10, of which 5 were waited for; matrix products, arithmetic and copies ran while one was open for 0% of the time, Pallas kernels for 6%

profile of v12, /device:TPU:1, one launch (start us, length us, event | category | flops | bytes accessed | tf_op | source)
XLA Modules:
  0.0 90.0 jit_solution(16879348416284225236)
XLA Ops:
  0.6 0.0 copy-start
  0.6 5.3 %collective-permute-start.1 = (bf16[384,256]{1,0:T(8,128)(2,1)}, bf16[384,256]{1,0:T(8,128)(2,1)S(1)}, u32[]{:S(2)}, u32[]{:S(2)}) collective-permute-start(bf16[384,256]{1,0:T(8,128)(2,1)} %feat0.1), channel_id=1, source_target_pairs={{0,1},{1,0},{2,3},{3,2},{4,7},{5,6},{6,5},{7,4},{8,9},{9,8},{10,11... | collective-permute-start | bytes 589832 | tf_op jit(solution)/shard_map/ppermute | solution.py:176
  6.6 3.4 %tile_sums.1 = (bf16[12,256,128]{2,1,0:T(8,128)(2,1)S(1)}, bf16[12,256,128]{2,1,0:T(8,128)(2,1)S(1)}, f32[12,256,128]{2,1,0:T(8,128)S(1)}) custom-call(s32[1]{0:T(128)S(6)} %copy.9.count, s32[3,72]{1,0:T(4,128)} %bitcast.8, bf16[384,256]{1,0:T(8,128)(2,1)} %pre_hbm.1, f32[384,256]{1,0:T(8,128)} %up_hbm.1, bf16[72,128,128]{2,1,0:T(8,128)(2,1)} %tiles_hbm.1), custom_call_target="tpu_custom_call" | custom-call | tf_op jit(solution)/shard_map/tile_sums/pallas_call | solution.py:154
  10.0 3.0 %collective-permute-start = (bf16[12,256,128]{2,1,0:T(8,128)(2,1)S(1)}, bf16[12,256,128]{2,1,0:T(8,128)(2,1)S(1)}, u32[]{:S(2)}, u32[]{:S(2)}) collective-permute-start(bf16[12,256,128]{2,1,0:T(8,128)(2,1)S(1)} %get-tuple-element.16), channel_id=1, source_target_pairs={{4,8},{12,16},{20,24},{28,32},{36,40},{44,48},{52,56},{60,64},{68,... | collective-permute-start | bytes 2359304 | tf_op jit(solution)/shard_map/ppermute | solution.py:139
  13.0 0.0 collective-permute-done.1.feat1
  13.0 7.9 %collective-permute-start.2 = (bf16[12,256,128]{2,1,0:T(8,128)(2,1)S(1)}, bf16[12,256,128]{2,1,0:T(8,128)(2,1)S(1)}, u32[]{:S(2)}, u32[]{:S(2)}) collective-permute-start(bf16[12,256,128]{2,1,0:T(8,128)(2,1)S(1)} %get-tuple-element.18), channel_id=1, source_target_pairs={{0,4},{4,0},{1,5},{5,1},{2,6},{6,2},{3,7},{7,3},{8,12},{12,8},{9,1... | collective-permute-start | bytes 2359304 | tf_op jit(solution)/shard_map/ppermute | solution.py:139
  21.0 0.0 copy-done
  21.0 2.0 %collective-permute-start.3 = (bf16[768,256]{1,0:T(8,128)(2,1)S(1)}, bf16[768,256]{1,0:T(8,128)(2,1)S(1)}, u32[]{:S(2)}, u32[]{:S(2)}) collective-permute-start(bf16[768,256]{1,0:T(8,128)(2,1)S(1)} %pad_maximum_fusion), channel_id=1, source_target_pairs={{0,3},{1,2},{2,1},{3,0},{4,5},{5,4},{6,7},{7,6},{8,11},{9,10},{10,... | collective-permute-start | bytes 1179656 | tf_op jit(solution)/shard_map/ppermute | solution.py:180
  23.0 6.8 %collective-permute-done.3.feat32 = bf16[768,256]{1,0:T(8,128)(2,1)S(1)} collective-permute-done((bf16[768,256]{1,0:T(8,128)(2,1)S(1)}, bf16[768,256]{1,0:T(8,128)(2,1)S(1)}, u32[]{:S(2)}, u32[]{:S(2)}) %collective-permute-start.3) | collective-permute-done | bytes 393248 | tf_op jit(solution)/shard_map/ppermute | solution.py:180
  29.8 0.0 collective-permute-done.cross
  29.8 0.0 collective-permute-done.2.chip
  29.8 0.0 copy-start.1
  29.8 1.4 %weight_term.1 = (bf16[3,256,128]{2,1,0:T(8,128)(2,1)S(1)}, bf16[3,256,128]{2,1,0:T(8,128)(2,1)S(1)}, f32[3,256,128]{2,1,0:T(8,128)S(1)}, f32[3,256,128]{2,1,0:T(8,128)S(1)}, bf16[32,16,128]{2,1,0:T(8,128)(2,1)}) custom-call(f32[12,256,128]{2,1,0:T(8,128)S(1)} %get-tuple-element.15.own, bf16[12,256,128]{2,1,0:T(8,128)(2,1)S(1)} %collective-permute-done.cross, ...), custom_call_target="tpu_custom_call" | custom-call | tf_op jit(solution)/shard_map/weight_term/pallas_call | solution.py:184
  31.2 12.9 %all-to-all-start = ((bf16[32,16,128]{2,1,0:T(8,128)(2,1)}), bf16[32,16,128]{2,1,0:T(8,128)(2,1)S(1)}, u32[]{:S(2)}, u32[]{:S(2)}) async-start(bf16[32,16,128]{2,1,0:T(8,128)(2,1)} %get-tuple-element.21), calls=%async_computation | async-start | bytes 262144 | tf_op jit(solution)/shard_map/all_to_all | solution.py:202
  44.2 4.4 %collective-permute-start.5 = (bf16[3,256,128]{2,1,0:T(8,128)(2,1)S(1)}, bf16[3,256,128]{2,1,0:T(8,128)(2,1)S(1)}, u32[]{:S(2)}, u32[]{:S(2)}) collective-permute-start(bf16[3,256,128]{2,1,0:T(8,128)(2,1)S(1)} %get-tuple-element.24), channel_id=1, source_target_pairs={{0,1},{1,0},{2,3},{3,2},{4,7},{5,6},{6,5},{7,4},{8,9},{9,8},{10,11... | collective-permute-start | bytes 589832 | tf_op jit(solution)/shard_map/ppermute | solution.py:198
  48.6 2.1 %collective-permute-start.4 = (bf16[3,256,128]{2,1,0:T(8,128)(2,1)S(1)}, bf16[3,256,128]{2,1,0:T(8,128)(2,1)S(1)}, u32[]{:S(2)}, u32[]{:S(2)}) collective-permute-start(bf16[3,256,128]{2,1,0:T(8,128)(2,1)S(1)} %get-tuple-element.22), channel_id=1, source_target_pairs={{0,1},{1,0},{2,3},{3,2},{4,7},{5,6},{6,5},{7,4},{8,9},{9,8},{10,11... | collective-permute-start | bytes 589832 | tf_op jit(solution)/shard_map/ppermute | solution.py:199
  50.7 2.7 %all-to-all-done.got = bf16[32,16,128]{2,1,0:T(8,128)(2,1)S(1)} async-done(((bf16[32,16,128]{2,1,0:T(8,128)(2,1)}), bf16[32,16,128]{2,1,0:T(8,128)(2,1)S(1)}, u32[]{:S(2)}, u32[]{:S(2)}) %all-to-all-start) | async-done | bytes 131104 | tf_op jit(solution)/shard_map/all_to_all | solution.py:202
  53.3 0.7 spread.2
  54.0 9.3 %all-to-all-start.1 = ((bf16[24,16,128]{2,1,0:T(8,128)(2,1)}), bf16[24,16,128]{2,1,0:T(8,128)(2,1)S(1)}, u32[]{:S(2)}, u32[]{:S(2)}) async-start(bf16[24,16,128]{2,1,0:T(8,128)(2,1)} %spread.2), calls=%async_computation.1 | async-start | bytes 196608 | tf_op jit(solution)/shard_map/all_to_all | solution.py:204
  63.4 0.0 collective-permute-done.5
  63.4 2.3 %collective-permute-start.6 = (bf16[3,256,128]{2,1,0:T(8,128)(2,1)S(1)}, bf16[3,256,128]{2,1,0:T(8,128)(2,1)S(1)}, u32[]{:S(2)}, u32[]{:S(2)}) collective-permute-start(bf16[3,256,128]{2,1,0:T(8,128)(2,1)S(1)} %add_convert_fusion), channel_id=1, source_target_pairs={{0,3},{1,2},{2,1},{3,0},{4,5},{5,4},{6,7},{7,6},{8,11},{9,10},{10,... | collective-permute-start | bytes 589832 | tf_op jit(solution)/shard_map/ppermute | solution.py:201
  65.7 0.0 collective-permute-done.4.pair
  65.7 4.4 %collective-permute-done.6.other = bf16[3,256,128]{2,1,0:T(8,128)(2,1)S(1)} collective-permute-done((bf16[3,256,128]{2,1,0:T(8,128)(2,1)S(1)}, bf16[3,256,128]{2,1,0:T(8,128)(2,1)S(1)}, u32[]{:S(2)}, u32[]{:S(2)}) %collective-permute-start.6) | collective-permute-done | bytes 196640 | tf_op jit(solution)/shard_map/ppermute | solution.py:201
  70.1 4.3 %all-to-all-done.1.got = bf16[24,16,128]{2,1,0:T(8,128)(2,1)S(1)} async-done(((bf16[24,16,128]{2,1,0:T(8,128)(2,1)}), bf16[24,16,128]{2,1,0:T(8,128)(2,1)S(1)}, u32[]{:S(2)}, u32[]{:S(2)}) %all-to-all-start.1) | async-done | bytes 98336 | tf_op jit(solution)/shard_map/all_to_all | solution.py:204
  74.4 0.7 spread.3
  75.1 5.0 %all-to-all-start.2 = ((bf16[32,16,128]{2,1,0:T(8,128)(2,1)}), bf16[32,16,128]{2,1,0:T(8,128)(2,1)S(1)}, u32[]{:S(2)}, u32[]{:S(2)}) async-start(bf16[32,16,128]{2,1,0:T(8,128)(2,1)} %spread.3), calls=%async_computation.2 | async-start | bytes 262144 | tf_op jit(solution)/shard_map/all_to_all | solution.py:215
  80.1 0.0 copy-done.1
  80.1 1.2 %feature_grad.1 = f32[384,256]{1,0:T(8,128)} custom-call(f32[3,256,128]{2,1,0:T(8,128)S(1)} %get-tuple-element.20.keep, bf16[3,256,128]{2,1,0:T(8,128)(2,1)S(1)} %collective-permute-done.4.pair, bf16[3,256,128]{2,1,0:T(8,128)(2,1)S(1)} %collective-permute-done.6.other, bf16[256,256]{1,0:T(8,128)(2,1)S(1)} %copy-done.1), custom_call_target="tpu_custom_call" | custom-call | tf_op jit(solution)/shard_map/feature_grad/pallas_call | solution.py:206
  81.2 8.0 %all-to-all-done.2 = bf16[32,16,128]{2,1,0:T(8,128)(2,1)S(1)} async-done(((bf16[32,16,128]{2,1,0:T(8,128)(2,1)}), bf16[32,16,128]{2,1,0:T(8,128)(2,1)S(1)}, u32[]{:S(2)}, u32[]{:S(2)}) %all-to-all-start.2) | async-done | bytes 131104 | tf_op jit(solution)/shard_map/all_to_all | solution.py:215
  89.2 0.7 convert_bitcast_fusion
  (2 shorter events, 0.1 us)
Async XLA Ops:
  0.6 20.3 %copy-start = (bf16[384,256]{1,0:T(8,128)(2,1)S(1)}, bf16[384,256]{1,0:T(8,128)(2,1)}, u32[]{:S(2)}) copy-start(bf16[384,256]{1,0:T(8,128)(2,1)} %feat0.1) | copy-start | bytes 589828
  0.6 12.4 %collective-permute-start.1 = (bf16[384,256]{1,0:T(8,128)(2,1)}, bf16[384,256]{1,0:T(8,128)(2,1)S(1)}, u32[]{:S(2)}, u32[]{:S(2)}) collective-permute-start(bf16[384,256]{1,0:T(8,128)(2,1)} %feat0.1), channel_id=1, source_target_pairs={{0,1},{1,0},{2,3},{3,2},{4,7},{5,6},{6,5},{7,4},{8,9},{9,8},{10,11... | collective-permute-start | bytes 589832 | tf_op jit(solution)/shard_map/ppermute | solution.py:176
  10.0 19.8 %collective-permute-start = (bf16[12,256,128]{2,1,0:T(8,128)(2,1)S(1)}, bf16[12,256,128]{2,1,0:T(8,128)(2,1)S(1)}, u32[]{:S(2)}, u32[]{:S(2)}) collective-permute-start(bf16[12,256,128]{2,1,0:T(8,128)(2,1)S(1)} %get-tuple-element.16), channel_id=1, source_target_pairs={{4,8},{12,16},{20,24},{28,32},{36,40},{44,48},{52,56},{60,64},{68,... | collective-permute-start | bytes 2359304 | tf_op jit(solution)/shard_map/ppermute | solution.py:139
  13.0 16.8 %collective-permute-start.2 = (bf16[12,256,128]{2,1,0:T(8,128)(2,1)S(1)}, bf16[12,256,128]{2,1,0:T(8,128)(2,1)S(1)}, u32[]{:S(2)}, u32[]{:S(2)}) collective-permute-start(bf16[12,256,128]{2,1,0:T(8,128)(2,1)S(1)} %get-tuple-element.18), channel_id=1, source_target_pairs={{0,4},{4,0},{1,5},{5,1},{2,6},{6,2},{3,7},{7,3},{8,12},{12,8},{9,1... | collective-permute-start | bytes 2359304 | tf_op jit(solution)/shard_map/ppermute | solution.py:139
  21.0 8.8 %collective-permute-start.3 = (bf16[768,256]{1,0:T(8,128)(2,1)S(1)}, bf16[768,256]{1,0:T(8,128)(2,1)S(1)}, u32[]{:S(2)}, u32[]{:S(2)}) collective-permute-start(bf16[768,256]{1,0:T(8,128)(2,1)S(1)} %pad_maximum_fusion), channel_id=1, source_target_pairs={{0,3},{1,2},{2,1},{3,0},{4,5},{5,4},{6,7},{7,6},{8,11},{9,10},{10,... | collective-permute-start | bytes 1179656 | tf_op jit(solution)/shard_map/ppermute | solution.py:180
  29.8 50.2 %copy-start.1 = (bf16[256,256]{1,0:T(8,128)(2,1)S(1)}, bf16[256,256]{1,0:T(8,128)(2,1)}, u32[]{:S(2)}) copy-start(bf16[256,256]{1,0:T(8,128)(2,1)} %weight.1) | copy-start | bytes 393220
  31.2 22.1 %all-to-all-start = ((bf16[32,16,128]{2,1,0:T(8,128)(2,1)}), bf16[32,16,128]{2,1,0:T(8,128)(2,1)S(1)}, u32[]{:S(2)}, u32[]{:S(2)}) async-start(bf16[32,16,128]{2,1,0:T(8,128)(2,1)} %get-tuple-element.21), calls=%async_computation | async-start | bytes 262144 | tf_op jit(solution)/shard_map/all_to_all | solution.py:202
  44.2 19.2 %collective-permute-start.5 = (bf16[3,256,128]{2,1,0:T(8,128)(2,1)S(1)}, bf16[3,256,128]{2,1,0:T(8,128)(2,1)S(1)}, u32[]{:S(2)}, u32[]{:S(2)}) collective-permute-start(bf16[3,256,128]{2,1,0:T(8,128)(2,1)S(1)} %get-tuple-element.24), channel_id=1, source_target_pairs={{0,1},{1,0},{2,3},{3,2},{4,7},{5,6},{6,5},{7,4},{8,9},{9,8},{10,11... | collective-permute-start | bytes 589832 | tf_op jit(solution)/shard_map/ppermute | solution.py:198
  48.6 17.1 %collective-permute-start.4 = (bf16[3,256,128]{2,1,0:T(8,128)(2,1)S(1)}, bf16[3,256,128]{2,1,0:T(8,128)(2,1)S(1)}, u32[]{:S(2)}, u32[]{:S(2)}) collective-permute-start(bf16[3,256,128]{2,1,0:T(8,128)(2,1)S(1)} %get-tuple-element.22), channel_id=1, source_target_pairs={{0,1},{1,0},{2,3},{3,2},{4,7},{5,6},{6,5},{7,4},{8,9},{9,8},{10,11... | collective-permute-start | bytes 589832 | tf_op jit(solution)/shard_map/ppermute | solution.py:199
  54.0 20.4 %all-to-all-start.1 = ((bf16[24,16,128]{2,1,0:T(8,128)(2,1)}), bf16[24,16,128]{2,1,0:T(8,128)(2,1)S(1)}, u32[]{:S(2)}, u32[]{:S(2)}) async-start(bf16[24,16,128]{2,1,0:T(8,128)(2,1)} %spread.2), calls=%async_computation.1 | async-start | bytes 196608 | tf_op jit(solution)/shard_map/all_to_all | solution.py:204
  63.4 6.7 %collective-permute-start.6 = (bf16[3,256,128]{2,1,0:T(8,128)(2,1)S(1)}, bf16[3,256,128]{2,1,0:T(8,128)(2,1)S(1)}, u32[]{:S(2)}, u32[]{:S(2)}) collective-permute-start(bf16[3,256,128]{2,1,0:T(8,128)(2,1)S(1)} %add_convert_fusion), channel_id=1, source_target_pairs={{0,3},{1,2},{2,1},{3,0},{4,5},{5,4},{6,7},{7,6},{8,11},{9,10},{10,... | collective-permute-start | bytes 589832 | tf_op jit(solution)/shard_map/ppermute | solution.py:201
  75.1 14.1 %all-to-all-start.2 = ((bf16[32,16,128]{2,1,0:T(8,128)(2,1)}), bf16[32,16,128]{2,1,0:T(8,128)(2,1)S(1)}, u32[]{:S(2)}, u32[]{:S(2)}) async-start(bf16[32,16,128]{2,1,0:T(8,128)(2,1)} %spread.3), calls=%async_computation.2 | async-start | bytes 262144 | tf_op jit(solution)/shard_map/all_to_all | solution.py:215
